TPU v7x, 128 devices: a whole 4x4x4 slice. The times are simulated.
128 devices in a mesh: tm: 64 (over x, z, y_lo, core), height: 2 (over y_hi).
Axes of the slice: x: 4, y: 4 (y_hi: 2, y_lo: 2; y = y_hi * 2 + y_lo), z: 4, core: 2. Of those that a mesh axis runs over, the one named last changes fastest.
Arguments:
- latents: bfloat16 [256, 4, 128, 320], P('tm', 'height'), may hold values from -6 to 6
- levels: int32 [256], P('tm'), may hold values from 0 to 999
- conv_first: bfloat16 [3, 3, 320, 320], replicated, may hold values from -0.109375 to 0.109375
- emb_weight: bfloat16 [320, 320], replicated, may hold values from -0.625 to 0.625
- conv_second: bfloat16 [3, 3, 320, 320], replicated, may hold values from -0.109375 to 0.109375
- ln_gain: float32 [320], replicated, may hold values from 0.1 to 1.9
- w_query: bfloat16 [320, 320], replicated, may hold values from -0.3125 to 0.3125
- w_key: bfloat16 [320, 320], replicated, may hold values from -0.3125 to 0.3125
- w_value: bfloat16 [320, 320], replicated, may hold values from -0.3125 to 0.3125
- w_out: bfloat16 [320, 320], replicated, may hold values from -0.3125 to 0.3125
Outputs:
- mixed: bfloat16 [256, 4, 128, 320], P('tm', 'height')
All inputs are finite; a program needn't handle non-finite values.
Results may differ from a plain program's by a relative error of at most 0.012.
Values may be sent and summed in bfloat16 or wider, within the bound.
No kernel may reach another device: no remote copies, remote signals or barrier semaphores. Data moves between devices by JAX's collectives and lax.ppermute only.
A program may use at most 128 MiB of HBM per device.

v0:
```python
import functools
import math

import jax
import jax.numpy as jnp
from jax import lax
from jax.experimental import pallas as pl
from jax.experimental.pallas import tpu as pltpu
from jax.sharding import PartitionSpec as P

HEADS = 5
GROUPS = 32
WINDOW = 16
C = 320
MAIN = 256
TAIL = C - MAIN
COLS = 128
CELLS = 512
AXES = ("tm", "height")
F32 = jnp.float32
BF16 = jnp.bfloat16


def dot32(a, b):
    return jnp.dot(a, b, preferred_element_type=F32)


def pack_conv(weight):
    by_input = jnp.transpose(weight, (1, 2, 0, 3))
    columns = jnp.concatenate(
        [
            by_input[..., :MAIN].reshape(3, C, 3 * MAIN),
            by_input[..., MAIN:].reshape(3, C, 3 * TAIL),
        ],
        axis=2,
    )
    rows = [columns[:, :MAIN].reshape(3 * MAIN, 3 * C), columns[:, MAIN:].reshape(3 * TAIL, 3 * C)]
    return jnp.concatenate(rows + [jnp.zeros((TAIL, 3 * C), weight.dtype)], axis=0)


def level_embedding(levels, emb_weight):
    half = emb_weight.shape[0] // 2
    freqs = jnp.exp(-math.log(10000.0) * jnp.arange(half).astype(jnp.float32) / half)
    angles = levels.astype(jnp.float32)[:, None] * freqs[None, :]
    sinus = jnp.concatenate([jnp.cos(angles), jnp.sin(angles)], axis=1)
    return jnp.dot(
        jax.nn.silu(sinus).astype(jnp.bfloat16), emb_weight, preferred_element_type=jnp.float32
    )


def split3(row):
    first = row.astype(BF16)
    rest = row - first.astype(F32)
    second = rest.astype(BF16)
    return [first, second, (rest - second.astype(F32)).astype(BF16)]


def group_scale(main, tail, group_map):
    parts = []
    for value in (main, tail):
        total = jnp.sum(value, axis=0, keepdims=True)
        square = jnp.sum(value * value, axis=0, keepdims=True)
        rows = split3(total) + split3(square)
        rows = [r.astype(F32) for r in rows] + [jnp.zeros_like(total)] * 2
        parts.append(jnp.concatenate(rows, axis=0).astype(BF16))
    sums = dot32(parts[0], group_map[:MAIN, :]) + dot32(parts[1], group_map[MAIN:, :])
    count = CELLS * (C // GROUPS)
    mean = (sums[0:1] + sums[1:2] + sums[2:3]) / count
    var = (sums[3:4] + sums[4:5] + sums[5:6]) / count - mean * mean
    scale = lax.rsqrt(var + 1e-05)
    return scale, -mean * scale


def silu(u):
    half = 0.5 * u
    return half + half * jnp.tanh(half)


def conv_input(act_ref, main, tail, group_map):
    scale, shift = group_scale(main, tail, group_map)
    column = lax.broadcasted_iota(jnp.int32, (CELLS, 1), 0) % COLS

    def three(value, lo, hi):
        act = silu(value * scale[:, lo:hi] + shift[:, lo:hi])
        before = jnp.where(column == 0, 0.0, pltpu.roll(act, 1, 0))
        after = jnp.where(column == COLS - 1, 0.0, pltpu.roll(act, CELLS - 1, 0))
        return before, act, after

    for index, value in enumerate(three(main, 0, MAIN)):
        act_ref[:, index * MAIN : (index + 1) * MAIN] = value.astype(BF16)
    before, act, after = three(tail, MAIN, C)
    base = 3 * MAIN
    act_ref[:, base : base + 2 * TAIL] = jnp.concatenate([before, act], axis=1).astype(BF16)
    zero = jnp.zeros_like(after)
    act_ref[:, base + 2 * TAIL :] = jnp.concatenate([after, zero], axis=1).astype(BF16)


def conv_rows(act_ref, weight_ref, taps_ref):
    taps_ref[...] = dot32(act_ref[...], weight_ref[...])

    def joined(base, width):
        rows = []
        for row in range(4):
            total = None
            for dy in range(3):
                source = row + dy - 1
                if 0 <= source < 4:
                    piece = taps_ref[
                        source * COLS : (source + 1) * COLS,
                        base + dy * width : base + (dy + 1) * width,
                    ]
                    total = piece if total is None else total + piece
            rows.append(total)
        return jnp.concatenate(rows, axis=0)

    return joined(0, MAIN), joined(3 * MAIN, TAIL)


def block_kernel(
    own_ref, got_ref, first_ref, second_ref, emb_ref, group_ref, out_ref,
    x_ref, act_ref, taps_ref, res_ref, w1_ref, w2_ref, sems,
):
    here = lax.axis_index("height")
    copies = []
    for frame in range(2):
        for side, source in ((here, own_ref.at[2 * here + frame]), (1 - here, got_ref.at[frame])):
            copies.append(
                pltpu.make_async_copy(
                    source, x_ref.at[frame, pl.ds(2 * side, 2)], sems.at[len(copies)]
                )
            )
    weights = [
        pltpu.make_async_copy(first_ref, w1_ref, sems.at[4]),
        pltpu.make_async_copy(second_ref, w2_ref, sems.at[5]),
    ]
    for copy in copies + weights:
        copy.start()
    group_map = group_ref[...]

    def hidden(frame):
        value = x_ref[frame].reshape(CELLS, C).astype(F32)
        return value[:, :MAIN], value[:, MAIN:]

    for frame in range(2):
        copies[2 * frame].wait()
        copies[2 * frame + 1].wait()
        conv_input(act_ref.at[frame], *hidden(frame), group_map)
    weights[0].wait()
    for frame in range(2):
        main, tail = conv_rows(act_ref.at[frame], w1_ref, taps_ref.at[frame])
        emb = emb_ref[pl.ds(2 * here + frame, 1), :]
        conv_input(
            act_ref.at[frame], main + emb[:, :MAIN], tail + emb[:, MAIN:], group_map
        )
    weights[1].wait()
    for frame in range(2):
        main, tail = conv_rows(act_ref.at[frame], w2_ref, taps_ref.at[frame])
        old_main, old_tail = hidden(frame)
        res_ref[frame, :, :MAIN] = main + old_main
        res_ref[frame, :, MAIN:] = tail + old_tail
    for t in range(4):
        for h in range(2):
            for b in range(8):
                start = 256 * h + 64 * t + 8 * b
                pair = [res_ref[f, start : start + 8, :] for f in range(2)]
                out_ref[2 * t + h, b] = jnp.concatenate(pair, axis=0).astype(BF16)


def attention_kernel(
    base_ref, own_ref, prev_ref, next_ref, gain_ref, wq_ref, wkv_ref, wo_ref, out_ref,
    norm_ref, q_ref, kv_ref, att_ref,
):
    base = base_ref[0, 0]
    gain = gain_ref[...]
    for b in range(8):
        value = jnp.concatenate(
            [
                prev_ref[:, b].reshape(64, C),
                own_ref[:, b].reshape(128, C),
                next_ref[:, b].reshape(64, C),
            ],
            axis=0,
        ).astype(F32)
        mean = jnp.mean(value, axis=-1, keepdims=True)
        centred = value - mean
        var = jnp.mean(centred * centred, axis=-1, keepdims=True)
        normed = (centred * lax.rsqrt(var + 1e-05) * gain).astype(BF16)
        norm_ref[b] = normed
    for b in range(8):
        normed = norm_ref[b]
        q_ref[b] = dot32(normed[64:192], wq_ref[...]).astype(BF16)
        kv_ref[b] = dot32(normed, wkv_ref[...]).astype(BF16)
    row = lax.broadcasted_iota(jnp.int32, (128, 256), 0)
    col = lax.broadcasted_iota(jnp.int32, (128, 256), 1)
    away = col // 8 - 8 - row // 8
    frame = base + col // 8 - 8
    keep = (row % 8 == col % 8) & (away >= -(WINDOW // 2)) & (away < WINDOW // 2)
    keep = keep & (frame >= 0) & (frame < 256)
    bias = jnp.where(keep, 0.0, -1e30).astype(F32)
    bias2 = jnp.concatenate([bias, bias], axis=0)
    ones = jnp.ones((256, 128), BF16)
    lane = lax.broadcasted_iota(jnp.int32, (128, 128), 1)
    for b in range(8):
        for pair in range(3):
            low = 128 * pair
            q = q_ref[b, :, low : low + 128]
            k = kv_ref[b, :, low : low + 128]
            v = kv_ref[b, :, 384 + low : 384 + low + 128]
            zero = jnp.zeros_like(q)
            q0 = jnp.where(lane < 64, q, zero)
            if pair < 2:
                q = jnp.concatenate([q0, jnp.where(lane < 64, zero, q)], axis=0)
                add = bias2
            else:
                q = q0
                add = bias
            score = lax.dot_general(
                q, k, (((1,), (1,)), ((), ())), preferred_element_type=F32
            )
            probs = jnp.exp(score + add).astype(BF16)
            mixed = dot32(probs, jnp.concatenate([v, ones], axis=1))
            mixed = mixed[:, :128] / mixed[:, 128:]
            if pair < 2:
                mixed = jnp.where(lane < 64, mixed[:128], mixed[128:])
            att_ref[b, :, low : low + 128] = mixed.astype(BF16)
    for two in range(4):
        parts = []
        for b in (2 * two, 2 * two + 1):
            value = dot32(att_ref[b][:, :C], wo_ref[...])
            parts.append(value + own_ref[:, b].reshape(128, C).astype(F32))
        for f in range(16):
            rows = jnp.concatenate([p[8 * f : 8 * f + 8] for p in parts], axis=0)
            out_ref[f // 4, f % 4, 16 * two : 16 * two + 16, :] = rows.astype(BF16)


def vmem(count):
    return [pl.BlockSpec(memory_space=pltpu.VMEM)] * count


def body(
    latents, levels, conv_first, emb_weight, conv_second, ln_gain, w_query, w_key, w_value, w_out
):
    here = lax.axis_index("height")
    tm = lax.axis_index("tm")
    send = lax.dynamic_slice_in_dim(latents, 2 * (1 - here), 2, axis=0)
    got = lax.ppermute(send, "height", [(0, 1), (1, 0)])
    first, second = pack_conv(conv_first), pack_conv(conv_second)
    emb = level_embedding(levels, emb_weight)
    ids = jnp.arange(C) // (C // GROUPS)
    group_map = (ids[:, None] == ids[None, :]).astype(BF16)
    wide = ((0, 0), (0, 64))
    wq = jnp.pad(w_query * jnp.asarray(0.125, BF16), wide)
    wkv = jnp.concatenate([jnp.pad(w_key, wide), jnp.pad(w_value, wide)], axis=1)

    chunks = pl.pallas_call(
        block_kernel,
        out_shape=jax.ShapeDtypeStruct((8, 8, 16, C), BF16),
        in_specs=[pl.BlockSpec(memory_space=pl.ANY)] * 4 + vmem(2),
        out_specs=pl.BlockSpec(memory_space=pltpu.VMEM),
        scratch_shapes=[
            pltpu.VMEM((2, 4, COLS, C), BF16),
            pltpu.VMEM((2, CELLS, 1024), BF16),
            pltpu.VMEM((2, CELLS, 960), F32),
            pltpu.VMEM((2, CELLS, C), F32),
            pltpu.VMEM((1024, 960), BF16),
            pltpu.VMEM((1024, 960), BF16),
            pltpu.SemaphoreType.DMA((6,)),
        ],
        compiler_params=pltpu.CompilerParams(vmem_limit_bytes=40 * 2**20),
        name="resblock",
    )(latents, got, first, second, emb, group_map)

    size = lax.axis_size("tm")
    rings = [[8 * i + j for j in range(8)] for i in range(size // 4)]
    own = lax.all_to_all(chunks, AXES, 0, 0, tiled=True, axis_index_groups=rings)
    up = [(i, i + 4) for i in range(size - 4)]
    prev = lax.ppermute(own[4:], "tm", up)
    later = lax.ppermute(own[:4], "tm", [(j, i) for i, j in up])
    base = (tm // 4 * 16).astype(jnp.int32).reshape(1, 1)
    mixed = pl.pallas_call(
        attention_kernel,
        out_shape=jax.ShapeDtypeStruct((4, 4, 64, C), BF16),
        in_specs=[pl.BlockSpec(memory_space=pltpu.SMEM)] + vmem(7),
        out_specs=pl.BlockSpec(memory_space=pltpu.VMEM),
        scratch_shapes=[
            pltpu.VMEM((8, 256, C), BF16),
            pltpu.VMEM((8, 128, 384), BF16),
            pltpu.VMEM((8, 256, 768), BF16),
            pltpu.VMEM((8, 128, 384), BF16),
        ],
        compiler_params=pltpu.CompilerParams(vmem_limit_bytes=40 * 2**20),
        name="window_attention",
    )(base, own, prev, later, ln_gain.reshape(1, C), wq, wkv, w_out)
    quads = [[4 * i + j for j in range(4)] for i in range(size // 4)]
    home = lax.all_to_all(mixed, "tm", 0, 0, tiled=True, axis_index_groups=quads)
    return jnp.transpose(home, (1, 0, 2, 3)).reshape(4, 2, COLS, C)


def solution(mesh):
    placed = (P("tm", "height", None, None), P("tm"), P(), P(), P(), P(), P(), P(), P(), P())
    return jax.shard_map(
        body, mesh=mesh, in_specs=placed, out_specs=P("tm", "height", None, None), check_vma=False
    )
```

profile of v0, /device:TPU:7, one launch (start us, length us, event | category | flops | bytes accessed | tf_op | source)
XLA Modules:
  0.0 101.4 jit_solution(7826673152838280906)
XLA Ops:
  0.0 1.5 %copy.20.own_ref = bf16[4,2,128,320]{3,2,1,0:T(8,128)(2,1)S(1)} copy(bf16[4,2,128,320]{2,3,1,0:T(8,128)(2,1)} %param.10) | data formatting | bytes 1310720 | tf_op args[0]
  1.5 0.8 constant_dynamic-slice_fusion
  2.3 2.9 %collective-permute-start = (bf16[2,2,128,320]{3,2,1,0:T(8,128)(2,1)}, bf16[2,2,128,320]{3,2,1,0:T(8,128)(2,1)S(1)}, u32[]{:S(2)}, u32[]{:S(2)}) collective-permute-start(bf16[2,2,128,320]{3,2,1,0:T(8,128)(2,1)} %constant_dynamic-slice_fusion), channel_id=1, source_target_pairs={{0,1},{1,0},{2,3},{3,2},{4,5},{5,4},{6,7},{7,6},{8,9},{9,8},{10,11... | collective-permute-start | bytes 983048 | tf_op jit(solution)/shard_map/ppermute | solution.py:246
  5.2 4.2 %copy.14 = bf16[3,3,320,320]{2,3,0,1:T(8,128)(2,1)} copy(bf16[3,3,320,320]{3,2,1,0:T(8,128)(2,1)} %param.12) | data formatting | bytes 3686400 | tf_op args[2]
  9.4 1.7 %slice.40 = bf16[3,320,3,256]{1,3,2,0:T(8,128)(2,1)S(1)} slice(bf16[3,320,3,320]{1,3,2,0:T(8,128)(2,1)} %bitcast.18), slice={[0:3], [0:320], [0:3], [0:256]} | slice | bytes 2949120 | tf_op jit(solution)/shard_map/slice | solution.py:32
  11.1 1.8 %slice.41 = bf16[3,320,3,64]{1,3,2,0:T(8,128)(2,1)} slice(bf16[3,320,3,320]{1,3,2,0:T(8,128)(2,1)} %bitcast.19), slice={[0:3], [0:320], [0:3], [256:320]} | slice | bytes 737280 | tf_op jit(solution)/shard_map/slice | solution.py:33
  13.0 4.2 %copy.17 = bf16[3,3,320,320]{2,3,0,1:T(8,128)(2,1)} copy(bf16[3,3,320,320]{3,2,1,0:T(8,128)(2,1)} %param.14) | data formatting | bytes 3686400 | tf_op args[4]
  17.2 1.7 %slice.44 = bf16[3,320,3,256]{1,3,2,0:T(8,128)(2,1)S(1)} slice(bf16[3,320,3,320]{1,3,2,0:T(8,128)(2,1)} %bitcast.20), slice={[0:3], [0:320], [0:3], [0:256]} | slice | bytes 2949120 | tf_op jit(solution)/shard_map/slice | solution.py:32
  18.9 1.1 %slice.45 = bf16[3,320,3,64]{1,3,2,0:T(8,128)(2,1)S(1)} slice(bf16[3,320,3,320]{1,3,2,0:T(8,128)(2,1)} %bitcast.21), slice={[0:3], [0:320], [0:3], [256:320]} | slice | bytes 737280 | tf_op jit(solution)/shard_map/slice | solution.py:33
  20.0 1.2 %fusion.1 = bf16[3,256,960]{1,2,0:T(8,128)(2,1)} fusion(bf16[3,320,768]{1,2,0:T(8,128)(2,1)S(1)} %bitcast.14, bf16[3,320,192]{1,2,0:T(8,128)(2,1)S(1)} %bitcast.24), kind=kLoop, calls=%fused_computation.7 | loop fusion | flops 2949120 | bytes 3317760 | tf_op jit(solution)/shard_map/concatenate | solution.py:30
  21.2 1.0 pad_maximum_fusion.1
  22.2 1.2 %fusion = bf16[3,256,960]{1,2,0:T(8,128)(2,1)} fusion(bf16[3,320,768]{1,2,0:T(8,128)(2,1)S(1)} %bitcast.16, bf16[3,320,192]{1,2,0:T(8,128)(2,1)S(1)} %bitcast.26), kind=kLoop, calls=%fused_computation.6 | loop fusion | flops 2949120 | bytes 3317760 | tf_op jit(solution)/shard_map/concatenate | solution.py:30
  23.4 1.0 %pad_maximum_fusion = bf16[3,64,960]{1,2,0:T(8,128)(2,1)} fusion(bf16[3,320,192]{1,2,0:T(8,128)(2,1)S(1)} %bitcast.27, bf16[3,320,768]{1,2,0:T(8,128)(2,1)S(1)} %bitcast.17), kind=kLoop, calls=%fused_computation.12 | loop fusion | flops 737280 | bytes 2211840 | tf_op jit(solution)/shard_map/concatenate | solution.py:30
  24.5 1.7 %copy.15 = bf16[3,256,960]{2,1,0:T(8,128)(2,1)S(1)} copy(bf16[3,256,960]{1,2,0:T(8,128)(2,1)} %fusion.1) | data formatting | bytes 2949120 | tf_op jit(solution)/shard_map/slice | solution.py:37
  26.2 2.6 %copy.18 = bf16[3,256,960]{2,1,0:T(8,128)(2,1)} copy(bf16[3,256,960]{1,2,0:T(8,128)(2,1)} %fusion) | data formatting | bytes 2949120 | tf_op jit(solution)/shard_map/slice | solution.py:37
  28.8 1.4 %copy.16 = bf16[3,64,960]{2,1,0:T(8,128)(2,1)S(1)} copy(bf16[3,64,960]{1,2,0:T(8,128)(2,1)} %pad_maximum_fusion.1) | data formatting | bytes 737280 | tf_op jit(solution)/shard_map/slice | solution.py:37
  30.1 2.1 %copy.19 = bf16[3,64,960]{2,1,0:T(8,128)(2,1)} copy(bf16[3,64,960]{1,2,0:T(8,128)(2,1)} %pad_maximum_fusion) | data formatting | bytes 737280 | tf_op jit(solution)/shard_map/slice | solution.py:37
  32.3 0.1 compare_convert_fusion.group_ref
  32.5 0.1 multiply_cosine_fusion
  32.6 0.2 fusion.6.emb_ref
  32.8 4.6 %maximum_maximum_fusion.1 = (bf16[1024,960]{1,0:T(8,128)(2,1)S(1)}, bf16[1024,960]{1,0:T(8,128)(2,1)S(1)}) fusion(bf16[192,960]{1,0:T(8,128)(2,1)} %bitcast.31, bf16[768,960]{1,0:T(8,128)(2,1)} %bitcast.23, bf16[1024]{0:T(1024)(128)(2,1)S(1)} %pad.24.clone, bf16[192,960]{1,0:T(8,128)(2,1)S(1)} %bitcast.30, bf16[768,960]{1,0:T(8,128)(2,1)S(1)} %bitcast.22), kind=kLoop, calls=%fused_computation.5 | loop fusion | flops 10813440 | bytes 7620608 | tf_op jit(solution)/shard_map/concatenate | solution.py:38
  37.4 10.7 %resblock.1 = bf16[8,8,16,320]{3,2,1,0:T(8,128)(2,1)} custom-call(bf16[4,2,128,320]{3,2,1,0:T(8,128)(2,1)S(1)} %copy.20.own_ref, bf16[2,2,128,320]{3,2,1,0:T(8,128)(2,1)S(1)} %collective-permute-done.got_ref, bf16[1024,960]{1,0:T(8,128)(2,1)S(1)} %get-tuple-element.8.first_ref, bf16[1024,960]{1,0:T(8,128)(2,1)S(1)} %get-tuple-element.7.second_ref, ...), custom_call_target="tpu_custom_call" | custom-call | tf_op jit(solution)/shard_map/resblock/pallas_call | solution.py:255
  48.1 4.6 %all-to-all-start = ((bf16[8,8,16,320]{3,2,1,0:T(8,128)(2,1)}), bf16[8,8,16,320]{3,2,1,0:T(8,128)(2,1)S(1)}, u32[]{:S(2)}, u32[]{:S(2)}) async-start(bf16[8,8,16,320]{3,2,1,0:T(8,128)(2,1)} %resblock.1), calls=%async_computation | async-start | bytes 1572864 | tf_op jit(solution)/shard_map/all_to_all | solution.py:275
  52.6 12.2 %all-to-all-done.own_ref = bf16[8,8,16,320]{3,2,1,0:T(8,128)(2,1)S(1)} async-done(((bf16[8,8,16,320]{3,2,1,0:T(8,128)(2,1)}), bf16[8,8,16,320]{3,2,1,0:T(8,128)(2,1)S(1)}, u32[]{:S(2)}, u32[]{:S(2)}) %all-to-all-start) | async-done | bytes 655392 | tf_op jit(solution)/shard_map/all_to_all | solution.py:275
  64.9 3.5 %collective-permute-start.1 = (bf16[4,8,16,320]{3,2,1,0:T(8,128)(2,1)S(1)}, bf16[4,8,16,320]{3,2,1,0:T(8,128)(2,1)S(1)}, u32[]{:S(2)}, u32[]{:S(2)}) collective-permute-start(bf16[4,8,16,320]{3,2,1,0:T(8,128)(2,1)S(1)} %get-tuple-element.6), channel_id=1, source_target_pairs={{0,8},{2,10},{4,12},{6,14},{8,16},{10,18},{12,20},{14,22},{16,24},... | collective-permute-start | bytes 983048 | tf_op jit(solution)/shard_map/ppermute | solution.py:277
  68.5 4.5 %collective-permute-start.2 = (bf16[4,8,16,320]{3,2,1,0:T(8,128)(2,1)S(1)}, bf16[4,8,16,320]{3,2,1,0:T(8,128)(2,1)S(1)}, u32[]{:S(2)}, u32[]{:S(2)}) collective-permute-start(bf16[4,8,16,320]{3,2,1,0:T(8,128)(2,1)S(1)} %get-tuple-element.5), channel_id=1, source_target_pairs={{8,0},{10,2},{12,4},{14,6},{16,8},{18,10},{20,12},{22,14},{24,16},... | collective-permute-start | bytes 983048 | tf_op jit(solution)/shard_map/ppermute | solution.py:278
  73.1 1.0 fusion.4.wkv_ref
  74.1 5.9 %collective-permute-done.1.prev_ref = bf16[4,8,16,320]{3,2,1,0:T(8,128)(2,1)S(1)} collective-permute-done((bf16[4,8,16,320]{3,2,1,0:T(8,128)(2,1)S(1)}, bf16[4,8,16,320]{3,2,1,0:T(8,128)(2,1)S(1)}, u32[]{:S(2)}, u32[]{:S(2)}) %collective-permute-start.1) | collective-permute-done | bytes 327712 | tf_op jit(solution)/shard_map/ppermute | solution.py:277
  80.0 0.9 collective-permute-done.2.next_ref
  80.9 5.0 %window_attention.1 = bf16[4,4,64,320]{3,2,1,0:T(8,128)(2,1)S(1)} custom-call(s32[1,1]{1,0:T(1,128)} %bitcast.base_ref, bf16[8,8,16,320]{3,2,1,0:T(8,128)(2,1)S(1)} %all-to-all-done.own_ref, bf16[4,8,16,320]{3,2,1,0:T(8,128)(2,1)S(1)} %collective-permute-done.1.prev_ref, bf16[4,8,16,320]{3,2,1,0:T(8,128)(2,1)S(1)} %collective-permute-done.2.next_ref, ...), custom_call_target="tpu_custom_call" | custom-call | tf_op jit(solution)/shard_map/window_attention/pallas_call | solution.py:280
  85.9 14.2 %all_to_all.10 = bf16[4,4,64,320]{3,2,1,0:T(8,128)(2,1)S(1)} all-to-all(bf16[4,4,64,320]{3,2,1,0:T(8,128)(2,1)S(1)} %window_attention.1), channel_id=1, replica_groups={{0,2,4,6},{8,10,12,14},{16,18,20,22},{24,26,28,30},{32,34,36,38},{40,42..., dimensions={0} | all-to-all | bytes 1310720 | tf_op jit(solution)/shard_map/all_to_all | solution.py:295
  100.3 1.1 %copy.22 = bf16[4,2,128,320]{2,3,1,0:T(8,128)(2,1)} copy(bf16[4,2,128,320]{3,2,1,0:T(8,128)(2,1)S(1)} %bitcast.29) | data formatting | bytes 1310720 | tf_op jit(solution)/shard_map/reshape | solution.py:296
  (25 shorter events, 0.4 us)
Async XLA Ops:
  0.0 32.6 %copy-start = (bf16[320,320]{1,0:T(8,128)(2,1)S(1)}, bf16[320,320]{1,0:T(8,128)(2,1)}, u32[]{:S(2)}) copy-start(bf16[320,320]{1,0:T(8,128)(2,1)} %param.13) | copy-start | bytes 614404
  2.3 35.1 %collective-permute-start = (bf16[2,2,128,320]{3,2,1,0:T(8,128)(2,1)}, bf16[2,2,128,320]{3,2,1,0:T(8,128)(2,1)S(1)}, u32[]{:S(2)}, u32[]{:S(2)}) collective-permute-start(bf16[2,2,128,320]{3,2,1,0:T(8,128)(2,1)} %constant_dynamic-slice_fusion), channel_id=1, source_target_pairs={{0,1},{1,0},{2,3},{3,2},{4,5},{5,4},{6,7},{7,6},{8,9},{9,8},{10,11... | collective-permute-start | bytes 983048 | tf_op jit(solution)/shard_map/ppermute | solution.py:246
  17.2 2.8 %copy-start.2 = (bf16[3,320,3,64]{1,3,2,0:T(8,128)(2,1)S(1)}, bf16[3,320,3,64]{1,3,2,0:T(8,128)(2,1)}, u32[]{:S(2)}) copy-start(bf16[3,320,3,64]{1,3,2,0:T(8,128)(2,1)} %slice.41) | copy-start | bytes 1105924
  26.2 6.1 %copy-start.6 = (s32[4]{0:T(128)S(1)}, s32[4]{0:T(128)}, u32[]{:S(2)}) copy-start(s32[4]{0:T(128)} %param.11) | copy-start | bytes 52
  48.1 24.9 %copy-start.3 = (bf16[320,320]{1,0:T(8,128)(2,1)S(1)}, bf16[320,320]{1,0:T(8,128)(2,1)}, u32[]{:S(2)}) copy-start(bf16[320,320]{1,0:T(8,128)(2,1)} %param.16) | copy-start | bytes 614404
  48.1 25.0 %copy-start.5 = (f32[320]{0:T(512)S(1)}, f32[320]{0:T(512)}, u32[]{:S(2)}) copy-start(f32[320]{0:T(512)} %param.15) | copy-start | bytes 3844
  48.1 25.0 %copy-start.4 = (bf16[320,320]{1,0:T(8,128)(2,1)S(1)}, bf16[320,320]{1,0:T(8,128)(2,1)}, u32[]{:S(2)}) copy-start(bf16[320,320]{1,0:T(8,128)(2,1)} %param.18) | copy-start | bytes 614404
  48.1 16.8 %all-to-all-start = ((bf16[8,8,16,320]{3,2,1,0:T(8,128)(2,1)}), bf16[8,8,16,320]{3,2,1,0:T(8,128)(2,1)S(1)}, u32[]{:S(2)}, u32[]{:S(2)}) async-start(bf16[8,8,16,320]{3,2,1,0:T(8,128)(2,1)} %resblock.1), calls=%async_computation | async-start | bytes 1572864 | tf_op jit(solution)/shard_map/all_to_all | solution.py:275
  52.6 28.2 %copy-start.1 = (bf16[320,320]{1,0:T(8,128)(2,1)S(1)}, bf16[320,320]{1,0:T(8,128)(2,1)}, u32[]{:S(2)}) copy-start(bf16[320,320]{1,0:T(8,128)(2,1)} %wo_ref.1) | copy-start | bytes 614404
  64.9 15.1 %collective-permute-start.1 = (bf16[4,8,16,320]{3,2,1,0:T(8,128)(2,1)S(1)}, bf16[4,8,16,320]{3,2,1,0:T(8,128)(2,1)S(1)}, u32[]{:S(2)}, u32[]{:S(2)}) collective-permute-start(bf16[4,8,16,320]{3,2,1,0:T(8,128)(2,1)S(1)} %get-tuple-element.6), channel_id=1, source_target_pairs={{0,8},{2,10},{4,12},{6,14},{8,16},{10,18},{12,20},{14,22},{16,24},... | collective-permute-start | bytes 983048 | tf_op jit(solution)/shard_map/ppermute | solution.py:277
  68.5 12.4 %collective-permute-start.2 = (bf16[4,8,16,320]{3,2,1,0:T(8,128)(2,1)S(1)}, bf16[4,8,16,320]{3,2,1,0:T(8,128)(2,1)S(1)}, u32[]{:S(2)}, u32[]{:S(2)}) collective-permute-start(bf16[4,8,16,320]{3,2,1,0:T(8,128)(2,1)S(1)} %get-tuple-element.5), channel_id=1, source_target_pairs={{8,0},{10,2},{12,4},{14,6},{16,8},{18,10},{20,12},{22,14},{24,16},... | collective-permute-start | bytes 983048 | tf_op jit(solution)/shard_map/ppermute | solution.py:278
where the time goes:
time: 103 us; the launch traced here: 101 us
  local copies, waits for them, and re-layouts  26.2 us (25%)
  waiting for transfers between devices  19 us (18%)
  Pallas kernels  15.7 us (15%)
  starting transfers between devices  15.5 us (15%)
  blocking collectives  14.2 us (14%)
  other arithmetic  10.3 us (10%)
    all_to_all x1, blocking collectives, body(): lax.all_to_all(mixed, 'tm', 0, 0, tiled=True, axis_index_groups=quads)  14.2 us
    all_to_all x1, waiting for transfers between devices, body(): lax.all_to_all(chunks, AXES, 0, 0, tiled=True, axis_index_groups=rings)  12.2 us
    pallas_call x1, Pallas kernels, body(): pl.pallas_call(block_kernel, out_shape=jax.ShapeDtypeStruct((8, 8, 16, C)...  10.7 us
    unnamed x17, local copies, waits for them, and re-layouts  9.99 us
    ppermute x1, waiting for transfers between devices, body(): prev = lax.ppermute(own[4:], 'tm', up)  5.9 us
    pallas_call x1, Pallas kernels, body(): pl.pallas_call(attention_kernel, out_shape=jax.ShapeDtypeStruct((4, 4, 64...  5.03 us
    concatenate x1, other arithmetic, pack_conv(): jnp.concatenate(rows + [jnp.zeros((TAIL, 3 * C), weight.dtype)], axis=0)  4.56 us
    all_to_all x1, starting transfers between devices, body(): lax.all_to_all(chunks, AXES, 0, 0, tiled=True, axis_index_groups=rings)  4.55 us
  transfers between devices with their start and end apart: 4, of which 3 were waited for; matrix products, arithmetic and copies ran while one was open for 33% of the time, Pallas kernels for 0%

commit v1 on v0

--- a/solution.py
+++ b/solution.py
@@ -25,17 +25,16 @@
     return jnp.dot(a, b, preferred_element_type=F32)
 
 
-def pack_conv(weight):
-    by_input = jnp.transpose(weight, (1, 2, 0, 3))
-    columns = jnp.concatenate(
-        [
-            by_input[..., :MAIN].reshape(3, C, 3 * MAIN),
-            by_input[..., MAIN:].reshape(3, C, 3 * TAIL),
-        ],
-        axis=2,
-    )
-    rows = [columns[:, :MAIN].reshape(3 * MAIN, 3 * C), columns[:, MAIN:].reshape(3 * TAIL, 3 * C)]
-    return jnp.concatenate(rows + [jnp.zeros((TAIL, 3 * C), weight.dtype)], axis=0)
+def pack_kernel(first_ref, second_ref, first_out, second_out):
+    for source, target in ((first_ref, first_out), (second_ref, second_out)):
+        for dx in range(3):
+            for lo, hi, row in ((0, MAIN, dx * MAIN), (MAIN, C, 3 * MAIN + dx * TAIL)):
+                rows = slice(row, row + hi - lo)
+                for dy in range(3):
+                    target[rows, dy * MAIN : (dy + 1) * MAIN] = source[dy, dx, lo:hi, :MAIN]
+                tails = [source[dy, dx, lo:hi, MAIN:] for dy in range(3)]
+                target[rows, 3 * MAIN :] = jnp.concatenate(tails, axis=1)
+        target[3 * C :, :] = jnp.zeros((TAIL, 3 * C), BF16)
 
 
 def level_embedding(levels, emb_weight):
@@ -117,16 +116,17 @@
 
 
 def block_kernel(
-    own_ref, got_ref, first_ref, second_ref, emb_ref, group_ref, out_ref,
-    x_ref, act_ref, taps_ref, res_ref, w1_ref, w2_ref, sems,
+    own_ref, got_ref, first_ref, second_ref, emb_ref, group_ref, *rest
 ):
+    outs, (raw_ref, x_ref, act_ref, taps_ref, res_ref, w1_ref, w2_ref, sems) = rest[:8], rest[8:]
     here = lax.axis_index("height")
+    ring = 2 * lax.rem(lax.axis_index("tm"), 4) + here
     copies = []
     for frame in range(2):
         for side, source in ((here, own_ref.at[2 * here + frame]), (1 - here, got_ref.at[frame])):
             copies.append(
                 pltpu.make_async_copy(
-                    source, x_ref.at[frame, pl.ds(2 * side, 2)], sems.at[len(copies)]
+                    source, raw_ref.at[frame, pl.ds(2 * side, 2)], sems.at[len(copies)]
                 )
             )
     weights = [
@@ -138,12 +138,13 @@
     group_map = group_ref[...]
 
     def hidden(frame):
-        value = x_ref[frame].reshape(CELLS, C).astype(F32)
-        return value[:, :MAIN], value[:, MAIN:]
+        return x_ref[frame, :, :MAIN], x_ref[frame, :, MAIN:]
 
     for frame in range(2):
         copies[2 * frame].wait()
         copies[2 * frame + 1].wait()
+        for row in range(4):
+            x_ref[frame, row * COLS : (row + 1) * COLS, :] = raw_ref[frame, row].astype(F32).T
         conv_input(act_ref.at[frame], *hidden(frame), group_map)
     weights[0].wait()
     for frame in range(2):
@@ -158,26 +159,44 @@
         old_main, old_tail = hidden(frame)
         res_ref[frame, :, :MAIN] = main + old_main
         res_ref[frame, :, MAIN:] = tail + old_tail
-    for t in range(4):
-        for h in range(2):
-            for b in range(8):
-                start = 256 * h + 64 * t + 8 * b
-                pair = [res_ref[f, start : start + 8, :] for f in range(2)]
-                out_ref[2 * t + h, b] = jnp.concatenate(pair, axis=0).astype(BF16)
+    for k in range(8):
+        other = lax.bitwise_xor(ring, k)
+        base = 256 * lax.rem(other, 2) + 64 * lax.div(other, 2)
+        for b in range(8):
+            start = pl.multiple_of(base + 8 * b, 8)
+            pair = [res_ref[f, pl.ds(start, 8), :] for f in range(2)]
+            outs[k][b] = jnp.concatenate(pair, axis=0).astype(BF16)
+
+
+def gather_kernel(*refs):
+    pieces, (own_ref, near_ref, far_ref) = refs[:8], refs[8:]
+    tm = lax.axis_index("tm")
+    ring = 2 * lax.rem(tm, 4) + lax.axis_index("height")
+    odd = lax.rem(lax.div(tm, 4), 2)
+    for k in range(8):
+        own_ref[lax.bitwise_xor(ring, k)] = pieces[k][...]
+    for j in range(4):
+        near_ref[j] = own_ref[4 * (1 - odd) + j]
+        far_ref[j] = own_ref[4 * odd + j]
 
 
 def attention_kernel(
-    base_ref, own_ref, prev_ref, next_ref, gain_ref, wq_ref, wkv_ref, wo_ref, out_ref,
-    norm_ref, q_ref, kv_ref, att_ref,
+    own_ref, near_ref, far_ref, gain_ref, wq_ref, wk_ref, wv_ref, wo_ref, *rest
 ):
-    base = base_ref[0, 0]
+    outs, (halo_ref, norm_ref, q_ref, kv_ref, att_ref, mixed_ref) = rest[:4], rest[4:]
+    tm = lax.axis_index("tm")
+    quad = lax.rem(tm, 4)
+    base = lax.div(tm, 4) * 16
+    odd = lax.rem(lax.div(tm, 4), 2)
+    halo_ref[1 - odd] = near_ref[...]
+    halo_ref[odd] = far_ref[...]
     gain = gain_ref[...]
     for b in range(8):
         value = jnp.concatenate(
             [
-                prev_ref[:, b].reshape(64, C),
+                halo_ref[0, :, b].reshape(64, C),
                 own_ref[:, b].reshape(128, C),
-                next_ref[:, b].reshape(64, C),
+                halo_ref[1, :, b].reshape(64, C),
             ],
             axis=0,
         ).astype(F32)
@@ -186,16 +205,20 @@
         var = jnp.mean(centred * centred, axis=-1, keepdims=True)
         normed = (centred * lax.rsqrt(var + 1e-05) * gain).astype(BF16)
         norm_ref[b] = normed
+    pad = jnp.zeros((256, TAIL), BF16)
     for b in range(8):
         normed = norm_ref[b]
-        q_ref[b] = dot32(normed[64:192], wq_ref[...]).astype(BF16)
-        kv_ref[b] = dot32(normed, wkv_ref[...]).astype(BF16)
+        q_ref[b, :, :C] = (dot32(normed[64:192], wq_ref[...]) * 0.125).astype(BF16)
+        q_ref[b, :, C:] = pad[:128]
+        for at, ref in ((0, wk_ref), (384, wv_ref)):
+            kv_ref[b, :, at : at + C] = dot32(normed, ref[...]).astype(BF16)
+            kv_ref[b, :, at + C : at + 384] = pad
     row = lax.broadcasted_iota(jnp.int32, (128, 256), 0)
     col = lax.broadcasted_iota(jnp.int32, (128, 256), 1)
     away = col // 8 - 8 - row // 8
     frame = base + col // 8 - 8
     keep = (row % 8 == col % 8) & (away >= -(WINDOW // 2)) & (away < WINDOW // 2)
-    keep = keep & (frame >= 0) & (frame < 256)
+    keep = keep & (frame >= 0) & (frame < 4 * lax.axis_size("tm"))
     bias = jnp.where(keep, 0.0, -1e30).astype(F32)
     bias2 = jnp.concatenate([bias, bias], axis=0)
     ones = jnp.ones((256, 128), BF16)
@@ -206,14 +229,13 @@
             q = q_ref[b, :, low : low + 128]
             k = kv_ref[b, :, low : low + 128]
             v = kv_ref[b, :, 384 + low : 384 + low + 128]
-            zero = jnp.zeros_like(q)
-            q0 = jnp.where(lane < 64, q, zero)
+            add = bias
             if pair < 2:
-                q = jnp.concatenate([q0, jnp.where(lane < 64, zero, q)], axis=0)
+                zero = jnp.zeros_like(q)
+                q = jnp.concatenate(
+                    [jnp.where(lane < 64, q, zero), jnp.where(lane < 64, zero, q)], axis=0
+                )
                 add = bias2
-            else:
-                q = q0
-                add = bias
             score = lax.dot_general(
                 q, k, (((1,), (1,)), ((), ())), preferred_element_type=F32
             )
@@ -230,7 +252,24 @@
             parts.append(value + own_ref[:, b].reshape(128, C).astype(F32))
         for f in range(16):
             rows = jnp.concatenate([p[8 * f : 8 * f + 8] for p in parts], axis=0)
-            out_ref[f // 4, f % 4, 16 * two : 16 * two + 16, :] = rows.astype(BF16)
+            mixed_ref[f, 16 * two : 16 * two + 16, :] = rows.astype(BF16)
+    for k in range(4):
+        other = lax.bitwise_xor(quad, k)
+        for f in range(4):
+            outs[k][f] = mixed_ref[4 * other + f]
+
+
+def home_kernel(*refs):
+    pieces, out_ref, cells_ref = refs[:4], refs[4], refs[5]
+    quad = lax.rem(lax.axis_index("tm"), 4)
+    for k in range(4):
+        start = pl.multiple_of(64 * lax.bitwise_xor(quad, k), 64)
+        for f in range(4):
+            cells_ref[f, pl.ds(start, 64), :] = pieces[k][f]
+    for f in range(4):
+        for row in range(2):
+            value = cells_ref[f, row * COLS : (row + 1) * COLS, :].astype(F32)
+            out_ref[f, row] = value.T.astype(BF16)
 
 
 def vmem(count):
@@ -241,24 +280,31 @@
     latents, levels, conv_first, emb_weight, conv_second, ln_gain, w_query, w_key, w_value, w_out
 ):
     here = lax.axis_index("height")
-    tm = lax.axis_index("tm")
+    size = lax.axis_size("tm")
+    latents = jnp.transpose(latents, (0, 1, 3, 2))
     send = lax.dynamic_slice_in_dim(latents, 2 * (1 - here), 2, axis=0)
     got = lax.ppermute(send, "height", [(0, 1), (1, 0)])
-    first, second = pack_conv(conv_first), pack_conv(conv_second)
+    first, second = pl.pallas_call(
+        pack_kernel,
+        out_shape=[jax.ShapeDtypeStruct((1024, 3 * C), BF16)] * 2,
+        in_specs=vmem(2),
+        out_specs=vmem(2),
+        compiler_params=pltpu.CompilerParams(vmem_limit_bytes=40 * 2**20),
+        cost_estimate=pl.CostEstimate(flops=0, bytes_accessed=8_000_000, transcendentals=0),
+        name="pack_weights",
+    )(conv_first, conv_second)
     emb = level_embedding(levels, emb_weight)
     ids = jnp.arange(C) // (C // GROUPS)
     group_map = (ids[:, None] == ids[None, :]).astype(BF16)
-    wide = ((0, 0), (0, 64))
-    wq = jnp.pad(w_query * jnp.asarray(0.125, BF16), wide)
-    wkv = jnp.concatenate([jnp.pad(w_key, wide), jnp.pad(w_value, wide)], axis=1)
-
-    chunks = pl.pallas_call(
+
+    pieces = pl.pallas_call(
         block_kernel,
-        out_shape=jax.ShapeDtypeStruct((8, 8, 16, C), BF16),
+        out_shape=[jax.ShapeDtypeStruct((8, 16, C), BF16)] * 8,
         in_specs=[pl.BlockSpec(memory_space=pl.ANY)] * 4 + vmem(2),
-        out_specs=pl.BlockSpec(memory_space=pltpu.VMEM),
+        out_specs=vmem(8),
         scratch_shapes=[
-            pltpu.VMEM((2, 4, COLS, C), BF16),
+            pltpu.VMEM((2, 4, C, COLS), BF16),
+            pltpu.VMEM((2, CELLS, C), F32),
             pltpu.VMEM((2, CELLS, 1024), BF16),
             pltpu.VMEM((2, CELLS, 960), F32),
             pltpu.VMEM((2, CELLS, C), F32),
@@ -270,30 +316,48 @@
         name="resblock",
     )(latents, got, first, second, emb, group_map)
 
-    size = lax.axis_size("tm")
-    rings = [[8 * i + j for j in range(8)] for i in range(size // 4)]
-    own = lax.all_to_all(chunks, AXES, 0, 0, tiled=True, axis_index_groups=rings)
-    up = [(i, i + 4) for i in range(size - 4)]
-    prev = lax.ppermute(own[4:], "tm", up)
-    later = lax.ppermute(own[:4], "tm", [(j, i) for i, j in up])
-    base = (tm // 4 * 16).astype(jnp.int32).reshape(1, 1)
-    mixed = pl.pallas_call(
+    swaps = [[(i, i ^ k) for i in range(2 * size)] for k in range(8)]
+    pieces = [pieces[0]] + [lax.ppermute(pieces[k], AXES, swaps[k]) for k in range(1, 8)]
+    half = jax.ShapeDtypeStruct((4, 8, 16, C), BF16)
+    own, near, far = pl.pallas_call(
+        gather_kernel,
+        out_shape=[jax.ShapeDtypeStruct((8, 8, 16, C), BF16), half, half],
+        in_specs=vmem(8),
+        out_specs=vmem(3),
+        compiler_params=pltpu.CompilerParams(vmem_limit_bytes=40 * 2**20),
+        name="by_frame",
+    )(*pieces)
+    up = [(i, i + 4) for i in range(size - 4) if i // 4 % 2 == 1]
+    far = lax.ppermute(far, "tm", up + [(j, i) for i, j in up])
+    near = lax.ppermute(near, "tm", [(i, i ^ 4) for i in range(size)])
+    pieces = pl.pallas_call(
         attention_kernel,
-        out_shape=jax.ShapeDtypeStruct((4, 4, 64, C), BF16),
-        in_specs=[pl.BlockSpec(memory_space=pltpu.SMEM)] + vmem(7),
-        out_specs=pl.BlockSpec(memory_space=pltpu.VMEM),
+        out_shape=[jax.ShapeDtypeStruct((4, 64, C), BF16)] * 4,
+        in_specs=vmem(8),
+        out_specs=vmem(4),
         scratch_shapes=[
+            pltpu.VMEM((2, 4, 8, 16, C), BF16),
             pltpu.VMEM((8, 256, C), BF16),
             pltpu.VMEM((8, 128, 384), BF16),
             pltpu.VMEM((8, 256, 768), BF16),
             pltpu.VMEM((8, 128, 384), BF16),
+            pltpu.VMEM((16, 64, C), BF16),
         ],
         compiler_params=pltpu.CompilerParams(vmem_limit_bytes=40 * 2**20),
         name="window_attention",
-    )(base, own, prev, later, ln_gain.reshape(1, C), wq, wkv, w_out)
-    quads = [[4 * i + j for j in range(4)] for i in range(size // 4)]
-    home = lax.all_to_all(mixed, "tm", 0, 0, tiled=True, axis_index_groups=quads)
-    return jnp.transpose(home, (1, 0, 2, 3)).reshape(4, 2, COLS, C)
+    )(own, near, far, ln_gain.reshape(1, C), w_query, w_key, w_value, w_out)
+    swaps = [[(i, i ^ k) for i in range(size)] for k in range(4)]
+    pieces = [pieces[0]] + [lax.ppermute(pieces[k], "tm", swaps[k]) for k in range(1, 4)]
+    home = pl.pallas_call(
+        home_kernel,
+        out_shape=jax.ShapeDtypeStruct((4, 2, C, COLS), BF16),
+        in_specs=vmem(4),
+        out_specs=pl.BlockSpec(memory_space=pltpu.VMEM),
+        scratch_shapes=[pltpu.VMEM((4, 256, C), BF16)],
+        compiler_params=pltpu.CompilerParams(vmem_limit_bytes=40 * 2**20),
+        name="home",
+    )(*pieces)
+    return jnp.transpose(home, (0, 1, 3, 2))
 
 
 def solution(mesh):

time: 103 us -> 70.9 us (0.69); the launches traced: 101 us -> 70.7 us
  local copies, waits for them, and re-layouts: 26.2 us -> 4.31 us
  blocking collectives: 14.2 us -> 0 us
  other arithmetic: 10.3 us -> 0.9 us
  starting transfers between devices: 15.5 us -> 23.1 us
  waiting for transfers between devices: 19 us -> 25.2 us
  Pallas kernels: 15.7 us -> 16.8 us
    ppermute x2 -> x12, waiting for transfers between devices: 6.77 us -> 23 us  [the longest x3 9.13 us: body(): lax.ppermute(pieces[k], 'tm', swaps[k])]
    all_to_all x1 -> x0, blocking collectives: 14.2 us -> none  [body(): lax.all_to_all(mixed, 'tm', 0, 0, tiled=True, axis_index_groups=quads)]
    slice x9 -> x0, local copies, waits for them, and re-layouts: 14.1 us -> none  [the longest x2 4.28 us: pack_conv(): columns[:, :MAIN].reshape(3 * MAIN, 3 * C)]
    all_to_all x1 -> x0, waiting for transfers between devices: 12.2 us -> none  [body(): lax.all_to_all(chunks, AXES, 0, 0, tiled=True, axis_index_groups=rings)]
    ppermute x2 -> x12, starting transfers between devices: 8.03 us -> 20.1 us  [the longest x7 10.8 us: body(): lax.ppermute(pieces[k], AXES, swaps[k])]
    concatenate x6 -> x0, other arithmetic: 10 us -> none  [the longest x1 4.56 us: pack_conv(): jnp.concatenate(rows + [jnp.zeros((TAIL, 3 * C), weight.dtype)], axis=0)]
    unnamed x17 -> x18, local copies, waits for them, and re-layouts: 9.99 us -> 3.27 us
    all_to_all x1 -> x0, starting transfers between devices: 4.55 us -> none  [body(): lax.all_to_all(chunks, AXES, 0, 0, tiled=True, axis_index_groups=rings)]
  transfers between devices with their start and end apart: 4 -> 13, of which waited for: 3 -> 10; matrix products, arithmetic and copies ran while one was open for 33% -> 2% of each run, Pallas kernels for 0% -> 1%
where the time goes in v1:
time: 70.9 us; the launch traced here: 70.7 us
  waiting for transfers between devices  25.2 us (36%)
  starting transfers between devices  23.1 us (33%)
  Pallas kernels  16.8 us (24%)
  local copies, waits for them, and re-layouts  4.31 us (6%)
  other arithmetic  0.9 us (1%)
    ppermute x7, starting transfers between devices, body(): lax.ppermute(pieces[k], AXES, swaps[k])  10.8 us
    pallas_call x1, Pallas kernels, body(): pl.pallas_call(block_kernel, out_shape=[jax.ShapeDtypeStruct((8, 16, C),...  9.77 us
    ppermute x3, waiting for transfers between devices, body(): lax.ppermute(pieces[k], 'tm', swaps[k])  9.13 us
    pallas_call x1, Pallas kernels, body(): pl.pallas_call(attention_kernel, out_shape=[jax.ShapeDtypeStruct((4, 64,...  5.16 us
    ppermute x1, waiting for transfers between devices, body(): far = lax.ppermute(far, 'tm', up + [(j, i) for i, j in up])  5.03 us
    ppermute x1, waiting for transfers between devices, body(): near = lax.ppermute(near, 'tm', [(i, i ^ 4) for i in range(size)])  4.72 us
    ppermute x1, starting transfers between devices, body(): far = lax.ppermute(far, 'tm', up + [(j, i) for i, j in up])  4.58 us
    ppermute x7, waiting for transfers between devices, body(): lax.ppermute(pieces[k], AXES, swaps[k])  4.14 us
  transfers between devices with their start and end apart: 13, of which 10 were waited for; matrix products, arithmetic and copies ran while one was open for 2% of the time, Pallas kernels for 1%

profile of v1, /device:TPU:7, one launch (start us, length us, event | category | flops | bytes accessed | tf_op | source)
XLA Modules:
  0.0 70.7 jit_solution(10234821610357653438)
XLA Ops:
  0.0 1.0 %dynamic-slice_bitcast_fusion = bf16[2,2,320,128]{3,2,1,0:T(8,128)(2,1)S(1)} fusion(bf16[4,2,128,320]{2,3,1,0:T(8,128)(2,1)} %param.10, s32[]{:T(128)S(6)} %select_n.16), kind=kLoop, calls=%fused_computation.1 | loop fusion | bytes 655364 | tf_op jit(solution)/shard_map/dynamic_slice | solution.py:285
  1.0 3.0 %collective-permute-start = (bf16[2,2,320,128]{3,2,1,0:T(8,128)(2,1)S(1)}, bf16[2,2,320,128]{3,2,1,0:T(8,128)(2,1)S(1)}, u32[]{:S(2)}, u32[]{:S(2)}) collective-permute-start(bf16[2,2,320,128]{3,2,1,0:T(8,128)(2,1)S(1)} %dynamic-slice_bitcast_fusion), channel_id=1, source_target_pairs={{0,1},{1,0},{2,3},{3,2},{4,5},{5,4},{6,7},{7,6},{8,9},{9,8},{10,11... | collective-permute-start | bytes 983048 | tf_op jit(solution)/shard_map/ppermute | solution.py:286
  4.1 0.7 convert_element_type.16
  4.8 0.1 multiply_cosine_fusion
  5.0 1.6 %copy-done.1 = bf16[3,3,320,320]{3,2,1,0:T(8,128)(2,1)S(1)} copy-done((bf16[3,3,320,320]{3,2,1,0:T(8,128)(2,1)S(1)}, bf16[3,3,320,320]{3,2,1,0:T(8,128)(2,1)}, u32[]{:S(2)}) %copy-start.1) | copy-done | bytes 1843224
  6.6 1.6 %copy-done.2 = bf16[3,3,320,320]{3,2,1,0:T(8,128)(2,1)S(1)} copy-done((bf16[3,3,320,320]{3,2,1,0:T(8,128)(2,1)S(1)}, bf16[3,3,320,320]{3,2,1,0:T(8,128)(2,1)}, u32[]{:S(2)}) %copy-start.2) | copy-done | bytes 1843224
  8.2 0.6 pack_weights.1
  8.8 0.2 fusion.1.emb_ref
  9.0 2.2 %collective-permute-done.got_ref = bf16[2,2,320,128]{3,2,1,0:T(8,128)(2,1)S(1)} collective-permute-done((bf16[2,2,320,128]{3,2,1,0:T(8,128)(2,1)S(1)}, bf16[2,2,320,128]{3,2,1,0:T(8,128)(2,1)S(1)}, u32[]{:S(2)}, u32[]{:S(2)}) %collective-permute-start) | collective-permute-done | bytes 327712 | tf_op jit(solution)/shard_map/ppermute | solution.py:286
  11.2 9.8 %resblock.1 = (bf16[8,16,320]{2,1,0:T(8,128)(2,1)S(1)}, bf16[8,16,320]{2,1,0:T(8,128)(2,1)S(1)}, bf16[8,16,320]{2,1,0:T(8,128)(2,1)S(1)}, bf16[8,16,320]{2,1,0:T...) custom-call(bf16[4,2,320,128]{3,2,1,0:T(8,128)(2,1)S(1)} %bitcast.5,, ...), custom_call_target="tpu_custom_call" | custom-call | tf_op jit(solution)/shard_map/resblock/pallas_call | solution.py:300
  21.0 3.0 %collective-permute-start.1 = (bf16[8,16,320]{2,1,0:T(8,128)(2,1)S(1)}, bf16[8,16,320]{2,1,0:T(8,128)(2,1)S(1)}, u32[]{:S(2)}, u32[]{:S(2)}) collective-permute-start(bf16[8,16,320]{2,1,0:T(8,128)(2,1)S(1)} %get-tuple-element.25), channel_id=1, source_target_pairs={{0,1},{1,0},{2,3},{3,2},{4,5},{5,4},{6,7},{7,6},{8,9},{9,8},{10,11... | collective-permute-start | bytes 245768 | tf_op jit(solution)/shard_map/ppermute | solution.py:320
  24.0 1.8 %collective-permute-start.2 = (bf16[8,16,320]{2,1,0:T(8,128)(2,1)S(1)}, bf16[8,16,320]{2,1,0:T(8,128)(2,1)S(1)}, u32[]{:S(2)}, u32[]{:S(2)}) collective-permute-start(bf16[8,16,320]{2,1,0:T(8,128)(2,1)S(1)} %get-tuple-element.26), channel_id=1, source_target_pairs={{0,2},{1,3},{2,0},{3,1},{4,6},{5,7},{6,4},{7,5},{8,10},{9,11},{10,... | collective-permute-start | bytes 245768 | tf_op jit(solution)/shard_map/ppermute | solution.py:320
  25.9 1.2 %collective-permute-start.4 = (bf16[8,16,320]{2,1,0:T(8,128)(2,1)S(1)}, bf16[8,16,320]{2,1,0:T(8,128)(2,1)S(1)}, u32[]{:S(2)}, u32[]{:S(2)}) collective-permute-start(bf16[8,16,320]{2,1,0:T(8,128)(2,1)S(1)} %get-tuple-element.28), channel_id=1, source_target_pairs={{0,4},{1,5},{2,6},{3,7},{4,0},{5,1},{6,2},{7,3},{8,12},{9,13},{10,... | collective-permute-start | bytes 245768 | tf_op jit(solution)/shard_map/ppermute | solution.py:320
  27.1 1.9 %collective-permute-start.5 = (bf16[8,16,320]{2,1,0:T(8,128)(2,1)S(1)}, bf16[8,16,320]{2,1,0:T(8,128)(2,1)S(1)}, u32[]{:S(2)}, u32[]{:S(2)}) collective-permute-start(bf16[8,16,320]{2,1,0:T(8,128)(2,1)S(1)} %get-tuple-element.29), channel_id=1, source_target_pairs={{0,5},{1,4},{2,7},{3,6},{4,1},{5,0},{6,3},{7,2},{8,13},{9,12},{10,... | collective-permute-start | bytes 245768 | tf_op jit(solution)/shard_map/ppermute | solution.py:320
  29.0 1.4 %collective-permute-start.6 = (bf16[8,16,320]{2,1,0:T(8,128)(2,1)S(1)}, bf16[8,16,320]{2,1,0:T(8,128)(2,1)S(1)}, u32[]{:S(2)}, u32[]{:S(2)}) collective-permute-start(bf16[8,16,320]{2,1,0:T(8,128)(2,1)S(1)} %get-tuple-element.30), channel_id=1, source_target_pairs={{0,6},{1,7},{2,4},{3,5},{4,2},{5,3},{6,0},{7,1},{8,14},{9,15},{10,... | collective-permute-start | bytes 245768 | tf_op jit(solution)/shard_map/ppermute | solution.py:320
  30.3 1.5 %collective-permute-start.7 = (bf16[8,16,320]{2,1,0:T(8,128)(2,1)S(1)}, bf16[8,16,320]{2,1,0:T(8,128)(2,1)S(1)}, u32[]{:S(2)}, u32[]{:S(2)}) collective-permute-start(bf16[8,16,320]{2,1,0:T(8,128)(2,1)S(1)} %get-tuple-element.31), channel_id=1, source_target_pairs={{0,7},{1,6},{2,5},{3,4},{4,3},{5,2},{6,1},{7,0},{8,15},{9,14},{10,... | collective-permute-start | bytes 245768 | tf_op jit(solution)/shard_map/ppermute | solution.py:320
  31.8 0.6 collective-permute-done.3.refs_3_
  32.5 1.2 %collective-permute-done.5.refs_5_ = bf16[8,16,320]{2,1,0:T(8,128)(2,1)S(1)} collective-permute-done((bf16[8,16,320]{2,1,0:T(8,128)(2,1)S(1)}, bf16[8,16,320]{2,1,0:T(8,128)(2,1)S(1)}, u32[]{:S(2)}, u32[]{:S(2)}) %collective-permute-start.5) | collective-permute-done | bytes 81952 | tf_op jit(solution)/shard_map/ppermute | solution.py:320
  33.7 1.3 %collective-permute-done.6.refs_6_ = bf16[8,16,320]{2,1,0:T(8,128)(2,1)S(1)} collective-permute-done((bf16[8,16,320]{2,1,0:T(8,128)(2,1)S(1)}, bf16[8,16,320]{2,1,0:T(8,128)(2,1)S(1)}, u32[]{:S(2)}, u32[]{:S(2)}) %collective-permute-start.6) | collective-permute-done | bytes 81952 | tf_op jit(solution)/shard_map/ppermute | solution.py:320
  35.0 0.9 %collective-permute-done.7.refs_7_ = bf16[8,16,320]{2,1,0:T(8,128)(2,1)S(1)} collective-permute-done((bf16[8,16,320]{2,1,0:T(8,128)(2,1)S(1)}, bf16[8,16,320]{2,1,0:T(8,128)(2,1)S(1)}, u32[]{:S(2)}, u32[]{:S(2)}) %collective-permute-start.7) | collective-permute-done | bytes 81952 | tf_op jit(solution)/shard_map/ppermute | solution.py:320
  36.0 0.2 by_frame.1
  36.1 1.7 %collective-permute-start.8 = (bf16[4,8,16,320]{3,2,1,0:T(8,128)(2,1)S(1)}, bf16[4,8,16,320]{3,2,1,0:T(8,128)(2,1)S(1)}, u32[]{:S(2)}, u32[]{:S(2)}) collective-permute-start(bf16[4,8,16,320]{3,2,1,0:T(8,128)(2,1)S(1)} %get-tuple-element.33), channel_id=1, source_target_pairs={{0,8},{2,10},{4,12},{6,14},{8,0},{10,2},{12,4},{14,6},{16,24},{18,... | collective-permute-start | bytes 983048 | tf_op jit(solution)/shard_map/ppermute | solution.py:332
  37.8 4.6 %collective-permute-start.9 = (bf16[4,8,16,320]{3,2,1,0:T(8,128)(2,1)S(1)}, bf16[4,8,16,320]{3,2,1,0:T(8,128)(2,1)S(1)}, u32[]{:S(2)}, u32[]{:S(2)}) collective-permute-start(bf16[4,8,16,320]{3,2,1,0:T(8,128)(2,1)S(1)} %get-tuple-element.34), channel_id=1, source_target_pairs={{8,16},{10,18},{12,20},{14,22},{24,32},{26,34},{28,36},{30,38},{40... | collective-permute-start | bytes 983048 | tf_op jit(solution)/shard_map/ppermute | solution.py:331
  42.5 4.7 %collective-permute-done.8.near_ref = bf16[4,8,16,320]{3,2,1,0:T(8,128)(2,1)S(1)} collective-permute-done((bf16[4,8,16,320]{3,2,1,0:T(8,128)(2,1)S(1)}, bf16[4,8,16,320]{3,2,1,0:T(8,128)(2,1)S(1)}, u32[]{:S(2)}, u32[]{:S(2)}) %collective-permute-start.8) | collective-permute-done | bytes 327712 | tf_op jit(solution)/shard_map/ppermute | solution.py:332
  47.2 5.0 %collective-permute-done.9.far_ref = bf16[4,8,16,320]{3,2,1,0:T(8,128)(2,1)S(1)} collective-permute-done((bf16[4,8,16,320]{3,2,1,0:T(8,128)(2,1)S(1)}, bf16[4,8,16,320]{3,2,1,0:T(8,128)(2,1)S(1)}, u32[]{:S(2)}, u32[]{:S(2)}) %collective-permute-start.9) | collective-permute-done | bytes 327712 | tf_op jit(solution)/shard_map/ppermute | solution.py:331
  52.2 5.2 %window_attention.1 = (bf16[4,64,320]{2,1,0:T(8,128)(2,1)S(1)}, bf16[4,64,320]{2,1,0:T(8,128)(2,1)S(1)}, bf16[4,64,320]{2,1,0:T(8,128)(2,1)S(1)}, bf16[4,64,320]{2,1,0:T(8,128)(2,1)S(1)}) custom-call(bf16[8,8,16,320]{3,2,1,0:T(8,128)(2,1)S(1)} %get-tuple-element.32.own_ref, bf16[4,8,16,320]{3,2,1,0:T(8,128)(2,1)S(1)} %collective-permute-done.8.near_ref, ...), custom_call_target="tpu_custom_call" | custom-call | tf_op jit(solution)/shard_map/window_attention/pallas_call | solution.py:333
  57.4 1.2 %collective-permute-start.10 = (bf16[4,64,320]{2,1,0:T(8,128)(2,1)S(1)}, bf16[4,64,320]{2,1,0:T(8,128)(2,1)S(1)}, u32[]{:S(2)}, u32[]{:S(2)}) collective-permute-start(bf16[4,64,320]{2,1,0:T(8,128)(2,1)S(1)} %get-tuple-element.36), channel_id=1, source_target_pairs={{0,2},{2,0},{4,6},{6,4},{8,10},{10,8},{12,14},{14,12},{16,18},{18,... | collective-permute-start | bytes 491528 | tf_op jit(solution)/shard_map/ppermute | solution.py:350
  58.6 0.5 collective-permute-start.11
  59.1 1.2 %collective-permute-start.12 = (bf16[4,64,320]{2,1,0:T(8,128)(2,1)S(1)}, bf16[4,64,320]{2,1,0:T(8,128)(2,1)S(1)}, u32[]{:S(2)}, u32[]{:S(2)}) collective-permute-start(bf16[4,64,320]{2,1,0:T(8,128)(2,1)S(1)} %get-tuple-element.38), channel_id=1, source_target_pairs={{0,6},{2,4},{4,2},{6,0},{8,14},{10,12},{12,10},{14,8},{16,22},{18,... | collective-permute-start | bytes 491528 | tf_op jit(solution)/shard_map/ppermute | solution.py:350
  60.4 4.7 %collective-permute-done.11.refs_2_ = bf16[4,64,320]{2,1,0:T(8,128)(2,1)S(1)} collective-permute-done((bf16[4,64,320]{2,1,0:T(8,128)(2,1)S(1)}, bf16[4,64,320]{2,1,0:T(8,128)(2,1)S(1)}, u32[]{:S(2)}, u32[]{:S(2)}) %collective-permute-start.11) | collective-permute-done | bytes 163872 | tf_op jit(solution)/shard_map/ppermute | solution.py:350
  65.1 4.4 %collective-permute-done.12.refs_3_ = bf16[4,64,320]{2,1,0:T(8,128)(2,1)S(1)} collective-permute-done((bf16[4,64,320]{2,1,0:T(8,128)(2,1)S(1)}, bf16[4,64,320]{2,1,0:T(8,128)(2,1)S(1)}, u32[]{:S(2)}, u32[]{:S(2)}) %collective-permute-start.12) | collective-permute-done | bytes 163872 | tf_op jit(solution)/shard_map/ppermute | solution.py:350
  69.5 1.2 %home.1 = bf16[4,2,320,128]{3,2,1,0:T(8,128)(2,1)} custom-call(bf16[4,64,320]{2,1,0:T(8,128)(2,1)S(1)} %get-tuple-element.35.refs_0_, bf16[4,64,320]{2,1,0:T(8,128)(2,1)S(1)} %collective-permute-done.10.refs_1_, bf16[4,64,320]{2,1,0:T(8,128)(2,1)S(1)} %collective-permute-done.11.refs_2_, bf16[4,64,320]{2,1,0:T(8,128)(2,1)S(1)} %collective-permute-done.12.refs_3_), custom_call_target="tpu_custom_call" | custom-call | tf_op jit(solution)/shard_map/home/pallas_call | solution.py:351
  (25 shorter events, 0.3 us)
Async XLA Ops:
  0.0 8.8 %copy-start = (bf16[320,320]{1,0:T(8,128)(2,1)S(1)}, bf16[320,320]{1,0:T(8,128)(2,1)}, u32[]{:S(2)}) copy-start(bf16[320,320]{1,0:T(8,128)(2,1)} %param.13) | copy-start | bytes 614404
  1.0 10.2 %collective-permute-start = (bf16[2,2,320,128]{3,2,1,0:T(8,128)(2,1)S(1)}, bf16[2,2,320,128]{3,2,1,0:T(8,128)(2,1)S(1)}, u32[]{:S(2)}, u32[]{:S(2)}) collective-permute-start(bf16[2,2,320,128]{3,2,1,0:T(8,128)(2,1)S(1)} %dynamic-slice_bitcast_fusion), channel_id=1, source_target_pairs={{0,1},{1,0},{2,3},{3,2},{4,5},{5,4},{6,7},{7,6},{8,9},{9,8},{10,11... | collective-permute-start | bytes 983048 | tf_op jit(solution)/shard_map/ppermute | solution.py:286
  5.0 1.6 %copy-start.1 = (bf16[3,3,320,320]{3,2,1,0:T(8,128)(2,1)S(1)}, bf16[3,3,320,320]{3,2,1,0:T(8,128)(2,1)}, u32[]{:S(2)}) copy-start(bf16[3,3,320,320]{3,2,1,0:T(8,128)(2,1)} %first_ref.1) | copy-start | bytes 5529604
  6.6 1.6 %copy-start.2 = (bf16[3,3,320,320]{3,2,1,0:T(8,128)(2,1)S(1)}, bf16[3,3,320,320]{3,2,1,0:T(8,128)(2,1)}, u32[]{:S(2)}) copy-start(bf16[3,3,320,320]{3,2,1,0:T(8,128)(2,1)} %second_ref.1) | copy-start | bytes 5529604
  8.2 3.0 %copy-start.3 = (bf16[4,2,128,320]{2,3,1,0:T(8,128)(2,1)S(1)}, bf16[4,2,128,320]{2,3,1,0:T(8,128)(2,1)}, u32[]{:S(2)}) copy-start(bf16[4,2,128,320]{2,3,1,0:T(8,128)(2,1)} %param.10) | copy-start | bytes 1966084
  11.2 31.2 %copy-start.8 = (f32[320]{0:T(512)S(1)}, f32[320]{0:T(512)}, u32[]{:S(2)}) copy-start(f32[320]{0:T(512)} %param.15) | copy-start | bytes 3844
  11.2 41.0 %copy-start.4 = (bf16[320,320]{1,0:T(8,128)(2,1)S(1)}, bf16[320,320]{1,0:T(8,128)(2,1)}, u32[]{:S(2)}) copy-start(bf16[320,320]{1,0:T(8,128)(2,1)} %wq_ref.1) | copy-start | bytes 614404
  11.2 41.0 %copy-start.5 = (bf16[320,320]{1,0:T(8,128)(2,1)S(1)}, bf16[320,320]{1,0:T(8,128)(2,1)}, u32[]{:S(2)}) copy-start(bf16[320,320]{1,0:T(8,128)(2,1)} %wk_ref.1) | copy-start | bytes 614404
  11.2 41.0 %copy-start.6 = (bf16[320,320]{1,0:T(8,128)(2,1)S(1)}, bf16[320,320]{1,0:T(8,128)(2,1)}, u32[]{:S(2)}) copy-start(bf16[320,320]{1,0:T(8,128)(2,1)} %wv_ref.1) | copy-start | bytes 614404
  11.2 41.0 %copy-start.7 = (bf16[320,320]{1,0:T(8,128)(2,1)S(1)}, bf16[320,320]{1,0:T(8,128)(2,1)}, u32[]{:S(2)}) copy-start(bf16[320,320]{1,0:T(8,128)(2,1)} %wo_ref.1) | copy-start | bytes 614404
  21.0 8.0 %collective-permute-start.1 = (bf16[8,16,320]{2,1,0:T(8,128)(2,1)S(1)}, bf16[8,16,320]{2,1,0:T(8,128)(2,1)S(1)}, u32[]{:S(2)}, u32[]{:S(2)}) collective-permute-start(bf16[8,16,320]{2,1,0:T(8,128)(2,1)S(1)} %get-tuple-element.25), channel_id=1, source_target_pairs={{0,1},{1,0},{2,3},{3,2},{4,5},{5,4},{6,7},{7,6},{8,9},{9,8},{10,11... | collective-permute-start | bytes 245768 | tf_op jit(solution)/shard_map/ppermute | solution.py:320
  24.0 6.3 %collective-permute-start.2 = (bf16[8,16,320]{2,1,0:T(8,128)(2,1)S(1)}, bf16[8,16,320]{2,1,0:T(8,128)(2,1)S(1)}, u32[]{:S(2)}, u32[]{:S(2)}) collective-permute-start(bf16[8,16,320]{2,1,0:T(8,128)(2,1)S(1)} %get-tuple-element.26), channel_id=1, source_target_pairs={{0,2},{1,3},{2,0},{3,1},{4,6},{5,7},{6,4},{7,5},{8,10},{9,11},{10,... | collective-permute-start | bytes 245768 | tf_op jit(solution)/shard_map/ppermute | solution.py:320
  25.8 6.6 %collective-permute-start.3 = (bf16[8,16,320]{2,1,0:T(8,128)(2,1)S(1)}, bf16[8,16,320]{2,1,0:T(8,128)(2,1)S(1)}, u32[]{:S(2)}, u32[]{:S(2)}) collective-permute-start(bf16[8,16,320]{2,1,0:T(8,128)(2,1)S(1)} %get-tuple-element.27), channel_id=1, source_target_pairs={{0,3},{1,2},{2,1},{3,0},{4,7},{5,6},{6,5},{7,4},{8,11},{9,10},{10,... | collective-permute-start | bytes 245768 | tf_op jit(solution)/shard_map/ppermute | solution.py:320
  25.9 6.6 %collective-permute-start.4 = (bf16[8,16,320]{2,1,0:T(8,128)(2,1)S(1)}, bf16[8,16,320]{2,1,0:T(8,128)(2,1)S(1)}, u32[]{:S(2)}, u32[]{:S(2)}) collective-permute-start(bf16[8,16,320]{2,1,0:T(8,128)(2,1)S(1)} %get-tuple-element.28), channel_id=1, source_target_pairs={{0,4},{1,5},{2,6},{3,7},{4,0},{5,1},{6,2},{7,3},{8,12},{9,13},{10,... | collective-permute-start | bytes 245768 | tf_op jit(solution)/shard_map/ppermute | solution.py:320
  27.1 6.6 %collective-permute-start.5 = (bf16[8,16,320]{2,1,0:T(8,128)(2,1)S(1)}, bf16[8,16,320]{2,1,0:T(8,128)(2,1)S(1)}, u32[]{:S(2)}, u32[]{:S(2)}) collective-permute-start(bf16[8,16,320]{2,1,0:T(8,128)(2,1)S(1)} %get-tuple-element.29), channel_id=1, source_target_pairs={{0,5},{1,4},{2,7},{3,6},{4,1},{5,0},{6,3},{7,2},{8,13},{9,12},{10,... | collective-permute-start | bytes 245768 | tf_op jit(solution)/shard_map/ppermute | solution.py:320
  29.0 6.0 %collective-permute-start.6 = (bf16[8,16,320]{2,1,0:T(8,128)(2,1)S(1)}, bf16[8,16,320]{2,1,0:T(8,128)(2,1)S(1)}, u32[]{:S(2)}, u32[]{:S(2)}) collective-permute-start(bf16[8,16,320]{2,1,0:T(8,128)(2,1)S(1)} %get-tuple-element.30), channel_id=1, source_target_pairs={{0,6},{1,7},{2,4},{3,5},{4,2},{5,3},{6,0},{7,1},{8,14},{9,15},{10,... | collective-permute-start | bytes 245768 | tf_op jit(solution)/shard_map/ppermute | solution.py:320
  30.3 5.6 %collective-permute-start.7 = (bf16[8,16,320]{2,1,0:T(8,128)(2,1)S(1)}, bf16[8,16,320]{2,1,0:T(8,128)(2,1)S(1)}, u32[]{:S(2)}, u32[]{:S(2)}) collective-permute-start(bf16[8,16,320]{2,1,0:T(8,128)(2,1)S(1)} %get-tuple-element.31), channel_id=1, source_target_pairs={{0,7},{1,6},{2,5},{3,4},{4,3},{5,2},{6,1},{7,0},{8,15},{9,14},{10,... | collective-permute-start | bytes 245768 | tf_op jit(solution)/shard_map/ppermute | solution.py:320
  36.1 11.1 %collective-permute-start.8 = (bf16[4,8,16,320]{3,2,1,0:T(8,128)(2,1)S(1)}, bf16[4,8,16,320]{3,2,1,0:T(8,128)(2,1)S(1)}, u32[]{:S(2)}, u32[]{:S(2)}) collective-permute-start(bf16[4,8,16,320]{3,2,1,0:T(8,128)(2,1)S(1)} %get-tuple-element.33), channel_id=1, source_target_pairs={{0,8},{2,10},{4,12},{6,14},{8,0},{10,2},{12,4},{14,6},{16,24},{18,... | collective-permute-start | bytes 983048 | tf_op jit(solution)/shard_map/ppermute | solution.py:332
  37.8 14.4 %collective-permute-start.9 = (bf16[4,8,16,320]{3,2,1,0:T(8,128)(2,1)S(1)}, bf16[4,8,16,320]{3,2,1,0:T(8,128)(2,1)S(1)}, u32[]{:S(2)}, u32[]{:S(2)}) collective-permute-start(bf16[4,8,16,320]{3,2,1,0:T(8,128)(2,1)S(1)} %get-tuple-element.34), channel_id=1, source_target_pairs={{8,16},{10,18},{12,20},{14,22},{24,32},{26,34},{28,36},{30,38},{40... | collective-permute-start | bytes 983048 | tf_op jit(solution)/shard_map/ppermute | solution.py:331
  57.4 3.0 %collective-permute-start.10 = (bf16[4,64,320]{2,1,0:T(8,128)(2,1)S(1)}, bf16[4,64,320]{2,1,0:T(8,128)(2,1)S(1)}, u32[]{:S(2)}, u32[]{:S(2)}) collective-permute-start(bf16[4,64,320]{2,1,0:T(8,128)(2,1)S(1)} %get-tuple-element.36), channel_id=1, source_target_pairs={{0,2},{2,0},{4,6},{6,4},{8,10},{10,8},{12,14},{14,12},{16,18},{18,... | collective-permute-start | bytes 491528 | tf_op jit(solution)/shard_map/ppermute | solution.py:350
  58.6 6.5 %collective-permute-start.11 = (bf16[4,64,320]{2,1,0:T(8,128)(2,1)S(1)}, bf16[4,64,320]{2,1,0:T(8,128)(2,1)S(1)}, u32[]{:S(2)}, u32[]{:S(2)}) collective-permute-start(bf16[4,64,320]{2,1,0:T(8,128)(2,1)S(1)} %get-tuple-element.37), channel_id=1, source_target_pairs={{0,4},{2,6},{4,0},{6,2},{8,12},{10,14},{12,8},{14,10},{16,20},{18,... | collective-permute-start | bytes 491528 | tf_op jit(solution)/shard_map/ppermute | solution.py:350
  59.1 10.4 %collective-permute-start.12 = (bf16[4,64,320]{2,1,0:T(8,128)(2,1)S(1)}, bf16[4,64,320]{2,1,0:T(8,128)(2,1)S(1)}, u32[]{:S(2)}, u32[]{:S(2)}) collective-permute-start(bf16[4,64,320]{2,1,0:T(8,128)(2,1)S(1)} %get-tuple-element.38), channel_id=1, source_target_pairs={{0,6},{2,4},{4,2},{6,0},{8,14},{10,12},{12,10},{14,8},{16,22},{18,... | collective-permute-start | bytes 491528 | tf_op jit(solution)/shard_map/ppermute | solution.py:350

commit v2 on v1

v2 whole, which is shorter than its diff:
```python
import functools
import math

import jax
import jax.numpy as jnp
from jax import lax
from jax.experimental import pallas as pl
from jax.experimental.pallas import tpu as pltpu
from jax.sharding import PartitionSpec as P

HEADS = 5
GROUPS = 32
WINDOW = 16
C = 320
MAIN = 256
TAIL = C - MAIN
COLS = 128
CELLS = 512
AXES = ("tm", "height")
F32 = jnp.float32
BF16 = jnp.bfloat16


def dot32(a, b):
    return jnp.dot(a, b, preferred_element_type=F32)


def pack_kernel(first_ref, second_ref, first_out, second_out):
    for source, target in ((first_ref, first_out), (second_ref, second_out)):
        for dx in range(3):
            for lo, hi, row in ((0, MAIN, dx * MAIN), (MAIN, C, 3 * MAIN + dx * TAIL)):
                rows = slice(row, row + hi - lo)
                for dy in range(3):
                    target[rows, dy * MAIN : (dy + 1) * MAIN] = source[dy, dx, lo:hi, :MAIN]
                tails = [source[dy, dx, lo:hi, MAIN:] for dy in range(3)]
                target[rows, 3 * MAIN :] = jnp.concatenate(tails, axis=1)
        target[3 * C :, :] = jnp.zeros((TAIL, 3 * C), BF16)


def level_embedding(levels, emb_weight):
    half = emb_weight.shape[0] // 2
    freqs = jnp.exp(-math.log(10000.0) * jnp.arange(half).astype(jnp.float32) / half)
    angles = levels.astype(jnp.float32)[:, None] * freqs[None, :]
    sinus = jnp.concatenate([jnp.cos(angles), jnp.sin(angles)], axis=1)
    return jnp.dot(
        jax.nn.silu(sinus).astype(jnp.bfloat16), emb_weight, preferred_element_type=jnp.float32
    )


def split3(row):
    first = row.astype(BF16)
    rest = row - first.astype(F32)
    second = rest.astype(BF16)
    return [first, second, (rest - second.astype(F32)).astype(BF16)]


def group_scale(main, tail, group_map):
    parts = []
    for value in (main, tail):
        total = jnp.sum(value, axis=0, keepdims=True)
        square = jnp.sum(value * value, axis=0, keepdims=True)
        rows = split3(total) + split3(square)
        rows = [r.astype(F32) for r in rows] + [jnp.zeros_like(total)] * 2
        parts.append(jnp.concatenate(rows, axis=0).astype(BF16))
    sums = dot32(parts[0], group_map[:MAIN, :]) + dot32(parts[1], group_map[MAIN:, :])
    count = CELLS * (C // GROUPS)
    mean = (sums[0:1] + sums[1:2] + sums[2:3]) / count
    var = (sums[3:4] + sums[4:5] + sums[5:6]) / count - mean * mean
    scale = lax.rsqrt(var + 1e-05)
    return scale, -mean * scale


def silu(u):
    half = 0.5 * u
    return half + half * jnp.tanh(half)


def conv_input(act_ref, main, tail, group_map):
    scale, shift = group_scale(main, tail, group_map)
    column = lax.broadcasted_iota(jnp.int32, (CELLS, 1), 0) % COLS

    def three(value, lo, hi):
        act = silu(value * scale[:, lo:hi] + shift[:, lo:hi])
        before = jnp.where(column == 0, 0.0, pltpu.roll(act, 1, 0))
        after = jnp.where(column == COLS - 1, 0.0, pltpu.roll(act, CELLS - 1, 0))
        return before, act, after

    for index, value in enumerate(three(main, 0, MAIN)):
        act_ref[:, index * MAIN : (index + 1) * MAIN] = value.astype(BF16)
    before, act, after = three(tail, MAIN, C)
    base = 3 * MAIN
    act_ref[:, base : base + 2 * TAIL] = jnp.concatenate([before, act], axis=1).astype(BF16)
    zero = jnp.zeros_like(after)
    act_ref[:, base + 2 * TAIL :] = jnp.concatenate([after, zero], axis=1).astype(BF16)


def conv_rows(act_ref, weight_ref, taps_ref):
    taps_ref[...] = dot32(act_ref[...], weight_ref[...])

    def joined(base, width):
        rows = []
        for row in range(4):
            total = None
            for dy in range(3):
                source = row + dy - 1
                if 0 <= source < 4:
                    piece = taps_ref[
                        source * COLS : (source + 1) * COLS,
                        base + dy * width : base + (dy + 1) * width,
                    ]
                    total = piece if total is None else total + piece
            rows.append(total)
        return jnp.concatenate(rows, axis=0)

    return joined(0, MAIN), joined(3 * MAIN, TAIL)


def block_kernel(
    frame, own_ref, got_ref, first_ref, second_ref, emb_ref, group_ref, *rest
):
    x_ref, act_ref, taps_ref, res_ref = rest[-4:]
    here = lax.axis_index("height")
    ring = 2 * lax.rem(lax.axis_index("tm"), 4) + here
    group_map = group_ref[...]
    for row in range(2):
        for side, raw in ((here, own_ref[2 * here + frame, row]), (1 - here, got_ref[0, row])):
            start = pl.multiple_of((2 * side + row) * COLS, COLS)
            x_ref[pl.ds(start, COLS), :] = raw.astype(F32).T

    def hidden():
        return x_ref[:, :MAIN], x_ref[:, MAIN:]

    conv_input(act_ref, *hidden(), group_map)
    main, tail = conv_rows(act_ref, first_ref, taps_ref)
    emb = emb_ref[pl.ds(2 * here + frame, 1), :]
    conv_input(act_ref, main + emb[:, :MAIN], tail + emb[:, MAIN:], group_map)
    main, tail = conv_rows(act_ref, second_ref, taps_ref)
    old_main, old_tail = hidden()
    target = rest[0] if frame == 0 else res_ref
    target[:, :MAIN] = main + old_main
    target[:, MAIN:] = tail + old_tail
    if frame == 0:
        return
    before_ref, outs = rest[0], rest[1:9]
    for k in range(8):
        other = lax.bitwise_xor(ring, k)
        base = 256 * lax.rem(other, 2) + 64 * lax.div(other, 2)
        for b in range(8):
            rows = pl.ds(pl.multiple_of(base + 8 * b, 8), 8)
            pair = [before_ref[rows, :], res_ref[rows, :]]
            outs[k][b] = jnp.concatenate(pair, axis=0).astype(BF16)


def gather_kernel(*refs):
    pieces, (own_ref, near_refs, far_refs) = refs[:8], (refs[8], refs[9:11], refs[11:])
    tm = lax.axis_index("tm")
    ring = 2 * lax.rem(tm, 4) + lax.axis_index("height")
    odd = lax.rem(lax.div(tm, 4), 2)
    for k in range(8):
        own_ref[lax.bitwise_xor(ring, k)] = pieces[k][...]
    for part in range(2):
        for j in range(4):
            near_refs[part][j] = own_ref[4 * (1 - odd) + j, 4 * part : 4 * part + 4]
            far_refs[part][j] = own_ref[4 * odd + j, 4 * part : 4 * part + 4]


def project(value, gain, wk_ref, wv_ref, kv_ref, at):
    value = value.astype(F32)
    mean = jnp.mean(value, axis=-1, keepdims=True)
    centred = value - mean
    var = jnp.mean(centred * centred, axis=-1, keepdims=True)
    normed = (centred * lax.rsqrt(var + 1e-05) * gain).astype(BF16)
    rows = slice(at[1], at[1] + value.shape[0])
    pad = jnp.zeros((value.shape[0], TAIL), BF16)
    for low, ref in ((0, wk_ref), (384, wv_ref)):
        kv_ref[at[0], rows, low : low + C] = dot32(normed, ref[...]).astype(BF16)
        kv_ref[at[0], rows, low + C : low + 384] = pad
    return normed


def own_kernel(own_ref, gain_ref, wq_ref, wk_ref, wv_ref, q_ref, kv_ref):
    gain = gain_ref[...]
    for b in range(8):
        value = own_ref[:, b].reshape(128, C)
        normed = project(value, gain, wk_ref, wv_ref, kv_ref, (b, 0))
        q_ref[b, :, :C] = (dot32(normed, wq_ref[...]) * 0.125).astype(BF16)
        q_ref[b, :, C:] = jnp.zeros((128, TAIL), BF16)


def attention_kernel(
    part, own_ref, q_ref, mine_ref, far_ref, near_ref, gain_ref, wk_ref, wv_ref, wo_ref, *rest
):
    outs, (halo_ref, kv_ref, att_ref, mixed_ref) = rest[:4], rest[4:]
    tm = lax.axis_index("tm")
    quad = lax.rem(tm, 4)
    base = lax.div(tm, 4) * 16
    odd = lax.rem(lax.div(tm, 4), 2)
    halo_ref[1 - odd] = near_ref[...]
    halo_ref[odd] = far_ref[...]
    gain = gain_ref[...]
    for b in range(4):
        value = halo_ref[:, :, b].reshape(128, C)
        project(value, gain, wk_ref, wv_ref, kv_ref, (b, 0))
    row = lax.broadcasted_iota(jnp.int32, (128, 256), 0)
    col = lax.broadcasted_iota(jnp.int32, (128, 256), 1)
    key = jnp.where(col < 64, col // 8 - 8, jnp.where(col < 128, col // 8 + 8, col // 8 - 16))
    away = key - row // 8
    keep = (row % 8 == col % 8) & (away >= -(WINDOW // 2)) & (away < WINDOW // 2)
    keep = keep & (base + key >= 0) & (base + key < 4 * lax.axis_size("tm"))
    bias = jnp.where(keep, 0.0, -1e30).astype(F32)
    bias2 = jnp.concatenate([bias, bias], axis=0)
    ones = jnp.ones((256, 128), BF16)
    lane = lax.broadcasted_iota(jnp.int32, (128, 128), 1)
    for b in range(4):
        for pair in range(3):
            low = 128 * pair
            full = 4 * part + b
            q = q_ref[full, :, low : low + 128]
            k = [r[i, :, low : low + 128] for r, i in ((kv_ref, b), (mine_ref, full))]
            v = [r[i, :, 384 + low : 512 + low] for r, i in ((kv_ref, b), (mine_ref, full))]
            k, v = jnp.concatenate(k, axis=0), jnp.concatenate(v, axis=0)
            add = bias
            if pair < 2:
                zero = jnp.zeros_like(q)
                q = jnp.concatenate(
                    [jnp.where(lane < 64, q, zero), jnp.where(lane < 64, zero, q)], axis=0
                )
                add = bias2
            score = lax.dot_general(
                q, k, (((1,), (1,)), ((), ())), preferred_element_type=F32
            )
            probs = jnp.exp(score + add).astype(BF16)
            mixed = dot32(probs, jnp.concatenate([v, ones], axis=1))
            mixed = mixed[:, :128] / mixed[:, 128:]
            if pair < 2:
                mixed = jnp.where(lane < 64, mixed[:128], mixed[128:])
            att_ref[b, :, low : low + 128] = mixed.astype(BF16)
    for two in range(2):
        parts = []
        for b in (2 * two, 2 * two + 1):
            value = dot32(att_ref[b][:, :C], wo_ref[...])
            parts.append(value + own_ref[:, 4 * part + b].reshape(128, C).astype(F32))
        for f in range(16):
            rows = jnp.concatenate([p[8 * f : 8 * f + 8] for p in parts], axis=0)
            mixed_ref[f, 16 * two : 16 * two + 16, :] = rows.astype(BF16)
    for k in range(4):
        other = lax.bitwise_xor(quad, k)
        for f in range(4):
            outs[k][f] = mixed_ref[4 * other + f]


def home_kernel(*refs):
    pieces, out_ref, cells_ref = refs[:8], refs[8], refs[9]
    quad = lax.rem(lax.axis_index("tm"), 4)
    for k in range(4):
        for part in range(2):
            start = pl.multiple_of(64 * lax.bitwise_xor(quad, k) + 32 * part, 32)
            for f in range(4):
                cells_ref[f, pl.ds(start, 32), :] = pieces[4 * part + k][f]
    for f in range(4):
        for row in range(2):
            value = cells_ref[f, row * COLS : (row + 1) * COLS, :].astype(F32)
            out_ref[f, row] = value.T.astype(BF16)


def cost(flops):
    return pl.CostEstimate(flops=flops, bytes_accessed=0, transcendentals=0)


def vmem(count):
    return [pl.BlockSpec(memory_space=pltpu.VMEM)] * count


def body(
    latents, levels, conv_first, emb_weight, conv_second, ln_gain, w_query, w_key, w_value, w_out
):
    here = lax.axis_index("height")
    size = lax.axis_size("tm")
    latents = jnp.transpose(latents, (0, 1, 3, 2))
    got = []
    for frame in range(2):
        send = lax.dynamic_slice_in_dim(latents, 2 * (1 - here) + frame, 1, axis=0)
        got.append(lax.ppermute(send, "height", [(0, 1), (1, 0)]))
    params = pltpu.CompilerParams(vmem_limit_bytes=28 * 2**20)
    first, second = pl.pallas_call(
        pack_kernel,
        out_shape=[jax.ShapeDtypeStruct((1024, 3 * C), BF16)] * 2,
        in_specs=vmem(2),
        out_specs=vmem(2),
        compiler_params=params,
        cost_estimate=cost(1_000_000_000),
        name="pack_weights",
    )(conv_first, conv_second)
    emb = level_embedding(levels, emb_weight)
    ids = jnp.arange(C) // (C // GROUPS)
    group_map = (ids[:, None] == ids[None, :]).astype(BF16)

    before = []
    for frame in range(2):
        piece = [jax.ShapeDtypeStruct((8, 16, C), BF16)] * 8
        whole = [jax.ShapeDtypeStruct((CELLS, C), F32)]
        pieces = pl.pallas_call(
            functools.partial(block_kernel, frame),
            out_shape=piece if frame else whole,
            in_specs=vmem(6 + frame),
            out_specs=vmem(8 if frame else 1),
            scratch_shapes=[
                pltpu.VMEM((CELLS, C), F32),
                pltpu.VMEM((CELLS, 1024), BF16),
                pltpu.VMEM((CELLS, 960), F32),
                pltpu.VMEM((CELLS, C), F32),
            ],
            compiler_params=params,
            cost_estimate=cost(4_000_000_000),
            name="resblock",
        )(latents, got[frame], first, second, emb, group_map, *before)
        before = pieces

    swaps = [[(i, i ^ k) for i in range(2 * size)] for k in range(8)]
    pieces = [pieces[0]] + [lax.ppermute(pieces[k], AXES, swaps[k]) for k in range(1, 8)]
    half = [jax.ShapeDtypeStruct((4, 4, 16, C), BF16)]
    own, *halves = pl.pallas_call(
        gather_kernel,
        out_shape=[jax.ShapeDtypeStruct((8, 8, 16, C), BF16)] + half * 4,
        in_specs=vmem(8),
        out_specs=vmem(5),
        compiler_params=params,
        name="by_frame",
    )(*pieces)
    up = [(i, i + 4) for i in range(size - 4) if i // 4 % 2 == 1]
    both = up + [(j, i) for i, j in up]
    far = [lax.ppermute(x, "tm", both) for x in halves[2:]]
    near = [lax.ppermute(x, "tm", [(i, i ^ 4) for i in range(size)]) for x in halves[:2]]
    gain = ln_gain.reshape(1, C)
    query, mine = pl.pallas_call(
        own_kernel,
        out_shape=[
            jax.ShapeDtypeStruct((8, 128, 384), BF16),
            jax.ShapeDtypeStruct((8, 128, 768), BF16),
        ],
        in_specs=vmem(5),
        out_specs=vmem(2),
        compiler_params=params,
        cost_estimate=cost(2_000_000_000),
        name="own_frames",
    )(own, gain, w_query, w_key, w_value)
    swaps = [[(i, i ^ k) for i in range(size)] for k in range(4)]
    back = []
    for part in range(2):
        pieces = pl.pallas_call(
            functools.partial(attention_kernel, part),
            out_shape=[jax.ShapeDtypeStruct((4, 32, C), BF16)] * 4,
            in_specs=vmem(9),
            out_specs=vmem(4),
            scratch_shapes=[
                pltpu.VMEM((2, 4, 4, 16, C), BF16),
                pltpu.VMEM((4, 128, 768), BF16),
                pltpu.VMEM((4, 128, 384), BF16),
                pltpu.VMEM((16, 32, C), BF16),
            ],
            compiler_params=params,
            cost_estimate=cost(2_000_000_000),
            name="window_attention",
        )(own, query, mine, far[part], near[part], gain, w_key, w_value, w_out)
        back += [pieces[0]] + [lax.ppermute(pieces[k], "tm", swaps[k]) for k in range(1, 4)]
    home = pl.pallas_call(
        home_kernel,
        out_shape=jax.ShapeDtypeStruct((4, 2, C, COLS), BF16),
        in_specs=vmem(8),
        out_specs=pl.BlockSpec(memory_space=pltpu.VMEM),
        scratch_shapes=[pltpu.VMEM((4, 256, C), BF16)],
        compiler_params=params,
        name="home",
    )(*back)
    return jnp.transpose(home, (0, 1, 3, 2))


def solution(mesh):
    placed = (P("tm", "height", None, None), P("tm"), P(), P(), P(), P(), P(), P(), P(), P())
    return jax.shard_map(
        body, mesh=mesh, in_specs=placed, out_specs=P("tm", "height", None, None), check_vma=False
    )
```

time: 70.9 us -> 61.6 us (0.87)
  waiting for transfers between devices: 25.2 us -> 9.64 us
  starting transfers between devices: 23.1 us -> 29.5 us
    ppermute x3 -> x6, waiting for transfers between devices: 12 us -> 0.59 us  [the longest x2 0.58 us: body(): lax.ppermute(x, 'tm', [(i, i ^ 4) for i in range(size)])]
    ppermute x3 -> x6, waiting for transfers between devices: 9.13 us -> 4.91 us  [body(): lax.ppermute(pieces[k], 'tm', swaps[k])]
    ppermute x3 -> x6, starting transfers between devices: 2.96 us -> 6.36 us  [body(): lax.ppermute(pieces[k], 'tm', swaps[k])]
    ppermute x3 -> x6, starting transfers between devices: 9.29 us -> 12.6 us  [the longest x2 8.02 us: body(): far = [lax.ppermute(x, 'tm', both) for x in halves[2:]]]
    pallas_call x2 -> x5, Pallas kernels: 14.9 us -> 14.5 us  [the longest x2 8.44 us: body(): pl.pallas_call(functools.partial(block_kernel, frame), out_shape=piece if...]
  transfers between devices with their start and end apart: 13 -> 19, of which waited for: 10 -> 9; matrix products, arithmetic and copies ran while one was open for 2% -> 2% of each run, Pallas kernels for 1% -> 17%
where the time goes in v2:
time: 61.6 us; the launch traced here: 61.3 us
  starting transfers between devices  29.5 us (48%)
  Pallas kernels  16.3 us (26%)
  waiting for transfers between devices  9.64 us (16%)
  local copies, waits for them, and re-layouts  4.51 us (7%)
  other arithmetic  0.92 us (1%)
    ppermute x7, starting transfers between devices, body(): lax.ppermute(pieces[k], AXES, swaps[k])  10.5 us
    pallas_call x2, Pallas kernels, body(): pl.pallas_call(functools.partial(block_kernel, frame), out_shape=piece if...  8.44 us
    ppermute x2, starting transfers between devices, body(): far = [lax.ppermute(x, 'tm', both) for x in halves[2:]]  8.02 us
    ppermute x6, starting transfers between devices, body(): lax.ppermute(pieces[k], 'tm', swaps[k])  6.36 us
    ppermute x6, waiting for transfers between devices, body(): lax.ppermute(pieces[k], 'tm', swaps[k])  4.91 us
    ppermute x7, waiting for transfers between devices, body(): lax.ppermute(pieces[k], AXES, swaps[k])  4.13 us
    pallas_call x2, Pallas kernels, body(): pl.pallas_call(functools.partial(attention_kernel, part), out_shape=[jax....  4.06 us
    unnamed x18, local copies, waits for them, and re-layouts  3.44 us
  transfers between devices with their start and end apart: 19, of which 9 were waited for; matrix products, arithmetic and copies ran while one was open for 2% of the time, Pallas kernels for 17%

profile of v2, /device:TPU:7, one launch (start us, length us, event | category | flops | bytes accessed | tf_op | source)
XLA Modules:
  0.0 61.3 jit_solution(12466489282875791587)
XLA Ops:
  0.0 1.1 %dynamic-slice_bitcast_fusion = (bf16[1,2,320,128]{3,2,1,0:T(8,128)(2,1)S(1)}, bf16[1,2,320,128]{3,2,1,0:T(8,128)(2,1)S(1)}) fusion(bf16[4,2,128,320]{2,3,1,0:T(8,128)(2,1)} %param.10, s32[]{:T(128)S(6)} %select_n.23, s32[]{:T(128)S(6)} %select_n.21), kind=kLoop, calls=%fused_computation.1 | loop fusion | bytes 655368 | tf_op jit(solution)/shard_map/dynamic_slice | solution.py:282
  1.1 3.0 %collective-permute-start.1 = (bf16[1,2,320,128]{3,2,1,0:T(8,128)(2,1)S(1)}, bf16[1,2,320,128]{3,2,1,0:T(8,128)(2,1)S(1)}, u32[]{:S(2)}, u32[]{:S(2)}) collective-permute-start(bf16[1,2,320,128]{3,2,1,0:T(8,128)(2,1)S(1)} %get-tuple-element.55), channel_id=1, source_target_pairs={{0,1},{1,0},{2,3},{3,2},{4,5},{5,4},{6,7},{7,6},{8,9},{9,8},{10,11... | collective-permute-start | bytes 491528 | tf_op jit(solution)/shard_map/ppermute | solution.py:283
  4.2 0.7 %convert_element_type.18 = f32[4]{0:T(128)S(1)} convert(s32[4]{0:T(128)} %param.11) | non-fusion elementwise | flops 4 | bytes 32 | tf_op jit(solution)/shard_map/convert_element_type | solution.py:43
  5.0 1.6 %copy-done.1 = bf16[3,3,320,320]{3,2,1,0:T(8,128)(2,1)S(1)} copy-done((bf16[3,3,320,320]{3,2,1,0:T(8,128)(2,1)S(1)}, bf16[3,3,320,320]{3,2,1,0:T(8,128)(2,1)}, u32[]{:S(2)}) %copy-start.1) | copy-done | bytes 1843224
  6.6 1.6 %copy-done.2 = bf16[3,3,320,320]{3,2,1,0:T(8,128)(2,1)S(1)} copy-done((bf16[3,3,320,320]{3,2,1,0:T(8,128)(2,1)S(1)}, bf16[3,3,320,320]{3,2,1,0:T(8,128)(2,1)}, u32[]{:S(2)}) %copy-start.2) | copy-done | bytes 1843224
  9.3 4.2 %resblock.2.rest_0_ = f32[512,320]{1,0:T(8,128)S(1)} custom-call(bf16[4,2,320,128]{3,2,1,0:T(8,128)(2,1)S(1)} %bitcast.7, bf16[1,2,320,128]{3,2,1,0:T(8,128)(2,1)S(1)} %collective-permute-done.1.got_ref, bf16[1024,960]{1,0:T(8,128)(2,1)S(1)} %get-tuple-element.30.first_ref, bf16[1024,960]{1,0:T(8,128)(2,1)S(1)} %get-tuple-element.31.second_ref, ...), custom_call_target="tpu_custom_call" | custom-call | flops 4000000000 | tf_op jit(solution)/shard_map/resblock/pallas_call | solution.py:302
  13.5 4.3 %resblock.3 = (bf16[8,16,320]{2,1,0:T(8,128)(2,1)S(1)}, bf16[8,16,320]{2,1,0:T(8,128)(2,1)S(1)}, bf16[8,16,320]{2,1,0:T(8,128)(2,1)S(1)}, bf16[8,16,320]{2,1,0:T...) custom-call(bf16[4,2,320,128]{3,2,1,0:T(8,128)(2,1)S(1)} %bitcast.8,, ...), custom_call_target="tpu_custom_call" | custom-call | flops 4000000000 | tf_op jit(solution)/shard_map/resblock/pallas_call | solution.py:302
  17.8 3.0 %collective-permute-start.2 = (bf16[8,16,320]{2,1,0:T(8,128)(2,1)S(1)}, bf16[8,16,320]{2,1,0:T(8,128)(2,1)S(1)}, u32[]{:S(2)}, u32[]{:S(2)}) collective-permute-start(bf16[8,16,320]{2,1,0:T(8,128)(2,1)S(1)} %get-tuple-element.33), channel_id=1, source_target_pairs={{0,1},{1,0},{2,3},{3,2},{4,5},{5,4},{6,7},{7,6},{8,9},{9,8},{10,11... | collective-permute-start | bytes 245768 | tf_op jit(solution)/shard_map/ppermute | solution.py:320
  20.7 1.5 %collective-permute-start.3 = (bf16[8,16,320]{2,1,0:T(8,128)(2,1)S(1)}, bf16[8,16,320]{2,1,0:T(8,128)(2,1)S(1)}, u32[]{:S(2)}, u32[]{:S(2)}) collective-permute-start(bf16[8,16,320]{2,1,0:T(8,128)(2,1)S(1)} %get-tuple-element.34), channel_id=1, source_target_pairs={{0,2},{1,3},{2,0},{3,1},{4,6},{5,7},{6,4},{7,5},{8,10},{9,11},{10,... | collective-permute-start | bytes 245768 | tf_op jit(solution)/shard_map/ppermute | solution.py:320
  22.3 1.2 %collective-permute-start.5 = (bf16[8,16,320]{2,1,0:T(8,128)(2,1)S(1)}, bf16[8,16,320]{2,1,0:T(8,128)(2,1)S(1)}, u32[]{:S(2)}, u32[]{:S(2)}) collective-permute-start(bf16[8,16,320]{2,1,0:T(8,128)(2,1)S(1)} %get-tuple-element.36), channel_id=1, source_target_pairs={{0,4},{1,5},{2,6},{3,7},{4,0},{5,1},{6,2},{7,3},{8,12},{9,13},{10,... | collective-permute-start | bytes 245768 | tf_op jit(solution)/shard_map/ppermute | solution.py:320
  23.5 1.9 %collective-permute-start.6 = (bf16[8,16,320]{2,1,0:T(8,128)(2,1)S(1)}, bf16[8,16,320]{2,1,0:T(8,128)(2,1)S(1)}, u32[]{:S(2)}, u32[]{:S(2)}) collective-permute-start(bf16[8,16,320]{2,1,0:T(8,128)(2,1)S(1)} %get-tuple-element.37), channel_id=1, source_target_pairs={{0,5},{1,4},{2,7},{3,6},{4,1},{5,0},{6,3},{7,2},{8,13},{9,12},{10,... | collective-permute-start | bytes 245768 | tf_op jit(solution)/shard_map/ppermute | solution.py:320
  25.4 1.4 %collective-permute-start.7 = (bf16[8,16,320]{2,1,0:T(8,128)(2,1)S(1)}, bf16[8,16,320]{2,1,0:T(8,128)(2,1)S(1)}, u32[]{:S(2)}, u32[]{:S(2)}) collective-permute-start(bf16[8,16,320]{2,1,0:T(8,128)(2,1)S(1)} %get-tuple-element.38), channel_id=1, source_target_pairs={{0,6},{1,7},{2,4},{3,5},{4,2},{5,3},{6,0},{7,1},{8,14},{9,15},{10,... | collective-permute-start | bytes 245768 | tf_op jit(solution)/shard_map/ppermute | solution.py:320
  26.8 1.5 %collective-permute-start.8 = (bf16[8,16,320]{2,1,0:T(8,128)(2,1)S(1)}, bf16[8,16,320]{2,1,0:T(8,128)(2,1)S(1)}, u32[]{:S(2)}, u32[]{:S(2)}) collective-permute-start(bf16[8,16,320]{2,1,0:T(8,128)(2,1)S(1)} %get-tuple-element.39), channel_id=1, source_target_pairs={{0,7},{1,6},{2,5},{3,4},{4,3},{5,2},{6,1},{7,0},{8,15},{9,14},{10,... | collective-permute-start | bytes 245768 | tf_op jit(solution)/shard_map/ppermute | solution.py:320
  28.3 0.6 collective-permute-done.4.refs_3_
  28.9 1.2 %collective-permute-done.6.refs_5_ = bf16[8,16,320]{2,1,0:T(8,128)(2,1)S(1)} collective-permute-done((bf16[8,16,320]{2,1,0:T(8,128)(2,1)S(1)}, bf16[8,16,320]{2,1,0:T(8,128)(2,1)S(1)}, u32[]{:S(2)}, u32[]{:S(2)}) %collective-permute-start.6) | collective-permute-done | bytes 81952 | tf_op jit(solution)/shard_map/ppermute | solution.py:320
  30.1 1.3 %collective-permute-done.7.refs_6_ = bf16[8,16,320]{2,1,0:T(8,128)(2,1)S(1)} collective-permute-done((bf16[8,16,320]{2,1,0:T(8,128)(2,1)S(1)}, bf16[8,16,320]{2,1,0:T(8,128)(2,1)S(1)}, u32[]{:S(2)}, u32[]{:S(2)}) %collective-permute-start.7) | collective-permute-done | bytes 81952 | tf_op jit(solution)/shard_map/ppermute | solution.py:320
  31.5 0.9 %collective-permute-done.8.refs_7_ = bf16[8,16,320]{2,1,0:T(8,128)(2,1)S(1)} collective-permute-done((bf16[8,16,320]{2,1,0:T(8,128)(2,1)S(1)}, bf16[8,16,320]{2,1,0:T(8,128)(2,1)S(1)}, u32[]{:S(2)}, u32[]{:S(2)}) %collective-permute-start.8) | collective-permute-done | bytes 81952 | tf_op jit(solution)/shard_map/ppermute | solution.py:320
  32.6 5.9 %collective-permute-start.14 = (bf16[4,4,16,320]{3,2,1,0:T(8,128)(2,1)S(1)}, bf16[4,4,16,320]{3,2,1,0:T(8,128)(2,1)S(1)}, u32[]{:S(2)}, u32[]{:S(2)}) collective-permute-start(bf16[4,4,16,320]{3,2,1,0:T(8,128)(2,1)S(1)} %get-tuple-element.49), channel_id=1, source_target_pairs={{8,16},{10,18},{12,20},{14,22},{24,32},{26,34},{28,36},{30,38},{40... | collective-permute-start | bytes 491528 | tf_op jit(solution)/shard_map/ppermute | solution.py:332
  38.6 1.5 %collective-permute-start.10 = (bf16[4,4,16,320]{3,2,1,0:T(8,128)(2,1)S(1)}, bf16[4,4,16,320]{3,2,1,0:T(8,128)(2,1)S(1)}, u32[]{:S(2)}, u32[]{:S(2)}) collective-permute-start(bf16[4,4,16,320]{3,2,1,0:T(8,128)(2,1)S(1)} %get-tuple-element.44), channel_id=1, source_target_pairs={{0,8},{2,10},{4,12},{6,14},{8,0},{10,2},{12,4},{14,6},{16,24},{18,... | collective-permute-start | bytes 491528 | tf_op jit(solution)/shard_map/ppermute | solution.py:333
  40.0 2.1 %collective-permute-start.9 = (bf16[4,4,16,320]{3,2,1,0:T(8,128)(2,1)S(1)}, bf16[4,4,16,320]{3,2,1,0:T(8,128)(2,1)S(1)}, u32[]{:S(2)}, u32[]{:S(2)}) collective-permute-start(bf16[4,4,16,320]{3,2,1,0:T(8,128)(2,1)S(1)} %get-tuple-element.43), channel_id=1, source_target_pairs={{8,16},{10,18},{12,20},{14,22},{24,32},{26,34},{28,36},{30,38},{40... | collective-permute-start | bytes 491528 | tf_op jit(solution)/shard_map/ppermute | solution.py:332
  42.2 2.0 %own_frames.1 = (bf16[8,128,384]{2,1,0:T(8,128)(2,1)S(1)}, bf16[8,128,768]{2,1,0:T(8,128)(2,1)S(1)}) custom-call(bf16[8,8,16,320]{3,2,1,0:T(8,128)(2,1)S(1)} %get-tuple-element.40.own_ref, f32[1,320]{1,0:T(1,128)S(1)} %reshape.36.gain_ref, bf16[320,320]{1,0:T(8,128)(2,1)S(1)} %copy-done.4, bf16[320,320]{1,0:T(8,128)(2,1)S(1)} %copy-done.5, ...), custom_call_target="tpu_custom_call" | custom-call | flops 2000000000 | tf_op jit(solution)/shard_map/own_frames/pallas_call | solution.py:335
  44.2 0.6 collective-permute-done.15.near_ref
  44.7 2.0 %window_attention.3 = (bf16[4,32,320]{2,1,0:T(8,128)(2,1)S(1)}, bf16[4,32,320]{2,1,0:T(8,128)(2,1)S(1)}, bf16[4,32,320]{2,1,0:T(8,128)(2,1)S(1)}, bf16[4,32,320]{2,1,0:T(8,128)(2,1)S(1)}) custom-call(bf16[8,8,16,320]{3,2,1,0:T(8,128)(2,1)S(1)} %get-tuple-element.40.own_ref, bf16[8,128,384]{2,1,0:T(8,128)(2,1)S(1)} %get-tuple-element.41.q_ref, ...), custom_call_target="tpu_custom_call" | custom-call | flops 2000000000 | tf_op jit(solution)/shard_map/window_attention/pallas_call | solution.py:350
  46.8 2.0 %collective-permute-start.16 = (bf16[4,32,320]{2,1,0:T(8,128)(2,1)S(1)}, bf16[4,32,320]{2,1,0:T(8,128)(2,1)S(1)}, u32[]{:S(2)}, u32[]{:S(2)}) collective-permute-start(bf16[4,32,320]{2,1,0:T(8,128)(2,1)S(1)} %get-tuple-element.52), channel_id=1, source_target_pairs={{0,2},{2,0},{4,6},{6,4},{8,10},{10,8},{12,14},{14,12},{16,18},{18,... | collective-permute-start | bytes 245768 | tf_op jit(solution)/shard_map/ppermute | solution.py:365
  48.8 0.9 %collective-permute-start.17 = (bf16[4,32,320]{2,1,0:T(8,128)(2,1)S(1)}, bf16[4,32,320]{2,1,0:T(8,128)(2,1)S(1)}, u32[]{:S(2)}, u32[]{:S(2)}) collective-permute-start(bf16[4,32,320]{2,1,0:T(8,128)(2,1)S(1)} %get-tuple-element.53), channel_id=1, source_target_pairs={{0,4},{2,6},{4,0},{6,2},{8,12},{10,14},{12,8},{14,10},{16,20},{18,... | collective-permute-start | bytes 245768 | tf_op jit(solution)/shard_map/ppermute | solution.py:365
  49.7 0.8 %collective-permute-start.18 = (bf16[4,32,320]{2,1,0:T(8,128)(2,1)S(1)}, bf16[4,32,320]{2,1,0:T(8,128)(2,1)S(1)}, u32[]{:S(2)}, u32[]{:S(2)}) collective-permute-start(bf16[4,32,320]{2,1,0:T(8,128)(2,1)S(1)} %get-tuple-element.54), channel_id=1, source_target_pairs={{0,6},{2,4},{4,2},{6,0},{8,14},{10,12},{12,10},{14,8},{16,22},{18,... | collective-permute-start | bytes 245768 | tf_op jit(solution)/shard_map/ppermute | solution.py:365
  50.5 2.0 %window_attention.2 = (bf16[4,32,320]{2,1,0:T(8,128)(2,1)S(1)}, bf16[4,32,320]{2,1,0:T(8,128)(2,1)S(1)}, bf16[4,32,320]{2,1,0:T(8,128)(2,1)S(1)}, bf16[4,32,320]{2,1,0:T(8,128)(2,1)S(1)}) custom-call(bf16[8,8,16,320]{3,2,1,0:T(8,128)(2,1)S(1)} %get-tuple-element.40.own_ref, bf16[8,128,384]{2,1,0:T(8,128)(2,1)S(1)} %get-tuple-element.41.q_ref, ...), custom_call_target="tpu_custom_call" | custom-call | flops 2000000000 | tf_op jit(solution)/shard_map/window_attention/pallas_call | solution.py:350
  52.5 0.9 %collective-permute-start.11 = (bf16[4,32,320]{2,1,0:T(8,128)(2,1)S(1)}, bf16[4,32,320]{2,1,0:T(8,128)(2,1)S(1)}, u32[]{:S(2)}, u32[]{:S(2)}) collective-permute-start(bf16[4,32,320]{2,1,0:T(8,128)(2,1)S(1)} %get-tuple-element.46), channel_id=1, source_target_pairs={{0,2},{2,0},{4,6},{6,4},{8,10},{10,8},{12,14},{14,12},{16,18},{18,... | collective-permute-start | bytes 245768 | tf_op jit(solution)/shard_map/ppermute | solution.py:365
  54.0 1.2 %collective-permute-start.13 = (bf16[4,32,320]{2,1,0:T(8,128)(2,1)S(1)}, bf16[4,32,320]{2,1,0:T(8,128)(2,1)S(1)}, u32[]{:S(2)}, u32[]{:S(2)}) collective-permute-start(bf16[4,32,320]{2,1,0:T(8,128)(2,1)S(1)} %get-tuple-element.48), channel_id=1, source_target_pairs={{0,6},{2,4},{4,2},{6,0},{8,14},{10,12},{12,10},{14,8},{16,22},{18,... | collective-permute-start | bytes 245768 | tf_op jit(solution)/shard_map/ppermute | solution.py:365
  55.4 2.4 %collective-permute-done.12.refs_2_ = bf16[4,32,320]{2,1,0:T(8,128)(2,1)S(1)} collective-permute-done((bf16[4,32,320]{2,1,0:T(8,128)(2,1)S(1)}, bf16[4,32,320]{2,1,0:T(8,128)(2,1)S(1)}, u32[]{:S(2)}, u32[]{:S(2)}) %collective-permute-start.12) | collective-permute-done | bytes 81952 | tf_op jit(solution)/shard_map/ppermute | solution.py:365
  57.8 2.3 %collective-permute-done.13.refs_3_ = bf16[4,32,320]{2,1,0:T(8,128)(2,1)S(1)} collective-permute-done((bf16[4,32,320]{2,1,0:T(8,128)(2,1)S(1)}, bf16[4,32,320]{2,1,0:T(8,128)(2,1)S(1)}, u32[]{:S(2)}, u32[]{:S(2)}) %collective-permute-start.13) | collective-permute-done | bytes 81952 | tf_op jit(solution)/shard_map/ppermute | solution.py:365
  60.1 1.2 %home.1 = bf16[4,2,320,128]{3,2,1,0:T(8,128)(2,1)} custom-call(bf16[4,32,320]{2,1,0:T(8,128)(2,1)S(1)} %get-tuple-element.45.refs_0_, bf16[4,32,320]{2,1,0:T(8,128)(2,1)S(1)} %collective-permute-done.11.refs_1_, bf16[4,32,320]{2,1,0:T(8,128)(2,1)S(1)} %collective-permute-done.12.refs_2_, bf16[4,32,320]{2,1,0:T(8,128)(2,1)S(1)} %collective-permute-done.13.refs_3_, ...), custom_call_target="tpu_custom_call" | custom-call | tf_op jit(solution)/shard_map/home/pallas_call | solution.py:366
  (40 shorter events, 2.4 us)
Async XLA Ops:
  0.0 8.8 %copy-start = (bf16[320,320]{1,0:T(8,128)(2,1)S(1)}, bf16[320,320]{1,0:T(8,128)(2,1)}, u32[]{:S(2)}) copy-start(bf16[320,320]{1,0:T(8,128)(2,1)} %param.13) | copy-start | bytes 614404
  1.1 8.1 %collective-permute-start.1 = (bf16[1,2,320,128]{3,2,1,0:T(8,128)(2,1)S(1)}, bf16[1,2,320,128]{3,2,1,0:T(8,128)(2,1)S(1)}, u32[]{:S(2)}, u32[]{:S(2)}) collective-permute-start(bf16[1,2,320,128]{3,2,1,0:T(8,128)(2,1)S(1)} %get-tuple-element.55), channel_id=1, source_target_pairs={{0,1},{1,0},{2,3},{3,2},{4,5},{5,4},{6,7},{7,6},{8,9},{9,8},{10,11... | collective-permute-start | bytes 491528 | tf_op jit(solution)/shard_map/ppermute | solution.py:283
  4.1 9.4 %collective-permute-start = (bf16[1,2,320,128]{3,2,1,0:T(8,128)(2,1)S(1)}, bf16[1,2,320,128]{3,2,1,0:T(8,128)(2,1)S(1)}, u32[]{:S(2)}, u32[]{:S(2)}) collective-permute-start(bf16[1,2,320,128]{3,2,1,0:T(8,128)(2,1)S(1)} %get-tuple-element.56), channel_id=1, source_target_pairs={{0,1},{1,0},{2,3},{3,2},{4,5},{5,4},{6,7},{7,6},{8,9},{9,8},{10,11... | collective-permute-start | bytes 491528 | tf_op jit(solution)/shard_map/ppermute | solution.py:283
  5.0 1.6 %copy-start.1 = (bf16[3,3,320,320]{3,2,1,0:T(8,128)(2,1)S(1)}, bf16[3,3,320,320]{3,2,1,0:T(8,128)(2,1)}, u32[]{:S(2)}) copy-start(bf16[3,3,320,320]{3,2,1,0:T(8,128)(2,1)} %first_ref.1) | copy-start | bytes 5529604
  6.6 1.6 %copy-start.2 = (bf16[3,3,320,320]{3,2,1,0:T(8,128)(2,1)S(1)}, bf16[3,3,320,320]{3,2,1,0:T(8,128)(2,1)}, u32[]{:S(2)}) copy-start(bf16[3,3,320,320]{3,2,1,0:T(8,128)(2,1)} %second_ref.1) | copy-start | bytes 5529604
  8.2 1.1 %copy-start.3 = (bf16[4,2,128,320]{2,3,1,0:T(8,128)(2,1)S(1)}, bf16[4,2,128,320]{2,3,1,0:T(8,128)(2,1)}, u32[]{:S(2)}) copy-start(bf16[4,2,128,320]{2,3,1,0:T(8,128)(2,1)} %param.10) | copy-start | bytes 1966084
  13.5 14.8 %copy-start.8 = (f32[320]{0:T(512)S(1)}, f32[320]{0:T(512)}, u32[]{:S(2)}) copy-start(f32[320]{0:T(512)} %param.15) | copy-start | bytes 3844
  13.5 28.7 %copy-start.4 = (bf16[320,320]{1,0:T(8,128)(2,1)S(1)}, bf16[320,320]{1,0:T(8,128)(2,1)}, u32[]{:S(2)}) copy-start(bf16[320,320]{1,0:T(8,128)(2,1)} %wq_ref.1) | copy-start | bytes 614404
  13.5 28.7 %copy-start.5 = (bf16[320,320]{1,0:T(8,128)(2,1)S(1)}, bf16[320,320]{1,0:T(8,128)(2,1)}, u32[]{:S(2)}) copy-start(bf16[320,320]{1,0:T(8,128)(2,1)} %wk_ref.5) | copy-start | bytes 614404
  13.5 28.7 %copy-start.6 = (bf16[320,320]{1,0:T(8,128)(2,1)S(1)}, bf16[320,320]{1,0:T(8,128)(2,1)}, u32[]{:S(2)}) copy-start(bf16[320,320]{1,0:T(8,128)(2,1)} %wv_ref.5) | copy-start | bytes 614404
  17.8 7.6 %collective-permute-start.2 = (bf16[8,16,320]{2,1,0:T(8,128)(2,1)S(1)}, bf16[8,16,320]{2,1,0:T(8,128)(2,1)S(1)}, u32[]{:S(2)}, u32[]{:S(2)}) collective-permute-start(bf16[8,16,320]{2,1,0:T(8,128)(2,1)S(1)} %get-tuple-element.33), channel_id=1, source_target_pairs={{0,1},{1,0},{2,3},{3,2},{4,5},{5,4},{6,7},{7,6},{8,9},{9,8},{10,11... | collective-permute-start | bytes 245768 | tf_op jit(solution)/shard_map/ppermute | solution.py:320
  20.7 6.0 %collective-permute-start.3 = (bf16[8,16,320]{2,1,0:T(8,128)(2,1)S(1)}, bf16[8,16,320]{2,1,0:T(8,128)(2,1)S(1)}, u32[]{:S(2)}, u32[]{:S(2)}) collective-permute-start(bf16[8,16,320]{2,1,0:T(8,128)(2,1)S(1)} %get-tuple-element.34), channel_id=1, source_target_pairs={{0,2},{1,3},{2,0},{3,1},{4,6},{5,7},{6,4},{7,5},{8,10},{9,11},{10,... | collective-permute-start | bytes 245768 | tf_op jit(solution)/shard_map/ppermute | solution.py:320
  22.3 6.6 %collective-permute-start.4 = (bf16[8,16,320]{2,1,0:T(8,128)(2,1)S(1)}, bf16[8,16,320]{2,1,0:T(8,128)(2,1)S(1)}, u32[]{:S(2)}, u32[]{:S(2)}) collective-permute-start(bf16[8,16,320]{2,1,0:T(8,128)(2,1)S(1)} %get-tuple-element.35), channel_id=1, source_target_pairs={{0,3},{1,2},{2,1},{3,0},{4,7},{5,6},{6,5},{7,4},{8,11},{9,10},{10,... | collective-permute-start | bytes 245768 | tf_op jit(solution)/shard_map/ppermute | solution.py:320
  22.3 6.6 %collective-permute-start.5 = (bf16[8,16,320]{2,1,0:T(8,128)(2,1)S(1)}, bf16[8,16,320]{2,1,0:T(8,128)(2,1)S(1)}, u32[]{:S(2)}, u32[]{:S(2)}) collective-permute-start(bf16[8,16,320]{2,1,0:T(8,128)(2,1)S(1)} %get-tuple-element.36), channel_id=1, source_target_pairs={{0,4},{1,5},{2,6},{3,7},{4,0},{5,1},{6,2},{7,3},{8,12},{9,13},{10,... | collective-permute-start | bytes 245768 | tf_op jit(solution)/shard_map/ppermute | solution.py:320
  23.5 6.6 %collective-permute-start.6 = (bf16[8,16,320]{2,1,0:T(8,128)(2,1)S(1)}, bf16[8,16,320]{2,1,0:T(8,128)(2,1)S(1)}, u32[]{:S(2)}, u32[]{:S(2)}) collective-permute-start(bf16[8,16,320]{2,1,0:T(8,128)(2,1)S(1)} %get-tuple-element.37), channel_id=1, source_target_pairs={{0,5},{1,4},{2,7},{3,6},{4,1},{5,0},{6,3},{7,2},{8,13},{9,12},{10,... | collective-permute-start | bytes 245768 | tf_op jit(solution)/shard_map/ppermute | solution.py:320
  25.4 6.0 %collective-permute-start.7 = (bf16[8,16,320]{2,1,0:T(8,128)(2,1)S(1)}, bf16[8,16,320]{2,1,0:T(8,128)(2,1)S(1)}, u32[]{:S(2)}, u32[]{:S(2)}) collective-permute-start(bf16[8,16,320]{2,1,0:T(8,128)(2,1)S(1)} %get-tuple-element.38), channel_id=1, source_target_pairs={{0,6},{1,7},{2,4},{3,5},{4,2},{5,3},{6,0},{7,1},{8,14},{9,15},{10,... | collective-permute-start | bytes 245768 | tf_op jit(solution)/shard_map/ppermute | solution.py:320
  26.8 5.6 %collective-permute-start.8 = (bf16[8,16,320]{2,1,0:T(8,128)(2,1)S(1)}, bf16[8,16,320]{2,1,0:T(8,128)(2,1)S(1)}, u32[]{:S(2)}, u32[]{:S(2)}) collective-permute-start(bf16[8,16,320]{2,1,0:T(8,128)(2,1)S(1)} %get-tuple-element.39), channel_id=1, source_target_pairs={{0,7},{1,6},{2,5},{3,4},{4,3},{5,2},{6,1},{7,0},{8,15},{9,14},{10,... | collective-permute-start | bytes 245768 | tf_op jit(solution)/shard_map/ppermute | solution.py:320
  32.6 11.6 %collective-permute-start.14 = (bf16[4,4,16,320]{3,2,1,0:T(8,128)(2,1)S(1)}, bf16[4,4,16,320]{3,2,1,0:T(8,128)(2,1)S(1)}, u32[]{:S(2)}, u32[]{:S(2)}) collective-permute-start(bf16[4,4,16,320]{3,2,1,0:T(8,128)(2,1)S(1)} %get-tuple-element.49), channel_id=1, source_target_pairs={{8,16},{10,18},{12,20},{14,22},{24,32},{26,34},{28,36},{30,38},{40... | collective-permute-start | bytes 491528 | tf_op jit(solution)/shard_map/ppermute | solution.py:332
  38.5 6.2 %collective-permute-start.15 = (bf16[4,4,16,320]{3,2,1,0:T(8,128)(2,1)S(1)}, bf16[4,4,16,320]{3,2,1,0:T(8,128)(2,1)S(1)}, u32[]{:S(2)}, u32[]{:S(2)}) collective-permute-start(bf16[4,4,16,320]{3,2,1,0:T(8,128)(2,1)S(1)} %get-tuple-element.50), channel_id=1, source_target_pairs={{0,8},{2,10},{4,12},{6,14},{8,0},{10,2},{12,4},{14,6},{16,24},{18,... | collective-permute-start | bytes 491528 | tf_op jit(solution)/shard_map/ppermute | solution.py:333
  38.6 11.9 %collective-permute-start.10 = (bf16[4,4,16,320]{3,2,1,0:T(8,128)(2,1)S(1)}, bf16[4,4,16,320]{3,2,1,0:T(8,128)(2,1)S(1)}, u32[]{:S(2)}, u32[]{:S(2)}) collective-permute-start(bf16[4,4,16,320]{3,2,1,0:T(8,128)(2,1)S(1)} %get-tuple-element.44), channel_id=1, source_target_pairs={{0,8},{2,10},{4,12},{6,14},{8,0},{10,2},{12,4},{14,6},{16,24},{18,... | collective-permute-start | bytes 491528 | tf_op jit(solution)/shard_map/ppermute | solution.py:333
  40.0 10.5 %collective-permute-start.9 = (bf16[4,4,16,320]{3,2,1,0:T(8,128)(2,1)S(1)}, bf16[4,4,16,320]{3,2,1,0:T(8,128)(2,1)S(1)}, u32[]{:S(2)}, u32[]{:S(2)}) collective-permute-start(bf16[4,4,16,320]{3,2,1,0:T(8,128)(2,1)S(1)} %get-tuple-element.43), channel_id=1, source_target_pairs={{8,16},{10,18},{12,20},{14,22},{24,32},{26,34},{28,36},{30,38},{40... | collective-permute-start | bytes 491528 | tf_op jit(solution)/shard_map/ppermute | solution.py:332
  42.2 2.6 %copy-start.7 = (bf16[320,320]{1,0:T(8,128)(2,1)S(1)}, bf16[320,320]{1,0:T(8,128)(2,1)}, u32[]{:S(2)}) copy-start(bf16[320,320]{1,0:T(8,128)(2,1)} %wo_ref.3) | copy-start | bytes 614404
  46.8 7.2 %collective-permute-start.16 = (bf16[4,32,320]{2,1,0:T(8,128)(2,1)S(1)}, bf16[4,32,320]{2,1,0:T(8,128)(2,1)S(1)}, u32[]{:S(2)}, u32[]{:S(2)}) collective-permute-start(bf16[4,32,320]{2,1,0:T(8,128)(2,1)S(1)} %get-tuple-element.52), channel_id=1, source_target_pairs={{0,2},{2,0},{4,6},{6,4},{8,10},{10,8},{12,14},{14,12},{16,18},{18,... | collective-permute-start | bytes 245768 | tf_op jit(solution)/shard_map/ppermute | solution.py:365
  48.8 6.4 %collective-permute-start.17 = (bf16[4,32,320]{2,1,0:T(8,128)(2,1)S(1)}, bf16[4,32,320]{2,1,0:T(8,128)(2,1)S(1)}, u32[]{:S(2)}, u32[]{:S(2)}) collective-permute-start(bf16[4,32,320]{2,1,0:T(8,128)(2,1)S(1)} %get-tuple-element.53), channel_id=1, source_target_pairs={{0,4},{2,6},{4,0},{6,2},{8,12},{10,14},{12,8},{14,10},{16,20},{18,... | collective-permute-start | bytes 245768 | tf_op jit(solution)/shard_map/ppermute | solution.py:365
  49.7 5.8 %collective-permute-start.18 = (bf16[4,32,320]{2,1,0:T(8,128)(2,1)S(1)}, bf16[4,32,320]{2,1,0:T(8,128)(2,1)S(1)}, u32[]{:S(2)}, u32[]{:S(2)}) collective-permute-start(bf16[4,32,320]{2,1,0:T(8,128)(2,1)S(1)} %get-tuple-element.54), channel_id=1, source_target_pairs={{0,6},{2,4},{4,2},{6,0},{8,14},{10,12},{12,10},{14,8},{16,22},{18,... | collective-permute-start | bytes 245768 | tf_op jit(solution)/shard_map/ppermute | solution.py:365
  52.5 2.9 %collective-permute-start.11 = (bf16[4,32,320]{2,1,0:T(8,128)(2,1)S(1)}, bf16[4,32,320]{2,1,0:T(8,128)(2,1)S(1)}, u32[]{:S(2)}, u32[]{:S(2)}) collective-permute-start(bf16[4,32,320]{2,1,0:T(8,128)(2,1)S(1)} %get-tuple-element.46), channel_id=1, source_target_pairs={{0,2},{2,0},{4,6},{6,4},{8,10},{10,8},{12,14},{14,12},{16,18},{18,... | collective-permute-start | bytes 245768 | tf_op jit(solution)/shard_map/ppermute | solution.py:365
  53.5 4.4 %collective-permute-start.12 = (bf16[4,32,320]{2,1,0:T(8,128)(2,1)S(1)}, bf16[4,32,320]{2,1,0:T(8,128)(2,1)S(1)}, u32[]{:S(2)}, u32[]{:S(2)}) collective-permute-start(bf16[4,32,320]{2,1,0:T(8,128)(2,1)S(1)} %get-tuple-element.47), channel_id=1, source_target_pairs={{0,4},{2,6},{4,0},{6,2},{8,12},{10,14},{12,8},{14,10},{16,20},{18,... | collective-permute-start | bytes 245768 | tf_op jit(solution)/shard_map/ppermute | solution.py:365
  54.0 6.1 %collective-permute-start.13 = (bf16[4,32,320]{2,1,0:T(8,128)(2,1)S(1)}, bf16[4,32,320]{2,1,0:T(8,128)(2,1)S(1)}, u32[]{:S(2)}, u32[]{:S(2)}) collective-permute-start(bf16[4,32,320]{2,1,0:T(8,128)(2,1)S(1)} %get-tuple-element.48), channel_id=1, source_target_pairs={{0,6},{2,4},{4,2},{6,0},{8,14},{10,12},{12,10},{14,8},{16,22},{18,... | collective-permute-start | bytes 245768 | tf_op jit(solution)/shard_map/ppermute | solution.py:365

commit v3 on v2

--- a/solution.py
+++ b/solution.py
@@ -25,8 +25,33 @@
     return jnp.dot(a, b, preferred_element_type=F32)
 
 
-def pack_kernel(first_ref, second_ref, first_out, second_out):
-    for source, target in ((first_ref, first_out), (second_ref, second_out)):
+def pick(latents_ref, out_ref, sem, frame):
+    there = 1 - lax.axis_index("height")
+    return pltpu.make_async_copy(latents_ref.at[pl.ds(2 * there + frame, 1)], out_ref, sem)
+
+
+def pick_kernel(latents_ref, out_ref, sem):
+    copy = pick(latents_ref, out_ref, sem, 0)
+    copy.start()
+    copy.wait()
+
+
+def pack_kernel(
+    first_ref, second_ref, latents_ref, first_out, second_out, send_out, raw_ref, sems, sem
+):
+    send = pick(latents_ref, send_out, sem, 1)
+    send.start()
+    copies = []
+    for index, ref in enumerate((first_ref, second_ref)):
+        for dy in range(3):
+            copies.append(
+                pltpu.make_async_copy(ref.at[dy], raw_ref.at[index, dy], sems.at[index, dy])
+            )
+            copies[-1].start()
+    for index, target in enumerate((first_out, second_out)):
+        for copy in copies[3 * index : 3 * index + 3]:
+            copy.wait()
+        source = raw_ref.at[index]
         for dx in range(3):
             for lo, hi, row in ((0, MAIN, dx * MAIN), (MAIN, C, 3 * MAIN + dx * TAIL)):
                 rows = slice(row, row + hi - lo)
@@ -35,6 +60,11 @@
                 tails = [source[dy, dx, lo:hi, MAIN:] for dy in range(3)]
                 target[rows, 3 * MAIN :] = jnp.concatenate(tails, axis=1)
         target[3 * C :, :] = jnp.zeros((TAIL, 3 * C), BF16)
+    send.wait()
+
+
+def in_hbm(array):
+    return pltpu.with_memory_space_constraint(array, pltpu.HBM)
 
 
 def level_embedding(levels, emb_weight):
@@ -55,14 +85,11 @@
 
 
 def group_scale(main, tail, group_map):
-    parts = []
-    for value in (main, tail):
-        total = jnp.sum(value, axis=0, keepdims=True)
-        square = jnp.sum(value * value, axis=0, keepdims=True)
-        rows = split3(total) + split3(square)
-        rows = [r.astype(F32) for r in rows] + [jnp.zeros_like(total)] * 2
-        parts.append(jnp.concatenate(rows, axis=0).astype(BF16))
-    sums = dot32(parts[0], group_map[:MAIN, :]) + dot32(parts[1], group_map[MAIN:, :])
+    total = [jnp.sum(v, axis=0, keepdims=True) for v in (main, tail)]
+    square = [jnp.sum(v * v, axis=0, keepdims=True) for v in (main, tail)]
+    rows = split3(jnp.concatenate(total, axis=1)) + split3(jnp.concatenate(square, axis=1))
+    rows = [r.astype(F32) for r in rows] + [jnp.zeros((2, C), F32)]
+    sums = dot32(jnp.concatenate(rows, axis=0).astype(BF16), group_map)
     count = CELLS * (C // GROUPS)
     mean = (sums[0:1] + sums[1:2] + sums[2:3]) / count
     var = (sums[3:4] + sums[4:5] + sums[5:6]) / count - mean * mean
@@ -151,11 +178,14 @@
             outs[k][b] = jnp.concatenate(pair, axis=0).astype(BF16)
 
 
+def odd_ring():
+    return lax.rem(lax.div(lax.axis_index("tm"), 4), 2)
+
+
 def gather_kernel(*refs):
     pieces, (own_ref, near_refs, far_refs) = refs[:8], (refs[8], refs[9:11], refs[11:])
-    tm = lax.axis_index("tm")
-    ring = 2 * lax.rem(tm, 4) + lax.axis_index("height")
-    odd = lax.rem(lax.div(tm, 4), 2)
+    ring = 2 * lax.rem(lax.axis_index("tm"), 4) + lax.axis_index("height")
+    odd = odd_ring()
     for k in range(8):
         own_ref[lax.bitwise_xor(ring, k)] = pieces[k][...]
     for part in range(2):
@@ -164,46 +194,55 @@
             far_refs[part][j] = own_ref[4 * odd + j, 4 * part : 4 * part + 4]
 
 
-def project(value, gain, wk_ref, wv_ref, kv_ref, at):
+def layer_norm(value, gain):
     value = value.astype(F32)
     mean = jnp.mean(value, axis=-1, keepdims=True)
     centred = value - mean
     var = jnp.mean(centred * centred, axis=-1, keepdims=True)
-    normed = (centred * lax.rsqrt(var + 1e-05) * gain).astype(BF16)
-    rows = slice(at[1], at[1] + value.shape[0])
-    pad = jnp.zeros((value.shape[0], TAIL), BF16)
-    for low, ref in ((0, wk_ref), (384, wv_ref)):
-        kv_ref[at[0], rows, low : low + C] = dot32(normed, ref[...]).astype(BF16)
-        kv_ref[at[0], rows, low + C : low + 384] = pad
-    return normed
-
-
-def own_kernel(own_ref, gain_ref, wq_ref, wk_ref, wv_ref, q_ref, kv_ref):
+    return (centred * lax.rsqrt(var + 1e-05) * gain).astype(BF16)
+
+
+def keys_values(blocks, gain_ref, wk_ref, wv_ref, norm_ref, kv_ref):
     gain = gain_ref[...]
-    for b in range(8):
-        value = own_ref[:, b].reshape(128, C)
-        normed = project(value, gain, wk_ref, wv_ref, kv_ref, (b, 0))
-        q_ref[b, :, :C] = (dot32(normed, wq_ref[...]) * 0.125).astype(BF16)
-        q_ref[b, :, C:] = jnp.zeros((128, TAIL), BF16)
+    rows = blocks[0].shape[0]
+    for b, value in enumerate(blocks):
+        norm_ref[b * rows : (b + 1) * rows, :] = layer_norm(value, gain)
+    each = len(blocks) if rows * len(blocks) <= 512 else 512 // rows
+    for b in range(0, len(blocks), each):
+        normed = norm_ref[b * rows : (b + each) * rows, :]
+        for low, ref in ((0, wk_ref), (384, wv_ref)):
+            value = dot32(normed, ref[...]).astype(BF16).reshape(each, rows, C)
+            kv_ref[b : b + each, :, low : low + C] = value
+            pad = jnp.zeros((each, rows, TAIL), BF16)
+            kv_ref[b : b + each, :, low + C : low + 384] = pad
+
+
+def own_kernel(own_ref, gain_ref, wq_ref, wk_ref, wv_ref, q_ref, kv_ref, norm_ref):
+    blocks = [own_ref[:, b].reshape(128, C) for b in range(8)]
+    keys_values(blocks, gain_ref, wk_ref, wv_ref, norm_ref, kv_ref)
+    for b in range(0, 8, 4):
+        value = dot32(norm_ref[128 * b : 128 * b + 512, :], wq_ref[...]) * 0.125
+        q_ref[b : b + 4, :, :C] = value.astype(BF16).reshape(4, 128, C)
+        q_ref[b : b + 4, :, C:] = jnp.zeros((4, 128, TAIL), BF16)
 
 
 def attention_kernel(
     part, own_ref, q_ref, mine_ref, far_ref, near_ref, gain_ref, wk_ref, wv_ref, wo_ref, *rest
 ):
-    outs, (halo_ref, kv_ref, att_ref, mixed_ref) = rest[:4], rest[4:]
+    outs, (norm_ref, kv_ref, att_ref, mixed_ref) = rest[:4], rest[4:]
     tm = lax.axis_index("tm")
     quad = lax.rem(tm, 4)
     base = lax.div(tm, 4) * 16
-    odd = lax.rem(lax.div(tm, 4), 2)
-    halo_ref[1 - odd] = near_ref[...]
-    halo_ref[odd] = far_ref[...]
-    gain = gain_ref[...]
-    for b in range(4):
-        value = halo_ref[:, :, b].reshape(128, C)
-        project(value, gain, wk_ref, wv_ref, kv_ref, (b, 0))
+    odd = odd_ring()
+    blocks = [
+        jnp.concatenate([r[:, b].reshape(64, C) for r in (near_ref, far_ref)], axis=0)
+        for b in range(4)
+    ]
+    keys_values(blocks, gain_ref, wk_ref, wv_ref, norm_ref, kv_ref)
     row = lax.broadcasted_iota(jnp.int32, (128, 256), 0)
     col = lax.broadcasted_iota(jnp.int32, (128, 256), 1)
-    key = jnp.where(col < 64, col // 8 - 8, jnp.where(col < 128, col // 8 + 8, col // 8 - 16))
+    near_at, far_at = 16 - 24 * odd, 24 * odd - 16
+    key = col // 8 + jnp.where(col < 64, near_at, jnp.where(col < 128, far_at, -16))
     away = key - row // 8
     keep = (row % 8 == col % 8) & (away >= -(WINDOW // 2)) & (away < WINDOW // 2)
     keep = keep & (base + key >= 0) & (base + key < 4 * lax.axis_size("tm"))
@@ -211,28 +250,32 @@
     bias2 = jnp.concatenate([bias, bias], axis=0)
     ones = jnp.ones((256, 128), BF16)
     lane = lax.broadcasted_iota(jnp.int32, (128, 128), 1)
-    for b in range(4):
-        for pair in range(3):
-            low = 128 * pair
-            full = 4 * part + b
-            q = q_ref[full, :, low : low + 128]
-            k = [r[i, :, low : low + 128] for r, i in ((kv_ref, b), (mine_ref, full))]
-            v = [r[i, :, 384 + low : 512 + low] for r, i in ((kv_ref, b), (mine_ref, full))]
-            k, v = jnp.concatenate(k, axis=0), jnp.concatenate(v, axis=0)
+
+    def keys(b, low):
+        full = 4 * part + b
+        sides = [kv_ref[b], mine_ref[full]]
+        return jnp.concatenate([x[:, low : low + 128] for x in sides], axis=0)
+
+    for first in range(0, 4, 2):
+        items = [(b, 128 * pair) for b in (first, first + 1) for pair in range(3)]
+        probs = []
+        for b, low in items:
+            q = q_ref[4 * part + b, :, low : low + 128]
             add = bias
-            if pair < 2:
+            if low < 256:
                 zero = jnp.zeros_like(q)
                 q = jnp.concatenate(
                     [jnp.where(lane < 64, q, zero), jnp.where(lane < 64, zero, q)], axis=0
                 )
                 add = bias2
             score = lax.dot_general(
-                q, k, (((1,), (1,)), ((), ())), preferred_element_type=F32
+                q, keys(b, low), (((1,), (1,)), ((), ())), preferred_element_type=F32
             )
-            probs = jnp.exp(score + add).astype(BF16)
-            mixed = dot32(probs, jnp.concatenate([v, ones], axis=1))
+            probs.append(jnp.exp(score + add).astype(BF16))
+        for (b, low), prob in zip(items, probs):
+            mixed = dot32(prob, jnp.concatenate([keys(b, 384 + low), ones], axis=1))
             mixed = mixed[:, :128] / mixed[:, 128:]
-            if pair < 2:
+            if low < 256:
                 mixed = jnp.where(lane < 64, mixed[:128], mixed[128:])
             att_ref[b, :, low : low + 128] = mixed.astype(BF16)
     for two in range(2):
@@ -274,23 +317,36 @@
 def body(
     latents, levels, conv_first, emb_weight, conv_second, ln_gain, w_query, w_key, w_value, w_out
 ):
-    here = lax.axis_index("height")
     size = lax.axis_size("tm")
     latents = jnp.transpose(latents, (0, 1, 3, 2))
-    got = []
-    for frame in range(2):
-        send = lax.dynamic_slice_in_dim(latents, 2 * (1 - here) + frame, 1, axis=0)
-        got.append(lax.ppermute(send, "height", [(0, 1), (1, 0)]))
     params = pltpu.CompilerParams(vmem_limit_bytes=28 * 2**20)
-    first, second = pl.pallas_call(
+    halves = jax.ShapeDtypeStruct((1, 2, C, COLS), BF16)
+    hbm = pl.BlockSpec(memory_space=pltpu.HBM)
+    send = pl.pallas_call(
+        pick_kernel,
+        out_shape=halves,
+        in_specs=[hbm],
+        out_specs=pl.BlockSpec(memory_space=pltpu.VMEM),
+        scratch_shapes=[pltpu.SemaphoreType.DMA(())],
+        compiler_params=params,
+        name="pick",
+    )(in_hbm(latents))
+    got = [lax.ppermute(send, "height", [(0, 1), (1, 0)])]
+    first, second, send = pl.pallas_call(
         pack_kernel,
-        out_shape=[jax.ShapeDtypeStruct((1024, 3 * C), BF16)] * 2,
-        in_specs=vmem(2),
-        out_specs=vmem(2),
+        out_shape=[jax.ShapeDtypeStruct((1024, 3 * C), BF16)] * 2 + [halves],
+        in_specs=[hbm] * 3,
+        out_specs=vmem(3),
+        scratch_shapes=[
+            pltpu.VMEM((2, 3, 3, C, C), BF16),
+            pltpu.SemaphoreType.DMA((2, 3)),
+            pltpu.SemaphoreType.DMA(()),
+        ],
         compiler_params=params,
         cost_estimate=cost(1_000_000_000),
         name="pack_weights",
-    )(conv_first, conv_second)
+    )(in_hbm(conv_first), in_hbm(conv_second), in_hbm(latents))
+    got.append(lax.ppermute(send, "height", [(0, 1), (1, 0)]))
     emb = level_embedding(levels, emb_weight)
     ids = jnp.arange(C) // (C // GROUPS)
     group_map = (ids[:, None] == ids[None, :]).astype(BF16)
@@ -318,10 +374,12 @@
 
     swaps = [[(i, i ^ k) for i in range(2 * size)] for k in range(8)]
     pieces = [pieces[0]] + [lax.ppermute(pieces[k], AXES, swaps[k]) for k in range(1, 8)]
-    half = [jax.ShapeDtypeStruct((4, 4, 16, C), BF16)]
+    def array(*shape):
+        return jax.ShapeDtypeStruct(shape, BF16)
+
     own, *halves = pl.pallas_call(
         gather_kernel,
-        out_shape=[jax.ShapeDtypeStruct((8, 8, 16, C), BF16)] + half * 4,
+        out_shape=[array(8, 8, 16, C)] + [array(4, 4, 16, C)] * 4,
         in_specs=vmem(8),
         out_specs=vmem(5),
         compiler_params=params,
@@ -334,12 +392,10 @@
     gain = ln_gain.reshape(1, C)
     query, mine = pl.pallas_call(
         own_kernel,
-        out_shape=[
-            jax.ShapeDtypeStruct((8, 128, 384), BF16),
-            jax.ShapeDtypeStruct((8, 128, 768), BF16),
-        ],
+        out_shape=[array(8, 128, 384), array(8, 128, 768)],
         in_specs=vmem(5),
         out_specs=vmem(2),
+        scratch_shapes=[pltpu.VMEM((1024, C), BF16)],
         compiler_params=params,
         cost_estimate=cost(2_000_000_000),
         name="own_frames",
@@ -349,11 +405,11 @@
     for part in range(2):
         pieces = pl.pallas_call(
             functools.partial(attention_kernel, part),
-            out_shape=[jax.ShapeDtypeStruct((4, 32, C), BF16)] * 4,
+            out_shape=[array(4, 32, C)] * 4,
             in_specs=vmem(9),
             out_specs=vmem(4),
             scratch_shapes=[
-                pltpu.VMEM((2, 4, 4, 16, C), BF16),
+                pltpu.VMEM((512, C), BF16),
                 pltpu.VMEM((4, 128, 768), BF16),
                 pltpu.VMEM((4, 128, 384), BF16),
                 pltpu.VMEM((16, 32, C), BF16),

time: 61.6 us -> 60.6 us (0.984)
  local copies, waits for them, and re-layouts: 4.51 us -> 0.05 us
  Pallas kernels: 16.3 us -> 19 us
  waiting for transfers between devices: 9.64 us -> 11.9 us
  starting transfers between devices: 29.5 us -> 28.8 us
  other arithmetic: 0.92 us -> 0.26 us
    unnamed x18 -> x16, local copies, waits for them, and re-layouts: 3.44 us -> 0.05 us
    ppermute x0 -> x1, starting transfers between devices: none -> 2.99 us  [body(): got = [lax.ppermute(send, 'height', [(0, 1), (1, 0)])]]
    ppermute x2 -> x1, starting transfers between devices: 3.09 us -> 0.19 us  [body(): got.append(lax.ppermute(send, 'height', [(0, 1), (1, 0)]))]
    pallas_call x1, Pallas kernels: 0.54 us -> 2.6 us  [body(): pl.pallas_call(pack_kernel, out_shape=[jax.ShapeDtypeStruct((1024, 3 * C)...]
    ppermute x7, starting transfers between devices: 10.5 us -> 9.25 us  [body(): lax.ppermute(pieces[k], AXES, swaps[k])]
    ppermute x7, waiting for transfers between devices: 4.13 us -> 5.29 us  [body(): lax.ppermute(pieces[k], AXES, swaps[k])]
    ppermute x2 -> x1, waiting for transfers between devices: 0.01 us -> 1.16 us  [body(): got.append(lax.ppermute(send, 'height', [(0, 1), (1, 0)]))]
    dynamic_slice x1 -> x0, local copies, waits for them, and re-layouts: 1.06 us -> none  [body(): send = lax.dynamic_slice_in_dim(latents, 2 * (1 - here) + frame, 1, axis=0)]
  transfers between devices with their start and end apart: 19 -> 19, of which waited for: 9 -> 10; matrix products, arithmetic and copies ran while one was open for 2% -> 1% of each run, Pallas kernels for 17% -> 21%
where the time goes in v3:
time: 60.6 us; the launch traced here: 60.5 us
  starting transfers between devices  28.8 us (48%)
  Pallas kernels  19 us (31%)
  waiting for transfers between devices  11.9 us (20%)
    ppermute x7, starting transfers between devices, body(): lax.ppermute(pieces[k], AXES, swaps[k])  9.25 us
    pallas_call x2, Pallas kernels, body(): pl.pallas_call(functools.partial(block_kernel, frame), out_shape=piece if...  8.26 us
    ppermute x2, starting transfers between devices, body(): far = [lax.ppermute(x, 'tm', both) for x in halves[2:]]  8.01 us
    ppermute x6, starting transfers between devices, body(): lax.ppermute(pieces[k], 'tm', swaps[k])  6.84 us
    ppermute x7, waiting for transfers between devices, body(): lax.ppermute(pieces[k], AXES, swaps[k])  5.29 us
    ppermute x6, waiting for transfers between devices, body(): lax.ppermute(pieces[k], 'tm', swaps[k])  4.91 us
    pallas_call x2, Pallas kernels, body(): pl.pallas_call(functools.partial(attention_kernel, part), out_shape=[arra...  3.9 us
    ppermute x1, starting transfers between devices, body(): got = [lax.ppermute(send, 'height', [(0, 1), (1, 0)])]  2.99 us
  transfers between devices with their start and end apart: 19, of which 10 were waited for; matrix products, arithmetic and copies ran while one was open for 1% of the time, Pallas kernels for 21%

profile of v3, /device:TPU:7, one launch (start us, length us, event | category | flops | bytes accessed | tf_op | source)
XLA Modules:
  0.0 60.5 jit_solution(6665009948974902544)
XLA Ops:
  0.0 1.0 %pick.1 = bf16[1,2,320,128]{3,2,1,0:T(8,128)(2,1)S(1)} custom-call(bf16[4,2,320,128]{3,2,1,0:T(8,128)(2,1)} %bitcast.3), custom_call_target="tpu_custom_call" | custom-call | tf_op jit(solution)/shard_map/pick/pallas_call | solution.py:325
  1.0 3.0 %collective-permute-start.1 = (bf16[1,2,320,128]{3,2,1,0:T(8,128)(2,1)S(1)}, bf16[1,2,320,128]{3,2,1,0:T(8,128)(2,1)S(1)}, u32[]{:S(2)}, u32[]{:S(2)}) collective-permute-start(bf16[1,2,320,128]{3,2,1,0:T(8,128)(2,1)S(1)} %pick.1), channel_id=1, source_target_pairs={{0,1},{1,0},{2,3},{3,2},{4,5},{5,4},{6,7},{7,6},{8,9},{9,8},{10,11... | collective-permute-start | bytes 491528 | tf_op jit(solution)/shard_map/ppermute | solution.py:334
  4.0 2.6 %pack_weights.1 = (bf16[1024,960]{1,0:T(8,128)(2,1)S(1)}, bf16[1024,960]{1,0:T(8,128)(2,1)S(1)}, bf16[1,2,320,128]{3,2,1,0:T(8,128)(2,1)S(1)}) custom-call(bf16[3,3,320,320]{3,2,1,0:T(8,128)(2,1)} %first_ref.1, bf16[3,3,320,320]{3,2,1,0:T(8,128)(2,1)} %second_ref.1, bf16[4,2,320,128]{3,2,1,0:T(8,128)(2,1)} %bitcast.4), custom_call_target="tpu_custom_call" | custom-call | flops 1000000000 | tf_op jit(solution)/shard_map/pack_weights/pallas_call | solution.py:335
  7.3 0.3 collective-permute-done.1.got_ref
  7.7 4.1 %resblock.2.rest_0_ = f32[512,320]{1,0:T(8,128)S(1)} custom-call(bf16[4,2,320,128]{3,2,1,0:T(8,128)(2,1)S(1)} %bitcast.5, bf16[1,2,320,128]{3,2,1,0:T(8,128)(2,1)S(1)} %collective-permute-done.1.got_ref, bf16[1024,960]{1,0:T(8,128)(2,1)S(1)} %get-tuple-element.32.first_ref, bf16[1024,960]{1,0:T(8,128)(2,1)S(1)} %get-tuple-element.33.second_ref, ...), custom_call_target="tpu_custom_call" | custom-call | flops 4000000000 | tf_op jit(solution)/shard_map/resblock/pallas_call | solution.py:358
  11.8 1.2 %collective-permute-done.got_ref = bf16[1,2,320,128]{3,2,1,0:T(8,128)(2,1)S(1)} collective-permute-done((bf16[1,2,320,128]{3,2,1,0:T(8,128)(2,1)S(1)}, bf16[1,2,320,128]{3,2,1,0:T(8,128)(2,1)S(1)}, u32[]{:S(2)}, u32[]{:S(2)}) %collective-permute-start) | collective-permute-done | bytes 163872 | tf_op jit(solution)/shard_map/ppermute | solution.py:349
  12.9 4.2 %resblock.3 = (bf16[8,16,320]{2,1,0:T(8,128)(2,1)S(1)}, bf16[8,16,320]{2,1,0:T(8,128)(2,1)S(1)}, bf16[8,16,320]{2,1,0:T(8,128)(2,1)S(1)}, bf16[8,16,320]{2,1,0:T...) custom-call(bf16[4,2,320,128]{3,2,1,0:T(8,128)(2,1)S(1)} %bitcast.6,, ...), custom_call_target="tpu_custom_call" | custom-call | flops 4000000000 | tf_op jit(solution)/shard_map/resblock/pallas_call | solution.py:358
  17.1 1.9 %collective-permute-start.2 = (bf16[8,16,320]{2,1,0:T(8,128)(2,1)S(1)}, bf16[8,16,320]{2,1,0:T(8,128)(2,1)S(1)}, u32[]{:S(2)}, u32[]{:S(2)}) collective-permute-start(bf16[8,16,320]{2,1,0:T(8,128)(2,1)S(1)} %get-tuple-element.35), channel_id=1, source_target_pairs={{0,1},{1,0},{2,3},{3,2},{4,5},{5,4},{6,7},{7,6},{8,9},{9,8},{10,11... | collective-permute-start | bytes 245768 | tf_op jit(solution)/shard_map/ppermute | solution.py:376
  19.0 2.5 %collective-permute-start.3 = (bf16[8,16,320]{2,1,0:T(8,128)(2,1)S(1)}, bf16[8,16,320]{2,1,0:T(8,128)(2,1)S(1)}, u32[]{:S(2)}, u32[]{:S(2)}) collective-permute-start(bf16[8,16,320]{2,1,0:T(8,128)(2,1)S(1)} %get-tuple-element.36), channel_id=1, source_target_pairs={{0,2},{1,3},{2,0},{3,1},{4,6},{5,7},{6,4},{7,5},{8,10},{9,11},{10,... | collective-permute-start | bytes 245768 | tf_op jit(solution)/shard_map/ppermute | solution.py:376
  21.5 0.8 %collective-permute-start.4 = (bf16[8,16,320]{2,1,0:T(8,128)(2,1)S(1)}, bf16[8,16,320]{2,1,0:T(8,128)(2,1)S(1)}, u32[]{:S(2)}, u32[]{:S(2)}) collective-permute-start(bf16[8,16,320]{2,1,0:T(8,128)(2,1)S(1)} %get-tuple-element.37), channel_id=1, source_target_pairs={{0,3},{1,2},{2,1},{3,0},{4,7},{5,6},{6,5},{7,4},{8,11},{9,10},{10,... | collective-permute-start | bytes 245768 | tf_op jit(solution)/shard_map/ppermute | solution.py:376
  22.2 0.4 collective-permute-start.5
  22.6 2.0 %collective-permute-start.6 = (bf16[8,16,320]{2,1,0:T(8,128)(2,1)S(1)}, bf16[8,16,320]{2,1,0:T(8,128)(2,1)S(1)}, u32[]{:S(2)}, u32[]{:S(2)}) collective-permute-start(bf16[8,16,320]{2,1,0:T(8,128)(2,1)S(1)} %get-tuple-element.39), channel_id=1, source_target_pairs={{0,5},{1,4},{2,7},{3,6},{4,1},{5,0},{6,3},{7,2},{8,13},{9,12},{10,... | collective-permute-start | bytes 245768 | tf_op jit(solution)/shard_map/ppermute | solution.py:376
  24.6 0.9 %collective-permute-start.7 = (bf16[8,16,320]{2,1,0:T(8,128)(2,1)S(1)}, bf16[8,16,320]{2,1,0:T(8,128)(2,1)S(1)}, u32[]{:S(2)}, u32[]{:S(2)}) collective-permute-start(bf16[8,16,320]{2,1,0:T(8,128)(2,1)S(1)} %get-tuple-element.40), channel_id=1, source_target_pairs={{0,6},{1,7},{2,4},{3,5},{4,2},{5,3},{6,0},{7,1},{8,14},{9,15},{10,... | collective-permute-start | bytes 245768 | tf_op jit(solution)/shard_map/ppermute | solution.py:376
  25.5 0.9 %collective-permute-start.8 = (bf16[8,16,320]{2,1,0:T(8,128)(2,1)S(1)}, bf16[8,16,320]{2,1,0:T(8,128)(2,1)S(1)}, u32[]{:S(2)}, u32[]{:S(2)}) collective-permute-start(bf16[8,16,320]{2,1,0:T(8,128)(2,1)S(1)} %get-tuple-element.41), channel_id=1, source_target_pairs={{0,7},{1,6},{2,5},{3,4},{4,3},{5,2},{6,1},{7,0},{8,15},{9,14},{10,... | collective-permute-start | bytes 245768 | tf_op jit(solution)/shard_map/ppermute | solution.py:376
  26.4 1.6 %collective-permute-done.4.refs_3_ = bf16[8,16,320]{2,1,0:T(8,128)(2,1)S(1)} collective-permute-done((bf16[8,16,320]{2,1,0:T(8,128)(2,1)S(1)}, bf16[8,16,320]{2,1,0:T(8,128)(2,1)S(1)}, u32[]{:S(2)}, u32[]{:S(2)}) %collective-permute-start.4) | collective-permute-done | bytes 81952 | tf_op jit(solution)/shard_map/ppermute | solution.py:376
  28.0 1.3 %collective-permute-done.6.refs_5_ = bf16[8,16,320]{2,1,0:T(8,128)(2,1)S(1)} collective-permute-done((bf16[8,16,320]{2,1,0:T(8,128)(2,1)S(1)}, bf16[8,16,320]{2,1,0:T(8,128)(2,1)S(1)}, u32[]{:S(2)}, u32[]{:S(2)}) %collective-permute-start.6) | collective-permute-done | bytes 81952 | tf_op jit(solution)/shard_map/ppermute | solution.py:376
  29.4 0.5 collective-permute-done.7.refs_6_
  29.9 1.8 %collective-permute-done.8.refs_7_ = bf16[8,16,320]{2,1,0:T(8,128)(2,1)S(1)} collective-permute-done((bf16[8,16,320]{2,1,0:T(8,128)(2,1)S(1)}, bf16[8,16,320]{2,1,0:T(8,128)(2,1)S(1)}, u32[]{:S(2)}, u32[]{:S(2)}) %collective-permute-start.8) | collective-permute-done | bytes 81952 | tf_op jit(solution)/shard_map/ppermute | solution.py:376
  31.8 5.9 %collective-permute-start.14 = (bf16[4,4,16,320]{3,2,1,0:T(8,128)(2,1)S(1)}, bf16[4,4,16,320]{3,2,1,0:T(8,128)(2,1)S(1)}, u32[]{:S(2)}, u32[]{:S(2)}) collective-permute-start(bf16[4,4,16,320]{3,2,1,0:T(8,128)(2,1)S(1)} %get-tuple-element.51), channel_id=1, source_target_pairs={{8,16},{10,18},{12,20},{14,22},{24,32},{26,34},{28,36},{30,38},{40... | collective-permute-start | bytes 491528 | tf_op jit(solution)/shard_map/ppermute | solution.py:390
  37.8 1.5 %collective-permute-start.10 = (bf16[4,4,16,320]{3,2,1,0:T(8,128)(2,1)S(1)}, bf16[4,4,16,320]{3,2,1,0:T(8,128)(2,1)S(1)}, u32[]{:S(2)}, u32[]{:S(2)}) collective-permute-start(bf16[4,4,16,320]{3,2,1,0:T(8,128)(2,1)S(1)} %get-tuple-element.46), channel_id=1, source_target_pairs={{0,8},{2,10},{4,12},{6,14},{8,0},{10,2},{12,4},{14,6},{16,24},{18,... | collective-permute-start | bytes 491528 | tf_op jit(solution)/shard_map/ppermute | solution.py:391
  39.3 2.1 %collective-permute-start.9 = (bf16[4,4,16,320]{3,2,1,0:T(8,128)(2,1)S(1)}, bf16[4,4,16,320]{3,2,1,0:T(8,128)(2,1)S(1)}, u32[]{:S(2)}, u32[]{:S(2)}) collective-permute-start(bf16[4,4,16,320]{3,2,1,0:T(8,128)(2,1)S(1)} %get-tuple-element.45), channel_id=1, source_target_pairs={{8,16},{10,18},{12,20},{14,22},{24,32},{26,34},{28,36},{30,38},{40... | collective-permute-start | bytes 491528 | tf_op jit(solution)/shard_map/ppermute | solution.py:390
  41.4 1.9 %own_frames.1 = (bf16[8,128,384]{2,1,0:T(8,128)(2,1)S(1)}, bf16[8,128,768]{2,1,0:T(8,128)(2,1)S(1)}) custom-call(bf16[8,8,16,320]{3,2,1,0:T(8,128)(2,1)S(1)} %get-tuple-element.42.own_ref, f32[1,320]{1,0:T(1,128)S(1)} %reshape.36.gain_ref, bf16[320,320]{1,0:T(8,128)(2,1)S(1)} %copy-done.2, bf16[320,320]{1,0:T(8,128)(2,1)S(1)} %copy-done.3, ...), custom_call_target="tpu_custom_call" | custom-call | flops 2000000000 | tf_op jit(solution)/shard_map/own_frames/pallas_call | solution.py:393
  43.6 2.0 %window_attention.3 = (bf16[4,32,320]{2,1,0:T(8,128)(2,1)S(1)}, bf16[4,32,320]{2,1,0:T(8,128)(2,1)S(1)}, bf16[4,32,320]{2,1,0:T(8,128)(2,1)S(1)}, bf16[4,32,320]{2,1,0:T(8,128)(2,1)S(1)}) custom-call(bf16[8,8,16,320]{3,2,1,0:T(8,128)(2,1)S(1)} %get-tuple-element.42.own_ref, bf16[8,128,384]{2,1,0:T(8,128)(2,1)S(1)} %get-tuple-element.43.q_ref, ...), custom_call_target="tpu_custom_call" | custom-call | flops 2000000000 | tf_op jit(solution)/shard_map/window_attention/pallas_call | solution.py:406
  45.6 2.8 %collective-permute-start.16 = (bf16[4,32,320]{2,1,0:T(8,128)(2,1)S(1)}, bf16[4,32,320]{2,1,0:T(8,128)(2,1)S(1)}, u32[]{:S(2)}, u32[]{:S(2)}) collective-permute-start(bf16[4,32,320]{2,1,0:T(8,128)(2,1)S(1)} %get-tuple-element.54), channel_id=1, source_target_pairs={{0,2},{2,0},{4,6},{6,4},{8,10},{10,8},{12,14},{14,12},{16,18},{18,... | collective-permute-start | bytes 245768 | tf_op jit(solution)/shard_map/ppermute | solution.py:421
  48.3 1.7 %collective-permute-start.18 = (bf16[4,32,320]{2,1,0:T(8,128)(2,1)S(1)}, bf16[4,32,320]{2,1,0:T(8,128)(2,1)S(1)}, u32[]{:S(2)}, u32[]{:S(2)}) collective-permute-start(bf16[4,32,320]{2,1,0:T(8,128)(2,1)S(1)} %get-tuple-element.56), channel_id=1, source_target_pairs={{0,6},{2,4},{4,2},{6,0},{8,14},{10,12},{12,10},{14,8},{16,22},{18,... | collective-permute-start | bytes 245768 | tf_op jit(solution)/shard_map/ppermute | solution.py:421
  50.1 2.0 %window_attention.2 = (bf16[4,32,320]{2,1,0:T(8,128)(2,1)S(1)}, bf16[4,32,320]{2,1,0:T(8,128)(2,1)S(1)}, bf16[4,32,320]{2,1,0:T(8,128)(2,1)S(1)}, bf16[4,32,320]{2,1,0:T(8,128)(2,1)S(1)}) custom-call(bf16[8,8,16,320]{3,2,1,0:T(8,128)(2,1)S(1)} %get-tuple-element.42.own_ref, bf16[8,128,384]{2,1,0:T(8,128)(2,1)S(1)} %get-tuple-element.43.q_ref, ...), custom_call_target="tpu_custom_call" | custom-call | flops 2000000000 | tf_op jit(solution)/shard_map/window_attention/pallas_call | solution.py:406
  52.0 0.6 %collective-permute-start.11 = (bf16[4,32,320]{2,1,0:T(8,128)(2,1)S(1)}, bf16[4,32,320]{2,1,0:T(8,128)(2,1)S(1)}, u32[]{:S(2)}, u32[]{:S(2)}) collective-permute-start(bf16[4,32,320]{2,1,0:T(8,128)(2,1)S(1)} %get-tuple-element.48), channel_id=1, source_target_pairs={{0,2},{2,0},{4,6},{6,4},{8,10},{10,8},{12,14},{14,12},{16,18},{18,... | collective-permute-start | bytes 245768 | tf_op jit(solution)/shard_map/ppermute | solution.py:421
  52.7 1.7 %collective-permute-start.13 = (bf16[4,32,320]{2,1,0:T(8,128)(2,1)S(1)}, bf16[4,32,320]{2,1,0:T(8,128)(2,1)S(1)}, u32[]{:S(2)}, u32[]{:S(2)}) collective-permute-start(bf16[4,32,320]{2,1,0:T(8,128)(2,1)S(1)} %get-tuple-element.50), channel_id=1, source_target_pairs={{0,6},{2,4},{4,2},{6,0},{8,14},{10,12},{12,10},{14,8},{16,22},{18,... | collective-permute-start | bytes 245768 | tf_op jit(solution)/shard_map/ppermute | solution.py:421
  54.4 0.6 collective-permute-done.18.refs_7_
  55.0 2.0 %collective-permute-done.12.refs_2_ = bf16[4,32,320]{2,1,0:T(8,128)(2,1)S(1)} collective-permute-done((bf16[4,32,320]{2,1,0:T(8,128)(2,1)S(1)}, bf16[4,32,320]{2,1,0:T(8,128)(2,1)S(1)}, u32[]{:S(2)}, u32[]{:S(2)}) %collective-permute-start.12) | collective-permute-done | bytes 81952 | tf_op jit(solution)/shard_map/ppermute | solution.py:421
  57.0 2.3 %collective-permute-done.13.refs_3_ = bf16[4,32,320]{2,1,0:T(8,128)(2,1)S(1)} collective-permute-done((bf16[4,32,320]{2,1,0:T(8,128)(2,1)S(1)}, bf16[4,32,320]{2,1,0:T(8,128)(2,1)S(1)}, u32[]{:S(2)}, u32[]{:S(2)}) %collective-permute-start.13) | collective-permute-done | bytes 81952 | tf_op jit(solution)/shard_map/ppermute | solution.py:421
  59.3 1.2 %home.1 = bf16[4,2,320,128]{3,2,1,0:T(8,128)(2,1)} custom-call(bf16[4,32,320]{2,1,0:T(8,128)(2,1)S(1)} %get-tuple-element.47.refs_0_, bf16[4,32,320]{2,1,0:T(8,128)(2,1)S(1)} %collective-permute-done.11.refs_1_, bf16[4,32,320]{2,1,0:T(8,128)(2,1)S(1)} %collective-permute-done.12.refs_2_, bf16[4,32,320]{2,1,0:T(8,128)(2,1)S(1)} %collective-permute-done.13.refs_3_, ...), custom_call_target="tpu_custom_call" | custom-call | tf_op jit(solution)/shard_map/home/pallas_call | solution.py:422
  (38 shorter events, 1.2 us)
Async XLA Ops:
  0.0 7.0 %copy-start = (bf16[320,320]{1,0:T(8,128)(2,1)S(1)}, bf16[320,320]{1,0:T(8,128)(2,1)}, u32[]{:S(2)}) copy-start(bf16[320,320]{1,0:T(8,128)(2,1)} %param.13) | copy-start | bytes 614404
  1.0 5.8 %copy-start.7 = (s32[4]{0:T(128)S(1)}, s32[4]{0:T(128)}, u32[]{:S(2)}) copy-start(s32[4]{0:T(128)} %param.11) | copy-start | bytes 52
  1.0 6.7 %copy-start.1 = (bf16[4,2,128,320]{2,3,1,0:T(8,128)(2,1)S(1)}, bf16[4,2,128,320]{2,3,1,0:T(8,128)(2,1)}, u32[]{:S(2)}) copy-start(bf16[4,2,128,320]{2,3,1,0:T(8,128)(2,1)} %param.10) | copy-start | bytes 1966084
  1.0 6.7 %collective-permute-start.1 = (bf16[1,2,320,128]{3,2,1,0:T(8,128)(2,1)S(1)}, bf16[1,2,320,128]{3,2,1,0:T(8,128)(2,1)S(1)}, u32[]{:S(2)}, u32[]{:S(2)}) collective-permute-start(bf16[1,2,320,128]{3,2,1,0:T(8,128)(2,1)S(1)} %pick.1), channel_id=1, source_target_pairs={{0,1},{1,0},{2,3},{3,2},{4,5},{5,4},{6,7},{7,6},{8,9},{9,8},{10,11... | collective-permute-start | bytes 491528 | tf_op jit(solution)/shard_map/ppermute | solution.py:334
  6.6 6.3 %collective-permute-start = (bf16[1,2,320,128]{3,2,1,0:T(8,128)(2,1)S(1)}, bf16[1,2,320,128]{3,2,1,0:T(8,128)(2,1)S(1)}, u32[]{:S(2)}, u32[]{:S(2)}) collective-permute-start(bf16[1,2,320,128]{3,2,1,0:T(8,128)(2,1)S(1)} %get-tuple-element.31), channel_id=1, source_target_pairs={{0,1},{1,0},{2,3},{3,2},{4,5},{5,4},{6,7},{7,6},{8,9},{9,8},{10,11... | collective-permute-start | bytes 491528 | tf_op jit(solution)/shard_map/ppermute | solution.py:349
  11.7 14.6 %copy-start.6 = (f32[320]{0:T(512)S(1)}, f32[320]{0:T(512)}, u32[]{:S(2)}) copy-start(f32[320]{0:T(512)} %param.15) | copy-start | bytes 3844
  11.7 29.7 %copy-start.2 = (bf16[320,320]{1,0:T(8,128)(2,1)S(1)}, bf16[320,320]{1,0:T(8,128)(2,1)}, u32[]{:S(2)}) copy-start(bf16[320,320]{1,0:T(8,128)(2,1)} %wq_ref.1) | copy-start | bytes 614404
  11.8 29.7 %copy-start.3 = (bf16[320,320]{1,0:T(8,128)(2,1)S(1)}, bf16[320,320]{1,0:T(8,128)(2,1)}, u32[]{:S(2)}) copy-start(bf16[320,320]{1,0:T(8,128)(2,1)} %wk_ref.5) | copy-start | bytes 614404
  11.8 29.6 %copy-start.4 = (bf16[320,320]{1,0:T(8,128)(2,1)S(1)}, bf16[320,320]{1,0:T(8,128)(2,1)}, u32[]{:S(2)}) copy-start(bf16[320,320]{1,0:T(8,128)(2,1)} %wv_ref.5) | copy-start | bytes 614404
  17.1 7.5 %collective-permute-start.2 = (bf16[8,16,320]{2,1,0:T(8,128)(2,1)S(1)}, bf16[8,16,320]{2,1,0:T(8,128)(2,1)S(1)}, u32[]{:S(2)}, u32[]{:S(2)}) collective-permute-start(bf16[8,16,320]{2,1,0:T(8,128)(2,1)S(1)} %get-tuple-element.35), channel_id=1, source_target_pairs={{0,1},{1,0},{2,3},{3,2},{4,5},{5,4},{6,7},{7,6},{8,9},{9,8},{10,11... | collective-permute-start | bytes 245768 | tf_op jit(solution)/shard_map/ppermute | solution.py:376
  19.0 6.5 %collective-permute-start.3 = (bf16[8,16,320]{2,1,0:T(8,128)(2,1)S(1)}, bf16[8,16,320]{2,1,0:T(8,128)(2,1)S(1)}, u32[]{:S(2)}, u32[]{:S(2)}) collective-permute-start(bf16[8,16,320]{2,1,0:T(8,128)(2,1)S(1)} %get-tuple-element.36), channel_id=1, source_target_pairs={{0,2},{1,3},{2,0},{3,1},{4,6},{5,7},{6,4},{7,5},{8,10},{9,11},{10,... | collective-permute-start | bytes 245768 | tf_op jit(solution)/shard_map/ppermute | solution.py:376
  21.5 6.6 %collective-permute-start.4 = (bf16[8,16,320]{2,1,0:T(8,128)(2,1)S(1)}, bf16[8,16,320]{2,1,0:T(8,128)(2,1)S(1)}, u32[]{:S(2)}, u32[]{:S(2)}) collective-permute-start(bf16[8,16,320]{2,1,0:T(8,128)(2,1)S(1)} %get-tuple-element.37), channel_id=1, source_target_pairs={{0,3},{1,2},{2,1},{3,0},{4,7},{5,6},{6,5},{7,4},{8,11},{9,10},{10,... | collective-permute-start | bytes 245768 | tf_op jit(solution)/shard_map/ppermute | solution.py:376
  22.2 5.8 %collective-permute-start.5 = (bf16[8,16,320]{2,1,0:T(8,128)(2,1)S(1)}, bf16[8,16,320]{2,1,0:T(8,128)(2,1)S(1)}, u32[]{:S(2)}, u32[]{:S(2)}) collective-permute-start(bf16[8,16,320]{2,1,0:T(8,128)(2,1)S(1)} %get-tuple-element.38), channel_id=1, source_target_pairs={{0,4},{1,5},{2,6},{3,7},{4,0},{5,1},{6,2},{7,3},{8,12},{9,13},{10,... | collective-permute-start | bytes 245768 | tf_op jit(solution)/shard_map/ppermute | solution.py:376
  22.6 6.8 %collective-permute-start.6 = (bf16[8,16,320]{2,1,0:T(8,128)(2,1)S(1)}, bf16[8,16,320]{2,1,0:T(8,128)(2,1)S(1)}, u32[]{:S(2)}, u32[]{:S(2)}) collective-permute-start(bf16[8,16,320]{2,1,0:T(8,128)(2,1)S(1)} %get-tuple-element.39), channel_id=1, source_target_pairs={{0,5},{1,4},{2,7},{3,6},{4,1},{5,0},{6,3},{7,2},{8,13},{9,12},{10,... | collective-permute-start | bytes 245768 | tf_op jit(solution)/shard_map/ppermute | solution.py:376
  24.6 5.3 %collective-permute-start.7 = (bf16[8,16,320]{2,1,0:T(8,128)(2,1)S(1)}, bf16[8,16,320]{2,1,0:T(8,128)(2,1)S(1)}, u32[]{:S(2)}, u32[]{:S(2)}) collective-permute-start(bf16[8,16,320]{2,1,0:T(8,128)(2,1)S(1)} %get-tuple-element.40), channel_id=1, source_target_pairs={{0,6},{1,7},{2,4},{3,5},{4,2},{5,3},{6,0},{7,1},{8,14},{9,15},{10,... | collective-permute-start | bytes 245768 | tf_op jit(solution)/shard_map/ppermute | solution.py:376
  25.5 6.2 %collective-permute-start.8 = (bf16[8,16,320]{2,1,0:T(8,128)(2,1)S(1)}, bf16[8,16,320]{2,1,0:T(8,128)(2,1)S(1)}, u32[]{:S(2)}, u32[]{:S(2)}) collective-permute-start(bf16[8,16,320]{2,1,0:T(8,128)(2,1)S(1)} %get-tuple-element.41), channel_id=1, source_target_pairs={{0,7},{1,6},{2,5},{3,4},{4,3},{5,2},{6,1},{7,0},{8,15},{9,14},{10,... | collective-permute-start | bytes 245768 | tf_op jit(solution)/shard_map/ppermute | solution.py:376
  31.8 11.5 %collective-permute-start.14 = (bf16[4,4,16,320]{3,2,1,0:T(8,128)(2,1)S(1)}, bf16[4,4,16,320]{3,2,1,0:T(8,128)(2,1)S(1)}, u32[]{:S(2)}, u32[]{:S(2)}) collective-permute-start(bf16[4,4,16,320]{3,2,1,0:T(8,128)(2,1)S(1)} %get-tuple-element.51), channel_id=1, source_target_pairs={{8,16},{10,18},{12,20},{14,22},{24,32},{26,34},{28,36},{30,38},{40... | collective-permute-start | bytes 491528 | tf_op jit(solution)/shard_map/ppermute | solution.py:390
  37.8 5.8 %collective-permute-start.15 = (bf16[4,4,16,320]{3,2,1,0:T(8,128)(2,1)S(1)}, bf16[4,4,16,320]{3,2,1,0:T(8,128)(2,1)S(1)}, u32[]{:S(2)}, u32[]{:S(2)}) collective-permute-start(bf16[4,4,16,320]{3,2,1,0:T(8,128)(2,1)S(1)} %get-tuple-element.52), channel_id=1, source_target_pairs={{0,8},{2,10},{4,12},{6,14},{8,0},{10,2},{12,4},{14,6},{16,24},{18,... | collective-permute-start | bytes 491528 | tf_op jit(solution)/shard_map/ppermute | solution.py:391
  37.8 12.2 %collective-permute-start.10 = (bf16[4,4,16,320]{3,2,1,0:T(8,128)(2,1)S(1)}, bf16[4,4,16,320]{3,2,1,0:T(8,128)(2,1)S(1)}, u32[]{:S(2)}, u32[]{:S(2)}) collective-permute-start(bf16[4,4,16,320]{3,2,1,0:T(8,128)(2,1)S(1)} %get-tuple-element.46), channel_id=1, source_target_pairs={{0,8},{2,10},{4,12},{6,14},{8,0},{10,2},{12,4},{14,6},{16,24},{18,... | collective-permute-start | bytes 491528 | tf_op jit(solution)/shard_map/ppermute | solution.py:391
  39.3 10.8 %collective-permute-start.9 = (bf16[4,4,16,320]{3,2,1,0:T(8,128)(2,1)S(1)}, bf16[4,4,16,320]{3,2,1,0:T(8,128)(2,1)S(1)}, u32[]{:S(2)}, u32[]{:S(2)}) collective-permute-start(bf16[4,4,16,320]{3,2,1,0:T(8,128)(2,1)S(1)} %get-tuple-element.45), channel_id=1, source_target_pairs={{8,16},{10,18},{12,20},{14,22},{24,32},{26,34},{28,36},{30,38},{40... | collective-permute-start | bytes 491528 | tf_op jit(solution)/shard_map/ppermute | solution.py:390
  41.4 2.2 %copy-start.5 = (bf16[320,320]{1,0:T(8,128)(2,1)S(1)}, bf16[320,320]{1,0:T(8,128)(2,1)}, u32[]{:S(2)}) copy-start(bf16[320,320]{1,0:T(8,128)(2,1)} %wo_ref.3) | copy-start | bytes 614404
  45.6 7.1 %collective-permute-start.16 = (bf16[4,32,320]{2,1,0:T(8,128)(2,1)S(1)}, bf16[4,32,320]{2,1,0:T(8,128)(2,1)S(1)}, u32[]{:S(2)}, u32[]{:S(2)}) collective-permute-start(bf16[4,32,320]{2,1,0:T(8,128)(2,1)S(1)} %get-tuple-element.54), channel_id=1, source_target_pairs={{0,2},{2,0},{4,6},{6,4},{8,10},{10,8},{12,14},{14,12},{16,18},{18,... | collective-permute-start | bytes 245768 | tf_op jit(solution)/shard_map/ppermute | solution.py:421
  48.3 6.0 %collective-permute-start.17 = (bf16[4,32,320]{2,1,0:T(8,128)(2,1)S(1)}, bf16[4,32,320]{2,1,0:T(8,128)(2,1)S(1)}, u32[]{:S(2)}, u32[]{:S(2)}) collective-permute-start(bf16[4,32,320]{2,1,0:T(8,128)(2,1)S(1)} %get-tuple-element.55), channel_id=1, source_target_pairs={{0,4},{2,6},{4,0},{6,2},{8,12},{10,14},{12,8},{14,10},{16,20},{18,... | collective-permute-start | bytes 245768 | tf_op jit(solution)/shard_map/ppermute | solution.py:421
  48.3 6.6 %collective-permute-start.18 = (bf16[4,32,320]{2,1,0:T(8,128)(2,1)S(1)}, bf16[4,32,320]{2,1,0:T(8,128)(2,1)S(1)}, u32[]{:S(2)}, u32[]{:S(2)}) collective-permute-start(bf16[4,32,320]{2,1,0:T(8,128)(2,1)S(1)} %get-tuple-element.56), channel_id=1, source_target_pairs={{0,6},{2,4},{4,2},{6,0},{8,14},{10,12},{12,10},{14,8},{16,22},{18,... | collective-permute-start | bytes 245768 | tf_op jit(solution)/shard_map/ppermute | solution.py:421
  52.0 3.0 %collective-permute-start.11 = (bf16[4,32,320]{2,1,0:T(8,128)(2,1)S(1)}, bf16[4,32,320]{2,1,0:T(8,128)(2,1)S(1)}, u32[]{:S(2)}, u32[]{:S(2)}) collective-permute-start(bf16[4,32,320]{2,1,0:T(8,128)(2,1)S(1)} %get-tuple-element.48), channel_id=1, source_target_pairs={{0,2},{2,0},{4,6},{6,4},{8,10},{10,8},{12,14},{14,12},{16,18},{18,... | collective-permute-start | bytes 245768 | tf_op jit(solution)/shard_map/ppermute | solution.py:421
  52.7 4.4 %collective-permute-start.12 = (bf16[4,32,320]{2,1,0:T(8,128)(2,1)S(1)}, bf16[4,32,320]{2,1,0:T(8,128)(2,1)S(1)}, u32[]{:S(2)}, u32[]{:S(2)}) collective-permute-start(bf16[4,32,320]{2,1,0:T(8,128)(2,1)S(1)} %get-tuple-element.49), channel_id=1, source_target_pairs={{0,4},{2,6},{4,0},{6,2},{8,12},{10,14},{12,8},{14,10},{16,20},{18,... | collective-permute-start | bytes 245768 | tf_op jit(solution)/shard_map/ppermute | solution.py:421
  52.7 6.6 %collective-permute-start.13 = (bf16[4,32,320]{2,1,0:T(8,128)(2,1)S(1)}, bf16[4,32,320]{2,1,0:T(8,128)(2,1)S(1)}, u32[]{:S(2)}, u32[]{:S(2)}) collective-permute-start(bf16[4,32,320]{2,1,0:T(8,128)(2,1)S(1)} %get-tuple-element.50), channel_id=1, source_target_pairs={{0,6},{2,4},{4,2},{6,0},{8,14},{10,12},{12,10},{14,8},{16,22},{18,... | collective-permute-start | bytes 245768 | tf_op jit(solution)/shard_map/ppermute | solution.py:421

commit v4 on v3

--- a/solution.py
+++ b/solution.py
@@ -171,9 +171,9 @@
     before_ref, outs = rest[0], rest[1:9]
     for k in range(8):
         other = lax.bitwise_xor(ring, k)
-        base = 256 * lax.rem(other, 2) + 64 * lax.div(other, 2)
+        base = 256 * lax.rem(other, 2) + 32 * lax.div(other, 2)
         for b in range(8):
-            rows = pl.ds(pl.multiple_of(base + 8 * b, 8), 8)
+            rows = pl.ds(pl.multiple_of(base + 128 * (b // 4) + 8 * (b % 4), 8), 8)
             pair = [before_ref[rows, :], res_ref[rows, :]]
             outs[k][b] = jnp.concatenate(pair, axis=0).astype(BF16)
 
@@ -227,8 +227,9 @@
 
 
 def attention_kernel(
-    part, own_ref, q_ref, mine_ref, far_ref, near_ref, gain_ref, wk_ref, wv_ref, wo_ref, *rest
+    part, own_ref, q_ref, mine_ref, one_ref, two_ref, gain_ref, wk_ref, wv_ref, wo_ref, *rest
 ):
+    near_ref, far_ref = one_ref, two_ref
     outs, (norm_ref, kv_ref, att_ref, mixed_ref) = rest[:4], rest[4:]
     tm = lax.axis_index("tm")
     quad = lax.rem(tm, 4)
@@ -292,18 +293,19 @@
             outs[k][f] = mixed_ref[4 * other + f]
 
 
-def home_kernel(*refs):
-    pieces, out_ref, cells_ref = refs[:8], refs[8], refs[9]
+def home_kernel(part, *refs):
+    pieces, (out_ref, cells_ref, row_ref, sems) = refs[:4], refs[-4:]
     quad = lax.rem(lax.axis_index("tm"), 4)
-    for k in range(4):
-        for part in range(2):
-            start = pl.multiple_of(64 * lax.bitwise_xor(quad, k) + 32 * part, 32)
-            for f in range(4):
-                cells_ref[f, pl.ds(start, 32), :] = pieces[4 * part + k][f]
+    copies = []
     for f in range(4):
-        for row in range(2):
-            value = cells_ref[f, row * COLS : (row + 1) * COLS, :].astype(F32)
-            out_ref[f, row] = value.T.astype(BF16)
+        for k in range(4):
+            start = pl.multiple_of(32 * lax.bitwise_xor(quad, k), 32)
+            cells_ref[f, pl.ds(start, 32), :] = pieces[k][f]
+        row_ref[f] = cells_ref[f].astype(F32).T.astype(BF16)
+        copies.append(pltpu.make_async_copy(row_ref.at[f], out_ref.at[f, part], sems.at[f]))
+        copies[-1].start()
+    for copy in copies:
+        copy.wait()
 
 
 def cost(flops):
@@ -401,8 +403,9 @@
         name="own_frames",
     )(own, gain, w_query, w_key, w_value)
     swaps = [[(i, i ^ k) for i in range(size)] for k in range(4)]
-    back = []
+    home = []
     for part in range(2):
+        halos = [near[part], far[part]]
         pieces = pl.pallas_call(
             functools.partial(attention_kernel, part),
             out_shape=[array(4, 32, C)] * 4,
@@ -417,17 +420,23 @@
             compiler_params=params,
             cost_estimate=cost(2_000_000_000),
             name="window_attention",
-        )(own, query, mine, far[part], near[part], gain, w_key, w_value, w_out)
-        back += [pieces[0]] + [lax.ppermute(pieces[k], "tm", swaps[k]) for k in range(1, 4)]
-    home = pl.pallas_call(
-        home_kernel,
-        out_shape=jax.ShapeDtypeStruct((4, 2, C, COLS), BF16),
-        in_specs=vmem(8),
-        out_specs=pl.BlockSpec(memory_space=pltpu.VMEM),
-        scratch_shapes=[pltpu.VMEM((4, 256, C), BF16)],
-        compiler_params=params,
-        name="home",
-    )(*back)
+        )(own, query, mine, *halos, gain, w_key, w_value, w_out)
+        back = [pieces[0]] + [lax.ppermute(pieces[k], "tm", swaps[k]) for k in range(1, 4)]
+        home = pl.pallas_call(
+            functools.partial(home_kernel, part),
+            out_shape=array(4, 2, C, COLS),
+            in_specs=vmem(4) + [hbm] * part,
+            out_specs=hbm,
+            input_output_aliases={4: 0} if part else {},
+            scratch_shapes=[
+                pltpu.VMEM((4, COLS, C), BF16),
+                pltpu.VMEM((4, C, COLS), BF16),
+                pltpu.SemaphoreType.DMA((4,)),
+            ],
+            compiler_params=params,
+            cost_estimate=cost(1_000_000),
+            name="home",
+        )(*back, *([home] if part else []))
     return jnp.transpose(home, (0, 1, 3, 2))
 
 

time: 60.6 us -> 59.2 us (0.977)
  starting transfers between devices: 28.8 us -> 27.6 us
  waiting for transfers between devices: 11.9 us -> 10.9 us
    ppermute x6, starting transfers between devices: 6.84 us -> 5.8 us  [body(): lax.ppermute(pieces[k], 'tm', swaps[k])]
    ppermute x6, waiting for transfers between devices: 4.91 us -> 3.99 us  [body(): lax.ppermute(pieces[k], 'tm', swaps[k])]
    ppermute x2, starting transfers between devices: 8.01 us -> 7.38 us  [body(): far = [lax.ppermute(x, 'tm', both) for x in halves[2:]]]
    pallas_call x1 -> x2, Pallas kernels: 1.2 us -> 1.82 us  [body(): pl.pallas_call(functools.partial(home_kernel, part), out_shape=array(4, 2...]
  transfers between devices with their start and end apart: 19 -> 19, of which waited for: 10 -> 10; matrix products, arithmetic and copies ran while one was open for 1% -> 1% of each run, Pallas kernels for 21% -> 23%
where the time goes in v4:
time: 59.2 us; the launch traced here: 59 us
  starting transfers between devices  27.6 us (47%)
  Pallas kernels  19.6 us (33%)
  waiting for transfers between devices  10.9 us (18%)
    ppermute x7, starting transfers between devices, body(): lax.ppermute(pieces[k], AXES, swaps[k])  9.25 us
    pallas_call x2, Pallas kernels, body(): pl.pallas_call(functools.partial(block_kernel, frame), out_shape=piece if...  8.26 us
    ppermute x2, starting transfers between devices, body(): far = [lax.ppermute(x, 'tm', both) for x in halves[2:]]  7.38 us
    ppermute x6, starting transfers between devices, body(): lax.ppermute(pieces[k], 'tm', swaps[k])  5.8 us
    ppermute x7, waiting for transfers between devices, body(): lax.ppermute(pieces[k], AXES, swaps[k])  5.29 us
    ppermute x6, waiting for transfers between devices, body(): lax.ppermute(pieces[k], 'tm', swaps[k])  3.99 us
    pallas_call x2, Pallas kernels, body(): pl.pallas_call(functools.partial(attention_kernel, part), out_shape=[arra...  3.9 us
    ppermute x1, starting transfers between devices, body(): got = [lax.ppermute(send, 'height', [(0, 1), (1, 0)])]  2.99 us
  transfers between devices with their start and end apart: 19, of which 10 were waited for; matrix products, arithmetic and copies ran while one was open for 1% of the time, Pallas kernels for 23%

profile of v4, /device:TPU:7, one launch (start us, length us, event | category | flops | bytes accessed | tf_op | source)
XLA Modules:
  0.0 59.0 jit_solution(9118586560921935992)
XLA Ops:
  0.0 1.0 %pick.1 = bf16[1,2,320,128]{3,2,1,0:T(8,128)(2,1)S(1)} custom-call(bf16[4,2,320,128]{3,2,1,0:T(8,128)(2,1)} %bitcast.3), custom_call_target="tpu_custom_call" | custom-call | tf_op jit(solution)/shard_map/pick/pallas_call | solution.py:327
  1.0 3.0 %collective-permute-start.1 = (bf16[1,2,320,128]{3,2,1,0:T(8,128)(2,1)S(1)}, bf16[1,2,320,128]{3,2,1,0:T(8,128)(2,1)S(1)}, u32[]{:S(2)}, u32[]{:S(2)}) collective-permute-start(bf16[1,2,320,128]{3,2,1,0:T(8,128)(2,1)S(1)} %pick.1), channel_id=1, source_target_pairs={{0,1},{1,0},{2,3},{3,2},{4,5},{5,4},{6,7},{7,6},{8,9},{9,8},{10,11... | collective-permute-start | bytes 491528 | tf_op jit(solution)/shard_map/ppermute | solution.py:336
  4.0 2.6 %pack_weights.1 = (bf16[1024,960]{1,0:T(8,128)(2,1)S(1)}, bf16[1024,960]{1,0:T(8,128)(2,1)S(1)}, bf16[1,2,320,128]{3,2,1,0:T(8,128)(2,1)S(1)}) custom-call(bf16[3,3,320,320]{3,2,1,0:T(8,128)(2,1)} %first_ref.1, bf16[3,3,320,320]{3,2,1,0:T(8,128)(2,1)} %second_ref.1, bf16[4,2,320,128]{3,2,1,0:T(8,128)(2,1)} %bitcast.4), custom_call_target="tpu_custom_call" | custom-call | flops 1000000000 | tf_op jit(solution)/shard_map/pack_weights/pallas_call | solution.py:337
  7.7 4.1 %resblock.2.rest_0_ = f32[512,320]{1,0:T(8,128)S(1)} custom-call(bf16[4,2,320,128]{3,2,1,0:T(8,128)(2,1)S(1)} %bitcast.5, bf16[1,2,320,128]{3,2,1,0:T(8,128)(2,1)S(1)} %collective-permute-done.1.got_ref, bf16[1024,960]{1,0:T(8,128)(2,1)S(1)} %get-tuple-element.32.first_ref, bf16[1024,960]{1,0:T(8,128)(2,1)S(1)} %get-tuple-element.33.second_ref, ...), custom_call_target="tpu_custom_call" | custom-call | flops 4000000000 | tf_op jit(solution)/shard_map/resblock/pallas_call | solution.py:360
  11.8 1.2 %collective-permute-done.got_ref = bf16[1,2,320,128]{3,2,1,0:T(8,128)(2,1)S(1)} collective-permute-done((bf16[1,2,320,128]{3,2,1,0:T(8,128)(2,1)S(1)}, bf16[1,2,320,128]{3,2,1,0:T(8,128)(2,1)S(1)}, u32[]{:S(2)}, u32[]{:S(2)}) %collective-permute-start) | collective-permute-done | bytes 163872 | tf_op jit(solution)/shard_map/ppermute | solution.py:351
  12.9 4.2 %resblock.3 = (bf16[8,16,320]{2,1,0:T(8,128)(2,1)S(1)}, bf16[8,16,320]{2,1,0:T(8,128)(2,1)S(1)}, bf16[8,16,320]{2,1,0:T(8,128)(2,1)S(1)}, bf16[8,16,320]{2,1,0:T...) custom-call(bf16[4,2,320,128]{3,2,1,0:T(8,128)(2,1)S(1)} %bitcast.6,, ...), custom_call_target="tpu_custom_call" | custom-call | flops 4000000000 | tf_op jit(solution)/shard_map/resblock/pallas_call | solution.py:360
  17.1 1.9 %collective-permute-start.2 = (bf16[8,16,320]{2,1,0:T(8,128)(2,1)S(1)}, bf16[8,16,320]{2,1,0:T(8,128)(2,1)S(1)}, u32[]{:S(2)}, u32[]{:S(2)}) collective-permute-start(bf16[8,16,320]{2,1,0:T(8,128)(2,1)S(1)} %get-tuple-element.35), channel_id=1, source_target_pairs={{0,1},{1,0},{2,3},{3,2},{4,5},{5,4},{6,7},{7,6},{8,9},{9,8},{10,11... | collective-permute-start | bytes 245768 | tf_op jit(solution)/shard_map/ppermute | solution.py:378
  19.0 2.5 %collective-permute-start.3 = (bf16[8,16,320]{2,1,0:T(8,128)(2,1)S(1)}, bf16[8,16,320]{2,1,0:T(8,128)(2,1)S(1)}, u32[]{:S(2)}, u32[]{:S(2)}) collective-permute-start(bf16[8,16,320]{2,1,0:T(8,128)(2,1)S(1)} %get-tuple-element.36), channel_id=1, source_target_pairs={{0,2},{1,3},{2,0},{3,1},{4,6},{5,7},{6,4},{7,5},{8,10},{9,11},{10,... | collective-permute-start | bytes 245768 | tf_op jit(solution)/shard_map/ppermute | solution.py:378
  21.5 0.8 %collective-permute-start.4 = (bf16[8,16,320]{2,1,0:T(8,128)(2,1)S(1)}, bf16[8,16,320]{2,1,0:T(8,128)(2,1)S(1)}, u32[]{:S(2)}, u32[]{:S(2)}) collective-permute-start(bf16[8,16,320]{2,1,0:T(8,128)(2,1)S(1)} %get-tuple-element.37), channel_id=1, source_target_pairs={{0,3},{1,2},{2,1},{3,0},{4,7},{5,6},{6,5},{7,4},{8,11},{9,10},{10,... | collective-permute-start | bytes 245768 | tf_op jit(solution)/shard_map/ppermute | solution.py:378
  22.2 0.4 collective-permute-start.5
  22.6 2.0 %collective-permute-start.6 = (bf16[8,16,320]{2,1,0:T(8,128)(2,1)S(1)}, bf16[8,16,320]{2,1,0:T(8,128)(2,1)S(1)}, u32[]{:S(2)}, u32[]{:S(2)}) collective-permute-start(bf16[8,16,320]{2,1,0:T(8,128)(2,1)S(1)} %get-tuple-element.39), channel_id=1, source_target_pairs={{0,5},{1,4},{2,7},{3,6},{4,1},{5,0},{6,3},{7,2},{8,13},{9,12},{10,... | collective-permute-start | bytes 245768 | tf_op jit(solution)/shard_map/ppermute | solution.py:378
  24.6 0.9 %collective-permute-start.7 = (bf16[8,16,320]{2,1,0:T(8,128)(2,1)S(1)}, bf16[8,16,320]{2,1,0:T(8,128)(2,1)S(1)}, u32[]{:S(2)}, u32[]{:S(2)}) collective-permute-start(bf16[8,16,320]{2,1,0:T(8,128)(2,1)S(1)} %get-tuple-element.40), channel_id=1, source_target_pairs={{0,6},{1,7},{2,4},{3,5},{4,2},{5,3},{6,0},{7,1},{8,14},{9,15},{10,... | collective-permute-start | bytes 245768 | tf_op jit(solution)/shard_map/ppermute | solution.py:378
  25.5 0.9 %collective-permute-start.8 = (bf16[8,16,320]{2,1,0:T(8,128)(2,1)S(1)}, bf16[8,16,320]{2,1,0:T(8,128)(2,1)S(1)}, u32[]{:S(2)}, u32[]{:S(2)}) collective-permute-start(bf16[8,16,320]{2,1,0:T(8,128)(2,1)S(1)} %get-tuple-element.41), channel_id=1, source_target_pairs={{0,7},{1,6},{2,5},{3,4},{4,3},{5,2},{6,1},{7,0},{8,15},{9,14},{10,... | collective-permute-start | bytes 245768 | tf_op jit(solution)/shard_map/ppermute | solution.py:378
  26.4 1.6 %collective-permute-done.4.refs_3_ = bf16[8,16,320]{2,1,0:T(8,128)(2,1)S(1)} collective-permute-done((bf16[8,16,320]{2,1,0:T(8,128)(2,1)S(1)}, bf16[8,16,320]{2,1,0:T(8,128)(2,1)S(1)}, u32[]{:S(2)}, u32[]{:S(2)}) %collective-permute-start.4) | collective-permute-done | bytes 81952 | tf_op jit(solution)/shard_map/ppermute | solution.py:378
  28.0 1.3 %collective-permute-done.6.refs_5_ = bf16[8,16,320]{2,1,0:T(8,128)(2,1)S(1)} collective-permute-done((bf16[8,16,320]{2,1,0:T(8,128)(2,1)S(1)}, bf16[8,16,320]{2,1,0:T(8,128)(2,1)S(1)}, u32[]{:S(2)}, u32[]{:S(2)}) %collective-permute-start.6) | collective-permute-done | bytes 81952 | tf_op jit(solution)/shard_map/ppermute | solution.py:378
  29.4 0.5 collective-permute-done.7.refs_6_
  29.9 1.8 %collective-permute-done.8.refs_7_ = bf16[8,16,320]{2,1,0:T(8,128)(2,1)S(1)} collective-permute-done((bf16[8,16,320]{2,1,0:T(8,128)(2,1)S(1)}, bf16[8,16,320]{2,1,0:T(8,128)(2,1)S(1)}, u32[]{:S(2)}, u32[]{:S(2)}) %collective-permute-start.8) | collective-permute-done | bytes 81952 | tf_op jit(solution)/shard_map/ppermute | solution.py:378
  31.8 1.7 %collective-permute-start.14 = (bf16[4,4,16,320]{3,2,1,0:T(8,128)(2,1)S(1)}, bf16[4,4,16,320]{3,2,1,0:T(8,128)(2,1)S(1)}, u32[]{:S(2)}, u32[]{:S(2)}) collective-permute-start(bf16[4,4,16,320]{3,2,1,0:T(8,128)(2,1)S(1)} %get-tuple-element.51), channel_id=1, source_target_pairs={{0,8},{2,10},{4,12},{6,14},{8,0},{10,2},{12,4},{14,6},{16,24},{18,... | collective-permute-start | bytes 491528 | tf_op jit(solution)/shard_map/ppermute | solution.py:393
  33.5 4.4 %collective-permute-start.15 = (bf16[4,4,16,320]{3,2,1,0:T(8,128)(2,1)S(1)}, bf16[4,4,16,320]{3,2,1,0:T(8,128)(2,1)S(1)}, u32[]{:S(2)}, u32[]{:S(2)}) collective-permute-start(bf16[4,4,16,320]{3,2,1,0:T(8,128)(2,1)S(1)} %get-tuple-element.52), channel_id=1, source_target_pairs={{8,16},{10,18},{12,20},{14,22},{24,32},{26,34},{28,36},{30,38},{40... | collective-permute-start | bytes 491528 | tf_op jit(solution)/shard_map/ppermute | solution.py:392
  37.9 3.0 %collective-permute-start.10 = (bf16[4,4,16,320]{3,2,1,0:T(8,128)(2,1)S(1)}, bf16[4,4,16,320]{3,2,1,0:T(8,128)(2,1)S(1)}, u32[]{:S(2)}, u32[]{:S(2)}) collective-permute-start(bf16[4,4,16,320]{3,2,1,0:T(8,128)(2,1)S(1)} %get-tuple-element.46), channel_id=1, source_target_pairs={{8,16},{10,18},{12,20},{14,22},{24,32},{26,34},{28,36},{30,38},{40... | collective-permute-start | bytes 491528 | tf_op jit(solution)/shard_map/ppermute | solution.py:392
  41.2 1.9 %own_frames.1 = (bf16[8,128,384]{2,1,0:T(8,128)(2,1)S(1)}, bf16[8,128,768]{2,1,0:T(8,128)(2,1)S(1)}) custom-call(bf16[8,8,16,320]{3,2,1,0:T(8,128)(2,1)S(1)} %get-tuple-element.42.own_ref, f32[1,320]{1,0:T(1,128)S(1)} %reshape.36.gain_ref, bf16[320,320]{1,0:T(8,128)(2,1)S(1)} %copy-done.2, bf16[320,320]{1,0:T(8,128)(2,1)S(1)} %copy-done.3, ...), custom_call_target="tpu_custom_call" | custom-call | flops 2000000000 | tf_op jit(solution)/shard_map/own_frames/pallas_call | solution.py:395
  43.3 2.0 %window_attention.3 = (bf16[4,32,320]{2,1,0:T(8,128)(2,1)S(1)}, bf16[4,32,320]{2,1,0:T(8,128)(2,1)S(1)}, bf16[4,32,320]{2,1,0:T(8,128)(2,1)S(1)}, bf16[4,32,320]{2,1,0:T(8,128)(2,1)S(1)}) custom-call(bf16[8,8,16,320]{3,2,1,0:T(8,128)(2,1)S(1)} %get-tuple-element.42.own_ref, bf16[8,128,384]{2,1,0:T(8,128)(2,1)S(1)} %get-tuple-element.43.q_ref, ...), custom_call_target="tpu_custom_call" | custom-call | flops 2000000000 | tf_op jit(solution)/shard_map/window_attention/pallas_call | solution.py:409
  45.3 1.6 %collective-permute-start.16 = (bf16[4,32,320]{2,1,0:T(8,128)(2,1)S(1)}, bf16[4,32,320]{2,1,0:T(8,128)(2,1)S(1)}, u32[]{:S(2)}, u32[]{:S(2)}) collective-permute-start(bf16[4,32,320]{2,1,0:T(8,128)(2,1)S(1)} %get-tuple-element.54), channel_id=1, source_target_pairs={{0,2},{2,0},{4,6},{6,4},{8,10},{10,8},{12,14},{14,12},{16,18},{18,... | collective-permute-start | bytes 245768 | tf_op jit(solution)/shard_map/ppermute | solution.py:424
  46.9 1.7 %collective-permute-start.18 = (bf16[4,32,320]{2,1,0:T(8,128)(2,1)S(1)}, bf16[4,32,320]{2,1,0:T(8,128)(2,1)S(1)}, u32[]{:S(2)}, u32[]{:S(2)}) collective-permute-start(bf16[4,32,320]{2,1,0:T(8,128)(2,1)S(1)} %get-tuple-element.56), channel_id=1, source_target_pairs={{0,6},{2,4},{4,2},{6,0},{8,14},{10,12},{12,10},{14,8},{16,22},{18,... | collective-permute-start | bytes 245768 | tf_op jit(solution)/shard_map/ppermute | solution.py:424
  48.6 2.0 %window_attention.2 = (bf16[4,32,320]{2,1,0:T(8,128)(2,1)S(1)}, bf16[4,32,320]{2,1,0:T(8,128)(2,1)S(1)}, bf16[4,32,320]{2,1,0:T(8,128)(2,1)S(1)}, bf16[4,32,320]{2,1,0:T(8,128)(2,1)S(1)}) custom-call(bf16[8,8,16,320]{3,2,1,0:T(8,128)(2,1)S(1)} %get-tuple-element.42.own_ref, bf16[8,128,384]{2,1,0:T(8,128)(2,1)S(1)} %get-tuple-element.43.q_ref, ...), custom_call_target="tpu_custom_call" | custom-call | flops 2000000000 | tf_op jit(solution)/shard_map/window_attention/pallas_call | solution.py:409
  50.6 0.7 %collective-permute-start.11 = (bf16[4,32,320]{2,1,0:T(8,128)(2,1)S(1)}, bf16[4,32,320]{2,1,0:T(8,128)(2,1)S(1)}, u32[]{:S(2)}, u32[]{:S(2)}) collective-permute-start(bf16[4,32,320]{2,1,0:T(8,128)(2,1)S(1)} %get-tuple-element.48), channel_id=1, source_target_pairs={{0,2},{2,0},{4,6},{6,4},{8,10},{10,8},{12,14},{14,12},{16,18},{18,... | collective-permute-start | bytes 245768 | tf_op jit(solution)/shard_map/ppermute | solution.py:424
  51.3 1.7 %collective-permute-start.13 = (bf16[4,32,320]{2,1,0:T(8,128)(2,1)S(1)}, bf16[4,32,320]{2,1,0:T(8,128)(2,1)S(1)}, u32[]{:S(2)}, u32[]{:S(2)}) collective-permute-start(bf16[4,32,320]{2,1,0:T(8,128)(2,1)S(1)} %get-tuple-element.50), channel_id=1, source_target_pairs={{0,6},{2,4},{4,2},{6,0},{8,14},{10,12},{12,10},{14,8},{16,22},{18,... | collective-permute-start | bytes 245768 | tf_op jit(solution)/shard_map/ppermute | solution.py:424
  53.0 0.5 collective-permute-done.18.refs_3_
  53.5 0.9 %home.2.refs_4_ = bf16[4,2,320,128]{3,2,1,0:T(8,128)(2,1)} custom-call(bf16[4,32,320]{2,1,0:T(8,128)(2,1)S(1)} %get-tuple-element.53.refs_0_, bf16[4,32,320]{2,1,0:T(8,128)(2,1)S(1)} %collective-permute-done.16.refs_1_, bf16[4,32,320]{2,1,0:T(8,128)(2,1)S(1)} %collective-permute-done.17.refs_2_, bf16[4,32,320]{2,1,0:T(8,128)(2,1)S(1)} %collective-permute-done.18.refs_3_), custom_call_target="tpu_custom_call" | custom-call | flops 1000000 | tf_op jit(solution)/shard_map/home/pallas_call | solution.py:425
  54.5 1.2 %collective-permute-done.12.refs_2_ = bf16[4,32,320]{2,1,0:T(8,128)(2,1)S(1)} collective-permute-done((bf16[4,32,320]{2,1,0:T(8,128)(2,1)S(1)}, bf16[4,32,320]{2,1,0:T(8,128)(2,1)S(1)}, u32[]{:S(2)}, u32[]{:S(2)}) %collective-permute-start.12) | collective-permute-done | bytes 81952 | tf_op jit(solution)/shard_map/ppermute | solution.py:424
  55.7 2.3 %collective-permute-done.13.refs_3_ = bf16[4,32,320]{2,1,0:T(8,128)(2,1)S(1)} collective-permute-done((bf16[4,32,320]{2,1,0:T(8,128)(2,1)S(1)}, bf16[4,32,320]{2,1,0:T(8,128)(2,1)S(1)}, u32[]{:S(2)}, u32[]{:S(2)}) %collective-permute-start.13) | collective-permute-done | bytes 81952 | tf_op jit(solution)/shard_map/ppermute | solution.py:424
  57.9 0.9 %home.3 = bf16[4,2,320,128]{3,2,1,0:T(8,128)(2,1)} custom-call(bf16[4,32,320]{2,1,0:T(8,128)(2,1)S(1)} %get-tuple-element.47.refs_0_, bf16[4,32,320]{2,1,0:T(8,128)(2,1)S(1)} %collective-permute-done.11.refs_1_, bf16[4,32,320]{2,1,0:T(8,128)(2,1)S(1)} %collective-permute-done.12.refs_2_, ...), custom_call_target="tpu_custom_call", output_to_operand_aliasing={{}: (4, {})} | custom-call | flops 1000000 | tf_op jit(solution)/shard_map/home/pallas_call | solution.py:425
  (39 shorter events, 1.6 us)
Async XLA Ops:
  0.0 7.0 %copy-start = (bf16[320,320]{1,0:T(8,128)(2,1)S(1)}, bf16[320,320]{1,0:T(8,128)(2,1)}, u32[]{:S(2)}) copy-start(bf16[320,320]{1,0:T(8,128)(2,1)} %param.13) | copy-start | bytes 614404
  1.0 5.8 %copy-start.7 = (s32[4]{0:T(128)S(1)}, s32[4]{0:T(128)}, u32[]{:S(2)}) copy-start(s32[4]{0:T(128)} %param.11) | copy-start | bytes 52
  1.0 6.7 %copy-start.1 = (bf16[4,2,128,320]{2,3,1,0:T(8,128)(2,1)S(1)}, bf16[4,2,128,320]{2,3,1,0:T(8,128)(2,1)}, u32[]{:S(2)}) copy-start(bf16[4,2,128,320]{2,3,1,0:T(8,128)(2,1)} %param.10) | copy-start | bytes 1966084
  1.0 6.7 %collective-permute-start.1 = (bf16[1,2,320,128]{3,2,1,0:T(8,128)(2,1)S(1)}, bf16[1,2,320,128]{3,2,1,0:T(8,128)(2,1)S(1)}, u32[]{:S(2)}, u32[]{:S(2)}) collective-permute-start(bf16[1,2,320,128]{3,2,1,0:T(8,128)(2,1)S(1)} %pick.1), channel_id=1, source_target_pairs={{0,1},{1,0},{2,3},{3,2},{4,5},{5,4},{6,7},{7,6},{8,9},{9,8},{10,11... | collective-permute-start | bytes 491528 | tf_op jit(solution)/shard_map/ppermute | solution.py:336
  6.6 6.3 %collective-permute-start = (bf16[1,2,320,128]{3,2,1,0:T(8,128)(2,1)S(1)}, bf16[1,2,320,128]{3,2,1,0:T(8,128)(2,1)S(1)}, u32[]{:S(2)}, u32[]{:S(2)}) collective-permute-start(bf16[1,2,320,128]{3,2,1,0:T(8,128)(2,1)S(1)} %get-tuple-element.31), channel_id=1, source_target_pairs={{0,1},{1,0},{2,3},{3,2},{4,5},{5,4},{6,7},{7,6},{8,9},{9,8},{10,11... | collective-permute-start | bytes 491528 | tf_op jit(solution)/shard_map/ppermute | solution.py:351
  11.7 14.6 %copy-start.6 = (f32[320]{0:T(512)S(1)}, f32[320]{0:T(512)}, u32[]{:S(2)}) copy-start(f32[320]{0:T(512)} %param.15) | copy-start | bytes 3844
  11.7 29.5 %copy-start.2 = (bf16[320,320]{1,0:T(8,128)(2,1)S(1)}, bf16[320,320]{1,0:T(8,128)(2,1)}, u32[]{:S(2)}) copy-start(bf16[320,320]{1,0:T(8,128)(2,1)} %wq_ref.1) | copy-start | bytes 614404
  11.8 29.5 %copy-start.3 = (bf16[320,320]{1,0:T(8,128)(2,1)S(1)}, bf16[320,320]{1,0:T(8,128)(2,1)}, u32[]{:S(2)}) copy-start(bf16[320,320]{1,0:T(8,128)(2,1)} %wk_ref.5) | copy-start | bytes 614404
  11.8 29.4 %copy-start.4 = (bf16[320,320]{1,0:T(8,128)(2,1)S(1)}, bf16[320,320]{1,0:T(8,128)(2,1)}, u32[]{:S(2)}) copy-start(bf16[320,320]{1,0:T(8,128)(2,1)} %wv_ref.5) | copy-start | bytes 614404
  17.1 7.5 %collective-permute-start.2 = (bf16[8,16,320]{2,1,0:T(8,128)(2,1)S(1)}, bf16[8,16,320]{2,1,0:T(8,128)(2,1)S(1)}, u32[]{:S(2)}, u32[]{:S(2)}) collective-permute-start(bf16[8,16,320]{2,1,0:T(8,128)(2,1)S(1)} %get-tuple-element.35), channel_id=1, source_target_pairs={{0,1},{1,0},{2,3},{3,2},{4,5},{5,4},{6,7},{7,6},{8,9},{9,8},{10,11... | collective-permute-start | bytes 245768 | tf_op jit(solution)/shard_map/ppermute | solution.py:378
  19.0 6.5 %collective-permute-start.3 = (bf16[8,16,320]{2,1,0:T(8,128)(2,1)S(1)}, bf16[8,16,320]{2,1,0:T(8,128)(2,1)S(1)}, u32[]{:S(2)}, u32[]{:S(2)}) collective-permute-start(bf16[8,16,320]{2,1,0:T(8,128)(2,1)S(1)} %get-tuple-element.36), channel_id=1, source_target_pairs={{0,2},{1,3},{2,0},{3,1},{4,6},{5,7},{6,4},{7,5},{8,10},{9,11},{10,... | collective-permute-start | bytes 245768 | tf_op jit(solution)/shard_map/ppermute | solution.py:378
  21.5 6.6 %collective-permute-start.4 = (bf16[8,16,320]{2,1,0:T(8,128)(2,1)S(1)}, bf16[8,16,320]{2,1,0:T(8,128)(2,1)S(1)}, u32[]{:S(2)}, u32[]{:S(2)}) collective-permute-start(bf16[8,16,320]{2,1,0:T(8,128)(2,1)S(1)} %get-tuple-element.37), channel_id=1, source_target_pairs={{0,3},{1,2},{2,1},{3,0},{4,7},{5,6},{6,5},{7,4},{8,11},{9,10},{10,... | collective-permute-start | bytes 245768 | tf_op jit(solution)/shard_map/ppermute | solution.py:378
  22.2 5.8 %collective-permute-start.5 = (bf16[8,16,320]{2,1,0:T(8,128)(2,1)S(1)}, bf16[8,16,320]{2,1,0:T(8,128)(2,1)S(1)}, u32[]{:S(2)}, u32[]{:S(2)}) collective-permute-start(bf16[8,16,320]{2,1,0:T(8,128)(2,1)S(1)} %get-tuple-element.38), channel_id=1, source_target_pairs={{0,4},{1,5},{2,6},{3,7},{4,0},{5,1},{6,2},{7,3},{8,12},{9,13},{10,... | collective-permute-start | bytes 245768 | tf_op jit(solution)/shard_map/ppermute | solution.py:378
  22.6 6.8 %collective-permute-start.6 = (bf16[8,16,320]{2,1,0:T(8,128)(2,1)S(1)}, bf16[8,16,320]{2,1,0:T(8,128)(2,1)S(1)}, u32[]{:S(2)}, u32[]{:S(2)}) collective-permute-start(bf16[8,16,320]{2,1,0:T(8,128)(2,1)S(1)} %get-tuple-element.39), channel_id=1, source_target_pairs={{0,5},{1,4},{2,7},{3,6},{4,1},{5,0},{6,3},{7,2},{8,13},{9,12},{10,... | collective-permute-start | bytes 245768 | tf_op jit(solution)/shard_map/ppermute | solution.py:378
  24.6 5.3 %collective-permute-start.7 = (bf16[8,16,320]{2,1,0:T(8,128)(2,1)S(1)}, bf16[8,16,320]{2,1,0:T(8,128)(2,1)S(1)}, u32[]{:S(2)}, u32[]{:S(2)}) collective-permute-start(bf16[8,16,320]{2,1,0:T(8,128)(2,1)S(1)} %get-tuple-element.40), channel_id=1, source_target_pairs={{0,6},{1,7},{2,4},{3,5},{4,2},{5,3},{6,0},{7,1},{8,14},{9,15},{10,... | collective-permute-start | bytes 245768 | tf_op jit(solution)/shard_map/ppermute | solution.py:378
  25.5 6.2 %collective-permute-start.8 = (bf16[8,16,320]{2,1,0:T(8,128)(2,1)S(1)}, bf16[8,16,320]{2,1,0:T(8,128)(2,1)S(1)}, u32[]{:S(2)}, u32[]{:S(2)}) collective-permute-start(bf16[8,16,320]{2,1,0:T(8,128)(2,1)S(1)} %get-tuple-element.41), channel_id=1, source_target_pairs={{0,7},{1,6},{2,5},{3,4},{4,3},{5,2},{6,1},{7,0},{8,15},{9,14},{10,... | collective-permute-start | bytes 245768 | tf_op jit(solution)/shard_map/ppermute | solution.py:378
  31.8 11.3 %collective-permute-start.14 = (bf16[4,4,16,320]{3,2,1,0:T(8,128)(2,1)S(1)}, bf16[4,4,16,320]{3,2,1,0:T(8,128)(2,1)S(1)}, u32[]{:S(2)}, u32[]{:S(2)}) collective-permute-start(bf16[4,4,16,320]{3,2,1,0:T(8,128)(2,1)S(1)} %get-tuple-element.51), channel_id=1, source_target_pairs={{0,8},{2,10},{4,12},{6,14},{8,0},{10,2},{12,4},{14,6},{16,24},{18,... | collective-permute-start | bytes 491528 | tf_op jit(solution)/shard_map/ppermute | solution.py:393
  33.5 9.8 %collective-permute-start.15 = (bf16[4,4,16,320]{3,2,1,0:T(8,128)(2,1)S(1)}, bf16[4,4,16,320]{3,2,1,0:T(8,128)(2,1)S(1)}, u32[]{:S(2)}, u32[]{:S(2)}) collective-permute-start(bf16[4,4,16,320]{3,2,1,0:T(8,128)(2,1)S(1)} %get-tuple-element.52), channel_id=1, source_target_pairs={{8,16},{10,18},{12,20},{14,22},{24,32},{26,34},{28,36},{30,38},{40... | collective-permute-start | bytes 491528 | tf_op jit(solution)/shard_map/ppermute | solution.py:392
  37.9 10.7 %collective-permute-start.10 = (bf16[4,4,16,320]{3,2,1,0:T(8,128)(2,1)S(1)}, bf16[4,4,16,320]{3,2,1,0:T(8,128)(2,1)S(1)}, u32[]{:S(2)}, u32[]{:S(2)}) collective-permute-start(bf16[4,4,16,320]{3,2,1,0:T(8,128)(2,1)S(1)} %get-tuple-element.46), channel_id=1, source_target_pairs={{8,16},{10,18},{12,20},{14,22},{24,32},{26,34},{28,36},{30,38},{40... | collective-permute-start | bytes 491528 | tf_op jit(solution)/shard_map/ppermute | solution.py:392
  40.9 7.7 %collective-permute-start.9 = (bf16[4,4,16,320]{3,2,1,0:T(8,128)(2,1)S(1)}, bf16[4,4,16,320]{3,2,1,0:T(8,128)(2,1)S(1)}, u32[]{:S(2)}, u32[]{:S(2)}) collective-permute-start(bf16[4,4,16,320]{3,2,1,0:T(8,128)(2,1)S(1)} %get-tuple-element.45), channel_id=1, source_target_pairs={{0,8},{2,10},{4,12},{6,14},{8,0},{10,2},{12,4},{14,6},{16,24},{18,... | collective-permute-start | bytes 491528 | tf_op jit(solution)/shard_map/ppermute | solution.py:393
  41.2 2.1 %copy-start.5 = (bf16[320,320]{1,0:T(8,128)(2,1)S(1)}, bf16[320,320]{1,0:T(8,128)(2,1)}, u32[]{:S(2)}) copy-start(bf16[320,320]{1,0:T(8,128)(2,1)} %wo_ref.3) | copy-start | bytes 614404
  45.3 6.1 %collective-permute-start.16 = (bf16[4,32,320]{2,1,0:T(8,128)(2,1)S(1)}, bf16[4,32,320]{2,1,0:T(8,128)(2,1)S(1)}, u32[]{:S(2)}, u32[]{:S(2)}) collective-permute-start(bf16[4,32,320]{2,1,0:T(8,128)(2,1)S(1)} %get-tuple-element.54), channel_id=1, source_target_pairs={{0,2},{2,0},{4,6},{6,4},{8,10},{10,8},{12,14},{14,12},{16,18},{18,... | collective-permute-start | bytes 245768 | tf_op jit(solution)/shard_map/ppermute | solution.py:424
  46.9 6.2 %collective-permute-start.17 = (bf16[4,32,320]{2,1,0:T(8,128)(2,1)S(1)}, bf16[4,32,320]{2,1,0:T(8,128)(2,1)S(1)}, u32[]{:S(2)}, u32[]{:S(2)}) collective-permute-start(bf16[4,32,320]{2,1,0:T(8,128)(2,1)S(1)} %get-tuple-element.55), channel_id=1, source_target_pairs={{0,4},{2,6},{4,0},{6,2},{8,12},{10,14},{12,8},{14,10},{16,20},{18,... | collective-permute-start | bytes 245768 | tf_op jit(solution)/shard_map/ppermute | solution.py:424
  46.9 6.6 %collective-permute-start.18 = (bf16[4,32,320]{2,1,0:T(8,128)(2,1)S(1)}, bf16[4,32,320]{2,1,0:T(8,128)(2,1)S(1)}, u32[]{:S(2)}, u32[]{:S(2)}) collective-permute-start(bf16[4,32,320]{2,1,0:T(8,128)(2,1)S(1)} %get-tuple-element.56), channel_id=1, source_target_pairs={{0,6},{2,4},{4,2},{6,0},{8,14},{10,12},{12,10},{14,8},{16,22},{18,... | collective-permute-start | bytes 245768 | tf_op jit(solution)/shard_map/ppermute | solution.py:424
  50.6 3.9 %collective-permute-start.11 = (bf16[4,32,320]{2,1,0:T(8,128)(2,1)S(1)}, bf16[4,32,320]{2,1,0:T(8,128)(2,1)S(1)}, u32[]{:S(2)}, u32[]{:S(2)}) collective-permute-start(bf16[4,32,320]{2,1,0:T(8,128)(2,1)S(1)} %get-tuple-element.48), channel_id=1, source_target_pairs={{0,2},{2,0},{4,6},{6,4},{8,10},{10,8},{12,14},{14,12},{16,18},{18,... | collective-permute-start | bytes 245768 | tf_op jit(solution)/shard_map/ppermute | solution.py:424
  51.3 4.4 %collective-permute-start.12 = (bf16[4,32,320]{2,1,0:T(8,128)(2,1)S(1)}, bf16[4,32,320]{2,1,0:T(8,128)(2,1)S(1)}, u32[]{:S(2)}, u32[]{:S(2)}) collective-permute-start(bf16[4,32,320]{2,1,0:T(8,128)(2,1)S(1)} %get-tuple-element.49), channel_id=1, source_target_pairs={{0,4},{2,6},{4,0},{6,2},{8,12},{10,14},{12,8},{14,10},{16,20},{18,... | collective-permute-start | bytes 245768 | tf_op jit(solution)/shard_map/ppermute | solution.py:424
  51.3 6.6 %collective-permute-start.13 = (bf16[4,32,320]{2,1,0:T(8,128)(2,1)S(1)}, bf16[4,32,320]{2,1,0:T(8,128)(2,1)S(1)}, u32[]{:S(2)}, u32[]{:S(2)}) collective-permute-start(bf16[4,32,320]{2,1,0:T(8,128)(2,1)S(1)} %get-tuple-element.50), channel_id=1, source_target_pairs={{0,6},{2,4},{4,2},{6,0},{8,14},{10,12},{12,10},{14,8},{16,22},{18,... | collective-permute-start | bytes 245768 | tf_op jit(solution)/shard_map/ppermute | solution.py:424

commit v5 on v4

--- a/solution.py
+++ b/solution.py
@@ -18,6 +18,8 @@
 CELLS = 512
 AXES = ("tm", "height")
 F32 = jnp.float32
+HOME = [0, 2, 3, 1]
+ORDER = [0, 1, 3, 4, 5, 6, 7, 2]
 BF16 = jnp.bfloat16
 
 
@@ -175,7 +177,7 @@
         for b in range(8):
             rows = pl.ds(pl.multiple_of(base + 128 * (b // 4) + 8 * (b % 4), 8), 8)
             pair = [before_ref[rows, :], res_ref[rows, :]]
-            outs[k][b] = jnp.concatenate(pair, axis=0).astype(BF16)
+            outs[ORDER.index(k)][b] = jnp.concatenate(pair, axis=0).astype(BF16)
 
 
 def odd_ring():
@@ -187,7 +189,7 @@
     ring = 2 * lax.rem(lax.axis_index("tm"), 4) + lax.axis_index("height")
     odd = odd_ring()
     for k in range(8):
-        own_ref[lax.bitwise_xor(ring, k)] = pieces[k][...]
+        own_ref[lax.bitwise_xor(ring, ORDER[k])] = pieces[k][...]
     for part in range(2):
         for j in range(4):
             near_refs[part][j] = own_ref[4 * (1 - odd) + j, 4 * part : 4 * part + 4]
@@ -290,7 +292,7 @@
     for k in range(4):
         other = lax.bitwise_xor(quad, k)
         for f in range(4):
-            outs[k][f] = mixed_ref[4 * other + f]
+            outs[HOME.index(k)][f] = mixed_ref[4 * other + f]
 
 
 def home_kernel(part, *refs):
@@ -299,7 +301,7 @@
     copies = []
     for f in range(4):
         for k in range(4):
-            start = pl.multiple_of(32 * lax.bitwise_xor(quad, k), 32)
+            start = pl.multiple_of(32 * lax.bitwise_xor(quad, HOME[k]), 32)
             cells_ref[f, pl.ds(start, 32), :] = pieces[k][f]
         row_ref[f] = cells_ref[f].astype(F32).T.astype(BF16)
         copies.append(pltpu.make_async_copy(row_ref.at[f], out_ref.at[f, part], sems.at[f]))
@@ -375,7 +377,7 @@
         before = pieces
 
     swaps = [[(i, i ^ k) for i in range(2 * size)] for k in range(8)]
-    pieces = [pieces[0]] + [lax.ppermute(pieces[k], AXES, swaps[k]) for k in range(1, 8)]
+    pieces = [pieces[0]] + [lax.ppermute(pieces[k], AXES, swaps[ORDER[k]]) for k in range(1, 8)]
     def array(*shape):
         return jax.ShapeDtypeStruct(shape, BF16)
 
@@ -421,7 +423,7 @@
             cost_estimate=cost(2_000_000_000),
             name="window_attention",
         )(own, query, mine, *halos, gain, w_key, w_value, w_out)
-        back = [pieces[0]] + [lax.ppermute(pieces[k], "tm", swaps[k]) for k in range(1, 4)]
+        back = [pieces[0]] + [lax.ppermute(pieces[k], "tm", swaps[HOME[k]]) for k in range(1, 4)]
         home = pl.pallas_call(
             functools.partial(home_kernel, part),
             out_shape=array(4, 2, C, COLS),

time: 59.2 us -> 57.9 us (0.978)
  waiting for transfers between devices: 10.9 us -> 7.95 us
  starting transfers between devices: 27.6 us -> 29.2 us
    ppermute x13, waiting for transfers between devices: 9.28 us -> 6.33 us  [the longest x6 3.46 us: body(): lax.ppermute(pieces[k], 'tm', swaps[HOME[k]])]
    ppermute x13, starting transfers between devices: 15.1 us -> 16.7 us  [the longest x7 11 us: body(): lax.ppermute(pieces[k], AXES, swaps[ORDER[k]])]
  transfers between devices with their start and end apart: 19 -> 19, of which waited for: 10 -> 8; matrix products, arithmetic and copies ran while one was open for 1% -> 1% of each run, Pallas kernels for 23% -> 23%
where the time goes in v5:
time: 57.9 us; the launch traced here: 57.7 us
  starting transfers between devices  29.2 us (50%)
  Pallas kernels  19.6 us (34%)
  waiting for transfers between devices  7.95 us (14%)
    ppermute x7, starting transfers between devices, body(): lax.ppermute(pieces[k], AXES, swaps[ORDER[k]])  11 us
    pallas_call x2, Pallas kernels, body(): pl.pallas_call(functools.partial(block_kernel, frame), out_shape=piece if...  8.26 us
    ppermute x2, starting transfers between devices, body(): far = [lax.ppermute(x, 'tm', both) for x in halves[2:]]  7.38 us
    ppermute x6, starting transfers between devices, body(): lax.ppermute(pieces[k], 'tm', swaps[HOME[k]])  5.71 us
    pallas_call x2, Pallas kernels, body(): pl.pallas_call(functools.partial(attention_kernel, part), out_shape=[arra...  3.91 us
    ppermute x6, waiting for transfers between devices, body(): lax.ppermute(pieces[k], 'tm', swaps[HOME[k]])  3.46 us
    ppermute x1, starting transfers between devices, body(): got = [lax.ppermute(send, 'height', [(0, 1), (1, 0)])]  2.99 us
    ppermute x7, waiting for transfers between devices, body(): lax.ppermute(pieces[k], AXES, swaps[ORDER[k]])  2.87 us
  transfers between devices with their start and end apart: 19, of which 8 were waited for; matrix products, arithmetic and copies ran while one was open for 1% of the time, Pallas kernels for 23%

profile of v5, /device:TPU:7, one launch (start us, length us, event | category | flops | bytes accessed | tf_op | source)
XLA Modules:
  0.0 57.7 jit_solution(11582849562594870590)
XLA Ops:
  0.0 1.0 %pick.1 = bf16[1,2,320,128]{3,2,1,0:T(8,128)(2,1)S(1)} custom-call(bf16[4,2,320,128]{3,2,1,0:T(8,128)(2,1)} %bitcast.3), custom_call_target="tpu_custom_call" | custom-call | tf_op jit(solution)/shard_map/pick/pallas_call | solution.py:329
  1.0 3.0 %collective-permute-start.1 = (bf16[1,2,320,128]{3,2,1,0:T(8,128)(2,1)S(1)}, bf16[1,2,320,128]{3,2,1,0:T(8,128)(2,1)S(1)}, u32[]{:S(2)}, u32[]{:S(2)}) collective-permute-start(bf16[1,2,320,128]{3,2,1,0:T(8,128)(2,1)S(1)} %pick.1), channel_id=1, source_target_pairs={{0,1},{1,0},{2,3},{3,2},{4,5},{5,4},{6,7},{7,6},{8,9},{9,8},{10,11... | collective-permute-start | bytes 491528 | tf_op jit(solution)/shard_map/ppermute | solution.py:338
  4.0 2.6 %pack_weights.1 = (bf16[1024,960]{1,0:T(8,128)(2,1)S(1)}, bf16[1024,960]{1,0:T(8,128)(2,1)S(1)}, bf16[1,2,320,128]{3,2,1,0:T(8,128)(2,1)S(1)}) custom-call(bf16[3,3,320,320]{3,2,1,0:T(8,128)(2,1)} %first_ref.1, bf16[3,3,320,320]{3,2,1,0:T(8,128)(2,1)} %second_ref.1, bf16[4,2,320,128]{3,2,1,0:T(8,128)(2,1)} %bitcast.4), custom_call_target="tpu_custom_call" | custom-call | flops 1000000000 | tf_op jit(solution)/shard_map/pack_weights/pallas_call | solution.py:339
  6.6 0.2 collective-permute-start
  7.0 0.2 fusion.1.emb_ref
  7.3 0.3 collective-permute-done.1.got_ref
  7.7 4.1 %resblock.2.rest_0_ = f32[512,320]{1,0:T(8,128)S(1)} custom-call(bf16[4,2,320,128]{3,2,1,0:T(8,128)(2,1)S(1)} %bitcast.5, bf16[1,2,320,128]{3,2,1,0:T(8,128)(2,1)S(1)} %collective-permute-done.1.got_ref, bf16[1024,960]{1,0:T(8,128)(2,1)S(1)} %get-tuple-element.32.first_ref, bf16[1024,960]{1,0:T(8,128)(2,1)S(1)} %get-tuple-element.33.second_ref, ...), custom_call_target="tpu_custom_call" | custom-call | flops 4000000000 | tf_op jit(solution)/shard_map/resblock/pallas_call | solution.py:362
  11.8 1.2 %collective-permute-done.got_ref = bf16[1,2,320,128]{3,2,1,0:T(8,128)(2,1)S(1)} collective-permute-done((bf16[1,2,320,128]{3,2,1,0:T(8,128)(2,1)S(1)}, bf16[1,2,320,128]{3,2,1,0:T(8,128)(2,1)S(1)}, u32[]{:S(2)}, u32[]{:S(2)}) %collective-permute-start) | collective-permute-done | bytes 163872 | tf_op jit(solution)/shard_map/ppermute | solution.py:353
  12.9 4.2 %resblock.3 = (bf16[8,16,320]{2,1,0:T(8,128)(2,1)S(1)}, bf16[8,16,320]{2,1,0:T(8,128)(2,1)S(1)}, bf16[8,16,320]{2,1,0:T(8,128)(2,1)S(1)}, bf16[8,16,320]{2,1,0:T...) custom-call(bf16[4,2,320,128]{3,2,1,0:T(8,128)(2,1)S(1)} %bitcast.6,, ...), custom_call_target="tpu_custom_call" | custom-call | flops 4000000000 | tf_op jit(solution)/shard_map/resblock/pallas_call | solution.py:362
  17.1 1.9 %collective-permute-start.2 = (bf16[8,16,320]{2,1,0:T(8,128)(2,1)S(1)}, bf16[8,16,320]{2,1,0:T(8,128)(2,1)S(1)}, u32[]{:S(2)}, u32[]{:S(2)}) collective-permute-start(bf16[8,16,320]{2,1,0:T(8,128)(2,1)S(1)} %get-tuple-element.35), channel_id=1, source_target_pairs={{0,1},{1,0},{2,3},{3,2},{4,5},{5,4},{6,7},{7,6},{8,9},{9,8},{10,11... | collective-permute-start | bytes 245768 | tf_op jit(solution)/shard_map/ppermute | solution.py:380
  19.0 3.2 %collective-permute-start.3 = (bf16[8,16,320]{2,1,0:T(8,128)(2,1)S(1)}, bf16[8,16,320]{2,1,0:T(8,128)(2,1)S(1)}, u32[]{:S(2)}, u32[]{:S(2)}) collective-permute-start(bf16[8,16,320]{2,1,0:T(8,128)(2,1)S(1)} %get-tuple-element.36), channel_id=1, source_target_pairs={{0,3},{1,2},{2,1},{3,0},{4,7},{5,6},{6,5},{7,4},{8,11},{9,10},{10,... | collective-permute-start | bytes 245768 | tf_op jit(solution)/shard_map/ppermute | solution.py:380
  22.2 0.4 collective-permute-start.4
  22.6 2.0 %collective-permute-start.5 = (bf16[8,16,320]{2,1,0:T(8,128)(2,1)S(1)}, bf16[8,16,320]{2,1,0:T(8,128)(2,1)S(1)}, u32[]{:S(2)}, u32[]{:S(2)}) collective-permute-start(bf16[8,16,320]{2,1,0:T(8,128)(2,1)S(1)} %get-tuple-element.38), channel_id=1, source_target_pairs={{0,5},{1,4},{2,7},{3,6},{4,1},{5,0},{6,3},{7,2},{8,13},{9,12},{10,... | collective-permute-start | bytes 245768 | tf_op jit(solution)/shard_map/ppermute | solution.py:380
  24.6 1.8 %collective-permute-start.7 = (bf16[8,16,320]{2,1,0:T(8,128)(2,1)S(1)}, bf16[8,16,320]{2,1,0:T(8,128)(2,1)S(1)}, u32[]{:S(2)}, u32[]{:S(2)}) collective-permute-start(bf16[8,16,320]{2,1,0:T(8,128)(2,1)S(1)} %get-tuple-element.40), channel_id=1, source_target_pairs={{0,7},{1,6},{2,5},{3,4},{4,3},{5,2},{6,1},{7,0},{8,15},{9,14},{10,... | collective-permute-start | bytes 245768 | tf_op jit(solution)/shard_map/ppermute | solution.py:380
  26.4 1.8 %collective-permute-start.8 = (bf16[8,16,320]{2,1,0:T(8,128)(2,1)S(1)}, bf16[8,16,320]{2,1,0:T(8,128)(2,1)S(1)}, u32[]{:S(2)}, u32[]{:S(2)}) collective-permute-start(bf16[8,16,320]{2,1,0:T(8,128)(2,1)S(1)} %get-tuple-element.41), channel_id=1, source_target_pairs={{0,2},{1,3},{2,0},{3,1},{4,6},{5,7},{6,4},{7,5},{8,10},{9,11},{10,... | collective-permute-start | bytes 245768 | tf_op jit(solution)/shard_map/ppermute | solution.py:380
  28.1 0.7 %collective-permute-done.5.refs_4_ = bf16[8,16,320]{2,1,0:T(8,128)(2,1)S(1)} collective-permute-done((bf16[8,16,320]{2,1,0:T(8,128)(2,1)S(1)}, bf16[8,16,320]{2,1,0:T(8,128)(2,1)S(1)}, u32[]{:S(2)}, u32[]{:S(2)}) %collective-permute-start.5) | collective-permute-done | bytes 81952 | tf_op jit(solution)/shard_map/ppermute | solution.py:380
  28.8 1.2 %collective-permute-done.6.refs_5_ = bf16[8,16,320]{2,1,0:T(8,128)(2,1)S(1)} collective-permute-done((bf16[8,16,320]{2,1,0:T(8,128)(2,1)S(1)}, bf16[8,16,320]{2,1,0:T(8,128)(2,1)S(1)}, u32[]{:S(2)}, u32[]{:S(2)}) %collective-permute-start.6) | collective-permute-done | bytes 81952 | tf_op jit(solution)/shard_map/ppermute | solution.py:380
  30.0 1.0 %collective-permute-done.7.refs_6_ = bf16[8,16,320]{2,1,0:T(8,128)(2,1)S(1)} collective-permute-done((bf16[8,16,320]{2,1,0:T(8,128)(2,1)S(1)}, bf16[8,16,320]{2,1,0:T(8,128)(2,1)S(1)}, u32[]{:S(2)}, u32[]{:S(2)}) %collective-permute-start.7) | collective-permute-done | bytes 81952 | tf_op jit(solution)/shard_map/ppermute | solution.py:380
  31.1 1.7 %collective-permute-start.14 = (bf16[4,4,16,320]{3,2,1,0:T(8,128)(2,1)S(1)}, bf16[4,4,16,320]{3,2,1,0:T(8,128)(2,1)S(1)}, u32[]{:S(2)}, u32[]{:S(2)}) collective-permute-start(bf16[4,4,16,320]{3,2,1,0:T(8,128)(2,1)S(1)} %get-tuple-element.51), channel_id=1, source_target_pairs={{0,8},{2,10},{4,12},{6,14},{8,0},{10,2},{12,4},{14,6},{16,24},{18,... | collective-permute-start | bytes 491528 | tf_op jit(solution)/shard_map/ppermute | solution.py:395
  32.8 4.4 %collective-permute-start.15 = (bf16[4,4,16,320]{3,2,1,0:T(8,128)(2,1)S(1)}, bf16[4,4,16,320]{3,2,1,0:T(8,128)(2,1)S(1)}, u32[]{:S(2)}, u32[]{:S(2)}) collective-permute-start(bf16[4,4,16,320]{3,2,1,0:T(8,128)(2,1)S(1)} %get-tuple-element.52), channel_id=1, source_target_pairs={{8,16},{10,18},{12,20},{14,22},{24,32},{26,34},{28,36},{30,38},{40... | collective-permute-start | bytes 491528 | tf_op jit(solution)/shard_map/ppermute | solution.py:394
  37.3 3.0 %collective-permute-start.10 = (bf16[4,4,16,320]{3,2,1,0:T(8,128)(2,1)S(1)}, bf16[4,4,16,320]{3,2,1,0:T(8,128)(2,1)S(1)}, u32[]{:S(2)}, u32[]{:S(2)}) collective-permute-start(bf16[4,4,16,320]{3,2,1,0:T(8,128)(2,1)S(1)} %get-tuple-element.46), channel_id=1, source_target_pairs={{8,16},{10,18},{12,20},{14,22},{24,32},{26,34},{28,36},{30,38},{40... | collective-permute-start | bytes 491528 | tf_op jit(solution)/shard_map/ppermute | solution.py:394
  40.2 0.3 collective-permute-start.9
  40.6 1.9 %own_frames.1 = (bf16[8,128,384]{2,1,0:T(8,128)(2,1)S(1)}, bf16[8,128,768]{2,1,0:T(8,128)(2,1)S(1)}) custom-call(bf16[8,8,16,320]{3,2,1,0:T(8,128)(2,1)S(1)} %get-tuple-element.42.own_ref, f32[1,320]{1,0:T(1,128)S(1)} %reshape.36.gain_ref, bf16[320,320]{1,0:T(8,128)(2,1)S(1)} %copy-done.2, bf16[320,320]{1,0:T(8,128)(2,1)S(1)} %copy-done.3, ...), custom_call_target="tpu_custom_call" | custom-call | flops 2000000000 | tf_op jit(solution)/shard_map/own_frames/pallas_call | solution.py:397
  42.6 2.0 %window_attention.3 = (bf16[4,32,320]{2,1,0:T(8,128)(2,1)S(1)}, bf16[4,32,320]{2,1,0:T(8,128)(2,1)S(1)}, bf16[4,32,320]{2,1,0:T(8,128)(2,1)S(1)}, bf16[4,32,320]{2,1,0:T(8,128)(2,1)S(1)}) custom-call(bf16[8,8,16,320]{3,2,1,0:T(8,128)(2,1)S(1)} %get-tuple-element.42.own_ref, bf16[8,128,384]{2,1,0:T(8,128)(2,1)S(1)} %get-tuple-element.43.q_ref, ...), custom_call_target="tpu_custom_call" | custom-call | flops 2000000000 | tf_op jit(solution)/shard_map/window_attention/pallas_call | solution.py:411
  44.6 0.6 %collective-permute-start.16 = (bf16[4,32,320]{2,1,0:T(8,128)(2,1)S(1)}, bf16[4,32,320]{2,1,0:T(8,128)(2,1)S(1)}, u32[]{:S(2)}, u32[]{:S(2)}) collective-permute-start(bf16[4,32,320]{2,1,0:T(8,128)(2,1)S(1)} %get-tuple-element.54), channel_id=1, source_target_pairs={{0,4},{2,6},{4,0},{6,2},{8,12},{10,14},{12,8},{14,10},{16,20},{18,... | collective-permute-start | bytes 245768 | tf_op jit(solution)/shard_map/ppermute | solution.py:426
  45.2 2.6 %collective-permute-start.17 = (bf16[4,32,320]{2,1,0:T(8,128)(2,1)S(1)}, bf16[4,32,320]{2,1,0:T(8,128)(2,1)S(1)}, u32[]{:S(2)}, u32[]{:S(2)}) collective-permute-start(bf16[4,32,320]{2,1,0:T(8,128)(2,1)S(1)} %get-tuple-element.55), channel_id=1, source_target_pairs={{0,6},{2,4},{4,2},{6,0},{8,14},{10,12},{12,10},{14,8},{16,22},{18,... | collective-permute-start | bytes 245768 | tf_op jit(solution)/shard_map/ppermute | solution.py:426
  47.8 2.0 %window_attention.2 = (bf16[4,32,320]{2,1,0:T(8,128)(2,1)S(1)}, bf16[4,32,320]{2,1,0:T(8,128)(2,1)S(1)}, bf16[4,32,320]{2,1,0:T(8,128)(2,1)S(1)}, bf16[4,32,320]{2,1,0:T(8,128)(2,1)S(1)}) custom-call(bf16[8,8,16,320]{3,2,1,0:T(8,128)(2,1)S(1)} %get-tuple-element.42.own_ref, bf16[8,128,384]{2,1,0:T(8,128)(2,1)S(1)} %get-tuple-element.43.q_ref, ...), custom_call_target="tpu_custom_call" | custom-call | flops 2000000000 | tf_op jit(solution)/shard_map/window_attention/pallas_call | solution.py:411
  49.8 0.6 %collective-permute-start.11 = (bf16[4,32,320]{2,1,0:T(8,128)(2,1)S(1)}, bf16[4,32,320]{2,1,0:T(8,128)(2,1)S(1)}, u32[]{:S(2)}, u32[]{:S(2)}) collective-permute-start(bf16[4,32,320]{2,1,0:T(8,128)(2,1)S(1)} %get-tuple-element.48), channel_id=1, source_target_pairs={{0,4},{2,6},{4,0},{6,2},{8,12},{10,14},{12,8},{14,10},{16,20},{18,... | collective-permute-start | bytes 245768 | tf_op jit(solution)/shard_map/ppermute | solution.py:426
  50.4 1.8 %collective-permute-start.12 = (bf16[4,32,320]{2,1,0:T(8,128)(2,1)S(1)}, bf16[4,32,320]{2,1,0:T(8,128)(2,1)S(1)}, u32[]{:S(2)}, u32[]{:S(2)}) collective-permute-start(bf16[4,32,320]{2,1,0:T(8,128)(2,1)S(1)} %get-tuple-element.49), channel_id=1, source_target_pairs={{0,6},{2,4},{4,2},{6,0},{8,14},{10,12},{12,10},{14,8},{16,22},{18,... | collective-permute-start | bytes 245768 | tf_op jit(solution)/shard_map/ppermute | solution.py:426
  52.3 0.9 %home.2.refs_4_ = bf16[4,2,320,128]{3,2,1,0:T(8,128)(2,1)} custom-call(bf16[4,32,320]{2,1,0:T(8,128)(2,1)S(1)} %get-tuple-element.53.refs_0_, bf16[4,32,320]{2,1,0:T(8,128)(2,1)S(1)} %collective-permute-done.16.refs_1_, bf16[4,32,320]{2,1,0:T(8,128)(2,1)S(1)} %collective-permute-done.17.refs_2_, bf16[4,32,320]{2,1,0:T(8,128)(2,1)S(1)} %collective-permute-done.18.refs_3_), custom_call_target="tpu_custom_call" | custom-call | flops 1000000 | tf_op jit(solution)/shard_map/home/pallas_call | solution.py:427
  53.3 3.3 %collective-permute-done.12.refs_2_ = bf16[4,32,320]{2,1,0:T(8,128)(2,1)S(1)} collective-permute-done((bf16[4,32,320]{2,1,0:T(8,128)(2,1)S(1)}, bf16[4,32,320]{2,1,0:T(8,128)(2,1)S(1)}, u32[]{:S(2)}, u32[]{:S(2)}) %collective-permute-start.12) | collective-permute-done | bytes 81952 | tf_op jit(solution)/shard_map/ppermute | solution.py:426
  56.7 0.9 %home.3 = bf16[4,2,320,128]{3,2,1,0:T(8,128)(2,1)} custom-call(bf16[4,32,320]{2,1,0:T(8,128)(2,1)S(1)} %get-tuple-element.47.refs_0_, bf16[4,32,320]{2,1,0:T(8,128)(2,1)S(1)} %collective-permute-done.11.refs_1_, bf16[4,32,320]{2,1,0:T(8,128)(2,1)S(1)} %collective-permute-done.12.refs_2_, ...), custom_call_target="tpu_custom_call", output_to_operand_aliasing={{}: (4, {})} | custom-call | flops 1000000 | tf_op jit(solution)/shard_map/home/pallas_call | solution.py:427
  (39 shorter events, 0.8 us)
Async XLA Ops:
  0.0 7.0 %copy-start = (bf16[320,320]{1,0:T(8,128)(2,1)S(1)}, bf16[320,320]{1,0:T(8,128)(2,1)}, u32[]{:S(2)}) copy-start(bf16[320,320]{1,0:T(8,128)(2,1)} %param.13) | copy-start | bytes 614404
  1.0 5.8 %copy-start.7 = (s32[4]{0:T(128)S(1)}, s32[4]{0:T(128)}, u32[]{:S(2)}) copy-start(s32[4]{0:T(128)} %param.11) | copy-start | bytes 52
  1.0 6.7 %copy-start.1 = (bf16[4,2,128,320]{2,3,1,0:T(8,128)(2,1)S(1)}, bf16[4,2,128,320]{2,3,1,0:T(8,128)(2,1)}, u32[]{:S(2)}) copy-start(bf16[4,2,128,320]{2,3,1,0:T(8,128)(2,1)} %param.10) | copy-start | bytes 1966084
  1.0 6.7 %collective-permute-start.1 = (bf16[1,2,320,128]{3,2,1,0:T(8,128)(2,1)S(1)}, bf16[1,2,320,128]{3,2,1,0:T(8,128)(2,1)S(1)}, u32[]{:S(2)}, u32[]{:S(2)}) collective-permute-start(bf16[1,2,320,128]{3,2,1,0:T(8,128)(2,1)S(1)} %pick.1), channel_id=1, source_target_pairs={{0,1},{1,0},{2,3},{3,2},{4,5},{5,4},{6,7},{7,6},{8,9},{9,8},{10,11... | collective-permute-start | bytes 491528 | tf_op jit(solution)/shard_map/ppermute | solution.py:338
  6.6 6.3 %collective-permute-start = (bf16[1,2,320,128]{3,2,1,0:T(8,128)(2,1)S(1)}, bf16[1,2,320,128]{3,2,1,0:T(8,128)(2,1)S(1)}, u32[]{:S(2)}, u32[]{:S(2)}) collective-permute-start(bf16[1,2,320,128]{3,2,1,0:T(8,128)(2,1)S(1)} %get-tuple-element.31), channel_id=1, source_target_pairs={{0,1},{1,0},{2,3},{3,2},{4,5},{5,4},{6,7},{7,6},{8,9},{9,8},{10,11... | collective-permute-start | bytes 491528 | tf_op jit(solution)/shard_map/ppermute | solution.py:353
  11.7 16.4 %copy-start.6 = (f32[320]{0:T(512)S(1)}, f32[320]{0:T(512)}, u32[]{:S(2)}) copy-start(f32[320]{0:T(512)} %param.15) | copy-start | bytes 3844
  11.7 28.8 %copy-start.2 = (bf16[320,320]{1,0:T(8,128)(2,1)S(1)}, bf16[320,320]{1,0:T(8,128)(2,1)}, u32[]{:S(2)}) copy-start(bf16[320,320]{1,0:T(8,128)(2,1)} %wq_ref.1) | copy-start | bytes 614404
  11.8 28.8 %copy-start.3 = (bf16[320,320]{1,0:T(8,128)(2,1)S(1)}, bf16[320,320]{1,0:T(8,128)(2,1)}, u32[]{:S(2)}) copy-start(bf16[320,320]{1,0:T(8,128)(2,1)} %wk_ref.5) | copy-start | bytes 614404
  11.8 28.8 %copy-start.4 = (bf16[320,320]{1,0:T(8,128)(2,1)S(1)}, bf16[320,320]{1,0:T(8,128)(2,1)}, u32[]{:S(2)}) copy-start(bf16[320,320]{1,0:T(8,128)(2,1)} %wv_ref.5) | copy-start | bytes 614404
  17.1 7.5 %collective-permute-start.2 = (bf16[8,16,320]{2,1,0:T(8,128)(2,1)S(1)}, bf16[8,16,320]{2,1,0:T(8,128)(2,1)S(1)}, u32[]{:S(2)}, u32[]{:S(2)}) collective-permute-start(bf16[8,16,320]{2,1,0:T(8,128)(2,1)S(1)} %get-tuple-element.35), channel_id=1, source_target_pairs={{0,1},{1,0},{2,3},{3,2},{4,5},{5,4},{6,7},{7,6},{8,9},{9,8},{10,11... | collective-permute-start | bytes 245768 | tf_op jit(solution)/shard_map/ppermute | solution.py:380
  19.0 7.4 %collective-permute-start.3 = (bf16[8,16,320]{2,1,0:T(8,128)(2,1)S(1)}, bf16[8,16,320]{2,1,0:T(8,128)(2,1)S(1)}, u32[]{:S(2)}, u32[]{:S(2)}) collective-permute-start(bf16[8,16,320]{2,1,0:T(8,128)(2,1)S(1)} %get-tuple-element.36), channel_id=1, source_target_pairs={{0,3},{1,2},{2,1},{3,0},{4,7},{5,6},{6,5},{7,4},{8,11},{9,10},{10,... | collective-permute-start | bytes 245768 | tf_op jit(solution)/shard_map/ppermute | solution.py:380
  22.2 5.9 %collective-permute-start.4 = (bf16[8,16,320]{2,1,0:T(8,128)(2,1)S(1)}, bf16[8,16,320]{2,1,0:T(8,128)(2,1)S(1)}, u32[]{:S(2)}, u32[]{:S(2)}) collective-permute-start(bf16[8,16,320]{2,1,0:T(8,128)(2,1)S(1)} %get-tuple-element.37), channel_id=1, source_target_pairs={{0,4},{1,5},{2,6},{3,7},{4,0},{5,1},{6,2},{7,3},{8,12},{9,13},{10,... | collective-permute-start | bytes 245768 | tf_op jit(solution)/shard_map/ppermute | solution.py:380
  22.6 6.2 %collective-permute-start.5 = (bf16[8,16,320]{2,1,0:T(8,128)(2,1)S(1)}, bf16[8,16,320]{2,1,0:T(8,128)(2,1)S(1)}, u32[]{:S(2)}, u32[]{:S(2)}) collective-permute-start(bf16[8,16,320]{2,1,0:T(8,128)(2,1)S(1)} %get-tuple-element.38), channel_id=1, source_target_pairs={{0,5},{1,4},{2,7},{3,6},{4,1},{5,0},{6,3},{7,2},{8,13},{9,12},{10,... | collective-permute-start | bytes 245768 | tf_op jit(solution)/shard_map/ppermute | solution.py:380
  24.6 5.4 %collective-permute-start.6 = (bf16[8,16,320]{2,1,0:T(8,128)(2,1)S(1)}, bf16[8,16,320]{2,1,0:T(8,128)(2,1)S(1)}, u32[]{:S(2)}, u32[]{:S(2)}) collective-permute-start(bf16[8,16,320]{2,1,0:T(8,128)(2,1)S(1)} %get-tuple-element.39), channel_id=1, source_target_pairs={{0,6},{1,7},{2,4},{3,5},{4,2},{5,3},{6,0},{7,1},{8,14},{9,15},{10,... | collective-permute-start | bytes 245768 | tf_op jit(solution)/shard_map/ppermute | solution.py:380
  24.6 6.4 %collective-permute-start.7 = (bf16[8,16,320]{2,1,0:T(8,128)(2,1)S(1)}, bf16[8,16,320]{2,1,0:T(8,128)(2,1)S(1)}, u32[]{:S(2)}, u32[]{:S(2)}) collective-permute-start(bf16[8,16,320]{2,1,0:T(8,128)(2,1)S(1)} %get-tuple-element.40), channel_id=1, source_target_pairs={{0,7},{1,6},{2,5},{3,4},{4,3},{5,2},{6,1},{7,0},{8,15},{9,14},{10,... | collective-permute-start | bytes 245768 | tf_op jit(solution)/shard_map/ppermute | solution.py:380
  26.4 4.6 %collective-permute-start.8 = (bf16[8,16,320]{2,1,0:T(8,128)(2,1)S(1)}, bf16[8,16,320]{2,1,0:T(8,128)(2,1)S(1)}, u32[]{:S(2)}, u32[]{:S(2)}) collective-permute-start(bf16[8,16,320]{2,1,0:T(8,128)(2,1)S(1)} %get-tuple-element.41), channel_id=1, source_target_pairs={{0,2},{1,3},{2,0},{3,1},{4,6},{5,7},{6,4},{7,5},{8,10},{9,11},{10,... | collective-permute-start | bytes 245768 | tf_op jit(solution)/shard_map/ppermute | solution.py:380
  31.1 11.3 %collective-permute-start.14 = (bf16[4,4,16,320]{3,2,1,0:T(8,128)(2,1)S(1)}, bf16[4,4,16,320]{3,2,1,0:T(8,128)(2,1)S(1)}, u32[]{:S(2)}, u32[]{:S(2)}) collective-permute-start(bf16[4,4,16,320]{3,2,1,0:T(8,128)(2,1)S(1)} %get-tuple-element.51), channel_id=1, source_target_pairs={{0,8},{2,10},{4,12},{6,14},{8,0},{10,2},{12,4},{14,6},{16,24},{18,... | collective-permute-start | bytes 491528 | tf_op jit(solution)/shard_map/ppermute | solution.py:395
  32.8 9.8 %collective-permute-start.15 = (bf16[4,4,16,320]{3,2,1,0:T(8,128)(2,1)S(1)}, bf16[4,4,16,320]{3,2,1,0:T(8,128)(2,1)S(1)}, u32[]{:S(2)}, u32[]{:S(2)}) collective-permute-start(bf16[4,4,16,320]{3,2,1,0:T(8,128)(2,1)S(1)} %get-tuple-element.52), channel_id=1, source_target_pairs={{8,16},{10,18},{12,20},{14,22},{24,32},{26,34},{28,36},{30,38},{40... | collective-permute-start | bytes 491528 | tf_op jit(solution)/shard_map/ppermute | solution.py:394
  37.3 10.6 %collective-permute-start.10 = (bf16[4,4,16,320]{3,2,1,0:T(8,128)(2,1)S(1)}, bf16[4,4,16,320]{3,2,1,0:T(8,128)(2,1)S(1)}, u32[]{:S(2)}, u32[]{:S(2)}) collective-permute-start(bf16[4,4,16,320]{3,2,1,0:T(8,128)(2,1)S(1)} %get-tuple-element.46), channel_id=1, source_target_pairs={{8,16},{10,18},{12,20},{14,22},{24,32},{26,34},{28,36},{30,38},{40... | collective-permute-start | bytes 491528 | tf_op jit(solution)/shard_map/ppermute | solution.py:394
  40.2 7.6 %collective-permute-start.9 = (bf16[4,4,16,320]{3,2,1,0:T(8,128)(2,1)S(1)}, bf16[4,4,16,320]{3,2,1,0:T(8,128)(2,1)S(1)}, u32[]{:S(2)}, u32[]{:S(2)}) collective-permute-start(bf16[4,4,16,320]{3,2,1,0:T(8,128)(2,1)S(1)} %get-tuple-element.45), channel_id=1, source_target_pairs={{0,8},{2,10},{4,12},{6,14},{8,0},{10,2},{12,4},{14,6},{16,24},{18,... | collective-permute-start | bytes 491528 | tf_op jit(solution)/shard_map/ppermute | solution.py:395
  40.5 2.1 %copy-start.5 = (bf16[320,320]{1,0:T(8,128)(2,1)S(1)}, bf16[320,320]{1,0:T(8,128)(2,1)}, u32[]{:S(2)}) copy-start(bf16[320,320]{1,0:T(8,128)(2,1)} %wo_ref.3) | copy-start | bytes 614404
  44.6 7.7 %collective-permute-start.16 = (bf16[4,32,320]{2,1,0:T(8,128)(2,1)S(1)}, bf16[4,32,320]{2,1,0:T(8,128)(2,1)S(1)}, u32[]{:S(2)}, u32[]{:S(2)}) collective-permute-start(bf16[4,32,320]{2,1,0:T(8,128)(2,1)S(1)} %get-tuple-element.54), channel_id=1, source_target_pairs={{0,4},{2,6},{4,0},{6,2},{8,12},{10,14},{12,8},{14,10},{16,20},{18,... | collective-permute-start | bytes 245768 | tf_op jit(solution)/shard_map/ppermute | solution.py:426
  45.2 7.1 %collective-permute-start.17 = (bf16[4,32,320]{2,1,0:T(8,128)(2,1)S(1)}, bf16[4,32,320]{2,1,0:T(8,128)(2,1)S(1)}, u32[]{:S(2)}, u32[]{:S(2)}) collective-permute-start(bf16[4,32,320]{2,1,0:T(8,128)(2,1)S(1)} %get-tuple-element.55), channel_id=1, source_target_pairs={{0,6},{2,4},{4,2},{6,0},{8,14},{10,12},{12,10},{14,8},{16,22},{18,... | collective-permute-start | bytes 245768 | tf_op jit(solution)/shard_map/ppermute | solution.py:426
  47.8 4.4 %collective-permute-start.18 = (bf16[4,32,320]{2,1,0:T(8,128)(2,1)S(1)}, bf16[4,32,320]{2,1,0:T(8,128)(2,1)S(1)}, u32[]{:S(2)}, u32[]{:S(2)}) collective-permute-start(bf16[4,32,320]{2,1,0:T(8,128)(2,1)S(1)} %get-tuple-element.56), channel_id=1, source_target_pairs={{0,2},{2,0},{4,6},{6,4},{8,10},{10,8},{12,14},{14,12},{16,18},{18,... | collective-permute-start | bytes 245768 | tf_op jit(solution)/shard_map/ppermute | solution.py:426
  49.8 3.5 %collective-permute-start.11 = (bf16[4,32,320]{2,1,0:T(8,128)(2,1)S(1)}, bf16[4,32,320]{2,1,0:T(8,128)(2,1)S(1)}, u32[]{:S(2)}, u32[]{:S(2)}) collective-permute-start(bf16[4,32,320]{2,1,0:T(8,128)(2,1)S(1)} %get-tuple-element.48), channel_id=1, source_target_pairs={{0,4},{2,6},{4,0},{6,2},{8,12},{10,14},{12,8},{14,10},{16,20},{18,... | collective-permute-start | bytes 245768 | tf_op jit(solution)/shard_map/ppermute | solution.py:426
  50.4 6.2 %collective-permute-start.12 = (bf16[4,32,320]{2,1,0:T(8,128)(2,1)S(1)}, bf16[4,32,320]{2,1,0:T(8,128)(2,1)S(1)}, u32[]{:S(2)}, u32[]{:S(2)}) collective-permute-start(bf16[4,32,320]{2,1,0:T(8,128)(2,1)S(1)} %get-tuple-element.49), channel_id=1, source_target_pairs={{0,6},{2,4},{4,2},{6,0},{8,14},{10,12},{12,10},{14,8},{16,22},{18,... | collective-permute-start | bytes 245768 | tf_op jit(solution)/shard_map/ppermute | solution.py:426
  52.2 4.4 %collective-permute-start.13 = (bf16[4,32,320]{2,1,0:T(8,128)(2,1)S(1)}, bf16[4,32,320]{2,1,0:T(8,128)(2,1)S(1)}, u32[]{:S(2)}, u32[]{:S(2)}) collective-permute-start(bf16[4,32,320]{2,1,0:T(8,128)(2,1)S(1)} %get-tuple-element.50), channel_id=1, source_target_pairs={{0,2},{2,0},{4,6},{6,4},{8,10},{10,8},{12,14},{14,12},{16,18},{18,... | collective-permute-start | bytes 245768 | tf_op jit(solution)/shard_map/ppermute | solution.py:426

commit v6 on v5

--- a/solution.py
+++ b/solution.py
@@ -154,7 +154,7 @@
     for row in range(2):
         for side, raw in ((here, own_ref[2 * here + frame, row]), (1 - here, got_ref[0, row])):
             start = pl.multiple_of((2 * side + row) * COLS, COLS)
-            x_ref[pl.ds(start, COLS), :] = raw.astype(F32).T
+            x_ref[pl.ds(start, COLS), :] = raw.T.astype(F32)
 
     def hidden():
         return x_ref[:, :MAIN], x_ref[:, MAIN:]
@@ -204,7 +204,7 @@
     return (centred * lax.rsqrt(var + 1e-05) * gain).astype(BF16)
 
 
-def keys_values(blocks, gain_ref, wk_ref, wv_ref, norm_ref, kv_ref):
+def keys_values(blocks, gain_ref, wkv_ref, norm_ref, kv_ref):
     gain = gain_ref[...]
     rows = blocks[0].shape[0]
     for b, value in enumerate(blocks):
@@ -212,36 +212,12 @@
     each = len(blocks) if rows * len(blocks) <= 512 else 512 // rows
     for b in range(0, len(blocks), each):
         normed = norm_ref[b * rows : (b + each) * rows, :]
-        for low, ref in ((0, wk_ref), (384, wv_ref)):
-            value = dot32(normed, ref[...]).astype(BF16).reshape(each, rows, C)
-            kv_ref[b : b + each, :, low : low + C] = value
-            pad = jnp.zeros((each, rows, TAIL), BF16)
-            kv_ref[b : b + each, :, low + C : low + 384] = pad
-
-
-def own_kernel(own_ref, gain_ref, wq_ref, wk_ref, wv_ref, q_ref, kv_ref, norm_ref):
-    blocks = [own_ref[:, b].reshape(128, C) for b in range(8)]
-    keys_values(blocks, gain_ref, wk_ref, wv_ref, norm_ref, kv_ref)
-    for b in range(0, 8, 4):
-        value = dot32(norm_ref[128 * b : 128 * b + 512, :], wq_ref[...]) * 0.125
-        q_ref[b : b + 4, :, :C] = value.astype(BF16).reshape(4, 128, C)
-        q_ref[b : b + 4, :, C:] = jnp.zeros((4, 128, TAIL), BF16)
-
-
-def attention_kernel(
-    part, own_ref, q_ref, mine_ref, one_ref, two_ref, gain_ref, wk_ref, wv_ref, wo_ref, *rest
-):
-    near_ref, far_ref = one_ref, two_ref
-    outs, (norm_ref, kv_ref, att_ref, mixed_ref) = rest[:4], rest[4:]
-    tm = lax.axis_index("tm")
-    quad = lax.rem(tm, 4)
-    base = lax.div(tm, 4) * 16
+        kv_ref[b : b + each] = dot32(normed, wkv_ref[...]).astype(BF16).reshape(each, rows, 768)
+
+
+def window_bias():
+    base = lax.div(lax.axis_index("tm"), 4) * 16
     odd = odd_ring()
-    blocks = [
-        jnp.concatenate([r[:, b].reshape(64, C) for r in (near_ref, far_ref)], axis=0)
-        for b in range(4)
-    ]
-    keys_values(blocks, gain_ref, wk_ref, wv_ref, norm_ref, kv_ref)
     row = lax.broadcasted_iota(jnp.int32, (128, 256), 0)
     col = lax.broadcasted_iota(jnp.int32, (128, 256), 1)
     near_at, far_at = 16 - 24 * odd, 24 * odd - 16
@@ -249,7 +225,36 @@
     away = key - row // 8
     keep = (row % 8 == col % 8) & (away >= -(WINDOW // 2)) & (away < WINDOW // 2)
     keep = keep & (base + key >= 0) & (base + key < 4 * lax.axis_size("tm"))
-    bias = jnp.where(keep, 0.0, -1e30).astype(F32)
+    return jnp.where(keep, 0.0, -1e30).astype(F32)
+
+
+def own_kernel(
+    own_ref, gain_ref, wq_ref, wk_ref, wv_ref, q_ref, kv_ref, wkv_ref, bias_ref, norm_ref
+):
+    for low, ref in ((0, wk_ref), (384, wv_ref)):
+        wkv_ref[:, low : low + C] = ref[...]
+        wkv_ref[:, low + C : low + 384] = jnp.zeros((C, TAIL), BF16)
+    bias_ref[...] = window_bias()
+    blocks = [own_ref[:, b].reshape(128, C) for b in range(8)]
+    keys_values(blocks, gain_ref, wkv_ref, norm_ref, kv_ref)
+    for b in range(0, 8, 4):
+        value = dot32(norm_ref[128 * b : 128 * b + 512, :], wq_ref[...]) * 0.125
+        q_ref[b : b + 4, :, :C] = value.astype(BF16).reshape(4, 128, C)
+        q_ref[b : b + 4, :, C:] = jnp.zeros((4, 128, TAIL), BF16)
+
+
+def attention_kernel(
+    part, own_ref, q_ref, mine_ref, one_ref, two_ref, gain_ref, wkv_ref, wo_ref, bias_ref, *rest
+):
+    near_ref, far_ref = one_ref, two_ref
+    outs, (norm_ref, kv_ref, att_ref, mixed_ref) = rest[:4], rest[4:]
+    quad = lax.rem(lax.axis_index("tm"), 4)
+    blocks = [
+        jnp.concatenate([r[:, b].reshape(64, C) for r in (near_ref, far_ref)], axis=0)
+        for b in range(4)
+    ]
+    keys_values(blocks, gain_ref, wkv_ref, norm_ref, kv_ref)
+    bias = bias_ref[...]
     bias2 = jnp.concatenate([bias, bias], axis=0)
     ones = jnp.ones((256, 128), BF16)
     lane = lax.broadcasted_iota(jnp.int32, (128, 128), 1)
@@ -259,8 +264,8 @@
         sides = [kv_ref[b], mine_ref[full]]
         return jnp.concatenate([x[:, low : low + 128] for x in sides], axis=0)
 
-    for first in range(0, 4, 2):
-        items = [(b, 128 * pair) for b in (first, first + 1) for pair in range(3)]
+    for first in range(1):
+        items = [(b, 128 * pair) for b in range(4) for pair in range(3)]
         probs = []
         for b, low in items:
             q = q_ref[4 * part + b, :, low : low + 128]
@@ -303,7 +308,7 @@
         for k in range(4):
             start = pl.multiple_of(32 * lax.bitwise_xor(quad, HOME[k]), 32)
             cells_ref[f, pl.ds(start, 32), :] = pieces[k][f]
-        row_ref[f] = cells_ref[f].astype(F32).T.astype(BF16)
+        row_ref[f] = cells_ref[f].T
         copies.append(pltpu.make_async_copy(row_ref.at[f], out_ref.at[f, part], sems.at[f]))
         copies[-1].start()
     for copy in copies:
@@ -394,11 +399,16 @@
     far = [lax.ppermute(x, "tm", both) for x in halves[2:]]
     near = [lax.ppermute(x, "tm", [(i, i ^ 4) for i in range(size)]) for x in halves[:2]]
     gain = ln_gain.reshape(1, C)
-    query, mine = pl.pallas_call(
+    query, mine, w_both, bias = pl.pallas_call(
         own_kernel,
-        out_shape=[array(8, 128, 384), array(8, 128, 768)],
+        out_shape=[
+            array(8, 128, 384),
+            array(8, 128, 768),
+            array(C, 768),
+            jax.ShapeDtypeStruct((128, 256), F32),
+        ],
         in_specs=vmem(5),
-        out_specs=vmem(2),
+        out_specs=vmem(4),
         scratch_shapes=[pltpu.VMEM((1024, C), BF16)],
         compiler_params=params,
         cost_estimate=cost(2_000_000_000),
@@ -422,7 +432,7 @@
             compiler_params=params,
             cost_estimate=cost(2_000_000_000),
             name="window_attention",
-        )(own, query, mine, *halos, gain, w_key, w_value, w_out)
+        )(own, query, mine, *halos, gain, w_both, w_out, bias)
         back = [pieces[0]] + [lax.ppermute(pieces[k], "tm", swaps[HOME[k]]) for k in range(1, 4)]
         home = pl.pallas_call(
             functools.partial(home_kernel, part),

time: 57.9 us -> 57.8 us (level)
  no operation moved by 1% of the time
where the time goes in v6:
time: 57.8 us; the launch traced here: 57.6 us
  starting transfers between devices  29.2 us (51%)
  Pallas kernels  19.3 us (33%)
  waiting for transfers between devices  8.24 us (14%)
    ppermute x7, starting transfers between devices, body(): lax.ppermute(pieces[k], AXES, swaps[ORDER[k]])  10.9 us
    pallas_call x2, Pallas kernels, body(): pl.pallas_call(functools.partial(block_kernel, frame), out_shape=piece if...  8.12 us
    ppermute x2, starting transfers between devices, body(): far = [lax.ppermute(x, 'tm', both) for x in halves[2:]]  7.38 us
    ppermute x6, starting transfers between devices, body(): lax.ppermute(pieces[k], 'tm', swaps[HOME[k]])  5.77 us
    pallas_call x2, Pallas kernels, body(): pl.pallas_call(functools.partial(attention_kernel, part), out_shape=[arra...  3.78 us
    ppermute x6, waiting for transfers between devices, body(): lax.ppermute(pieces[k], 'tm', swaps[HOME[k]])  3.48 us
    ppermute x7, waiting for transfers between devices, body(): lax.ppermute(pieces[k], AXES, swaps[ORDER[k]])  3 us
    ppermute x1, starting transfers between devices, body(): got = [lax.ppermute(send, 'height', [(0, 1), (1, 0)])]  2.99 us
  transfers between devices with their start and end apart: 19, of which 8 were waited for; matrix products, arithmetic and copies ran while one was open for 1% of the time, Pallas kernels for 23%

profile of v6, /device:TPU:7, one launch (start us, length us, event | category | flops | bytes accessed | tf_op | source)
XLA Modules:
  0.0 57.6 jit_solution(2385840166416679835)
XLA Ops:
  0.0 1.0 %pick.1 = bf16[1,2,320,128]{3,2,1,0:T(8,128)(2,1)S(1)} custom-call(bf16[4,2,320,128]{3,2,1,0:T(8,128)(2,1)} %bitcast.3), custom_call_target="tpu_custom_call" | custom-call | tf_op jit(solution)/shard_map/pick/pallas_call | solution.py:334
  1.0 3.0 %collective-permute-start.1 = (bf16[1,2,320,128]{3,2,1,0:T(8,128)(2,1)S(1)}, bf16[1,2,320,128]{3,2,1,0:T(8,128)(2,1)S(1)}, u32[]{:S(2)}, u32[]{:S(2)}) collective-permute-start(bf16[1,2,320,128]{3,2,1,0:T(8,128)(2,1)S(1)} %pick.1), channel_id=1, source_target_pairs={{0,1},{1,0},{2,3},{3,2},{4,5},{5,4},{6,7},{7,6},{8,9},{9,8},{10,11... | collective-permute-start | bytes 491528 | tf_op jit(solution)/shard_map/ppermute | solution.py:343
  4.0 2.6 %pack_weights.1 = (bf16[1024,960]{1,0:T(8,128)(2,1)S(1)}, bf16[1024,960]{1,0:T(8,128)(2,1)S(1)}, bf16[1,2,320,128]{3,2,1,0:T(8,128)(2,1)S(1)}) custom-call(bf16[3,3,320,320]{3,2,1,0:T(8,128)(2,1)} %first_ref.1, bf16[3,3,320,320]{3,2,1,0:T(8,128)(2,1)} %second_ref.1, bf16[4,2,320,128]{3,2,1,0:T(8,128)(2,1)} %bitcast.4), custom_call_target="tpu_custom_call" | custom-call | flops 1000000000 | tf_op jit(solution)/shard_map/pack_weights/pallas_call | solution.py:344
  6.6 0.2 collective-permute-start
  7.0 0.2 fusion.1.emb_ref
  7.3 0.3 collective-permute-done.1.got_ref
  7.7 4.0 %resblock.2.rest_0_ = f32[512,320]{1,0:T(8,128)S(1)} custom-call(bf16[4,2,320,128]{3,2,1,0:T(8,128)(2,1)S(1)} %bitcast.5, bf16[1,2,320,128]{3,2,1,0:T(8,128)(2,1)S(1)} %collective-permute-done.1.got_ref, bf16[1024,960]{1,0:T(8,128)(2,1)S(1)} %get-tuple-element.34.first_ref, bf16[1024,960]{1,0:T(8,128)(2,1)S(1)} %get-tuple-element.35.second_ref, ...), custom_call_target="tpu_custom_call" | custom-call | flops 4000000000 | tf_op jit(solution)/shard_map/resblock/pallas_call | solution.py:367
  11.7 1.2 %collective-permute-done.got_ref = bf16[1,2,320,128]{3,2,1,0:T(8,128)(2,1)S(1)} collective-permute-done((bf16[1,2,320,128]{3,2,1,0:T(8,128)(2,1)S(1)}, bf16[1,2,320,128]{3,2,1,0:T(8,128)(2,1)S(1)}, u32[]{:S(2)}, u32[]{:S(2)}) %collective-permute-start) | collective-permute-done | bytes 163872 | tf_op jit(solution)/shard_map/ppermute | solution.py:358
  12.9 4.1 %resblock.3 = (bf16[8,16,320]{2,1,0:T(8,128)(2,1)S(1)}, bf16[8,16,320]{2,1,0:T(8,128)(2,1)S(1)}, bf16[8,16,320]{2,1,0:T(8,128)(2,1)S(1)}, bf16[8,16,320]{2,1,0:T...) custom-call(bf16[4,2,320,128]{3,2,1,0:T(8,128)(2,1)S(1)} %bitcast.6,, ...), custom_call_target="tpu_custom_call" | custom-call | flops 4000000000 | tf_op jit(solution)/shard_map/resblock/pallas_call | solution.py:367
  17.1 1.8 %collective-permute-start.2 = (bf16[8,16,320]{2,1,0:T(8,128)(2,1)S(1)}, bf16[8,16,320]{2,1,0:T(8,128)(2,1)S(1)}, u32[]{:S(2)}, u32[]{:S(2)}) collective-permute-start(bf16[8,16,320]{2,1,0:T(8,128)(2,1)S(1)} %get-tuple-element.37), channel_id=1, source_target_pairs={{0,1},{1,0},{2,3},{3,2},{4,5},{5,4},{6,7},{7,6},{8,9},{9,8},{10,11... | collective-permute-start | bytes 245768 | tf_op jit(solution)/shard_map/ppermute | solution.py:385
  18.8 3.3 %collective-permute-start.3 = (bf16[8,16,320]{2,1,0:T(8,128)(2,1)S(1)}, bf16[8,16,320]{2,1,0:T(8,128)(2,1)S(1)}, u32[]{:S(2)}, u32[]{:S(2)}) collective-permute-start(bf16[8,16,320]{2,1,0:T(8,128)(2,1)S(1)} %get-tuple-element.38), channel_id=1, source_target_pairs={{0,3},{1,2},{2,1},{3,0},{4,7},{5,6},{6,5},{7,4},{8,11},{9,10},{10,... | collective-permute-start | bytes 245768 | tf_op jit(solution)/shard_map/ppermute | solution.py:385
  22.1 0.4 collective-permute-start.4
  22.5 1.9 %collective-permute-start.5 = (bf16[8,16,320]{2,1,0:T(8,128)(2,1)S(1)}, bf16[8,16,320]{2,1,0:T(8,128)(2,1)S(1)}, u32[]{:S(2)}, u32[]{:S(2)}) collective-permute-start(bf16[8,16,320]{2,1,0:T(8,128)(2,1)S(1)} %get-tuple-element.40), channel_id=1, source_target_pairs={{0,5},{1,4},{2,7},{3,6},{4,1},{5,0},{6,3},{7,2},{8,13},{9,12},{10,... | collective-permute-start | bytes 245768 | tf_op jit(solution)/shard_map/ppermute | solution.py:385
  24.4 1.8 %collective-permute-start.7 = (bf16[8,16,320]{2,1,0:T(8,128)(2,1)S(1)}, bf16[8,16,320]{2,1,0:T(8,128)(2,1)S(1)}, u32[]{:S(2)}, u32[]{:S(2)}) collective-permute-start(bf16[8,16,320]{2,1,0:T(8,128)(2,1)S(1)} %get-tuple-element.42), channel_id=1, source_target_pairs={{0,7},{1,6},{2,5},{3,4},{4,3},{5,2},{6,1},{7,0},{8,15},{9,14},{10,... | collective-permute-start | bytes 245768 | tf_op jit(solution)/shard_map/ppermute | solution.py:385
  26.2 1.7 %collective-permute-start.8 = (bf16[8,16,320]{2,1,0:T(8,128)(2,1)S(1)}, bf16[8,16,320]{2,1,0:T(8,128)(2,1)S(1)}, u32[]{:S(2)}, u32[]{:S(2)}) collective-permute-start(bf16[8,16,320]{2,1,0:T(8,128)(2,1)S(1)} %get-tuple-element.43), channel_id=1, source_target_pairs={{0,2},{1,3},{2,0},{3,1},{4,6},{5,7},{6,4},{7,5},{8,10},{9,11},{10,... | collective-permute-start | bytes 245768 | tf_op jit(solution)/shard_map/ppermute | solution.py:385
  28.0 0.8 %collective-permute-done.5.refs_4_ = bf16[8,16,320]{2,1,0:T(8,128)(2,1)S(1)} collective-permute-done((bf16[8,16,320]{2,1,0:T(8,128)(2,1)S(1)}, bf16[8,16,320]{2,1,0:T(8,128)(2,1)S(1)}, u32[]{:S(2)}, u32[]{:S(2)}) %collective-permute-start.5) | collective-permute-done | bytes 81952 | tf_op jit(solution)/shard_map/ppermute | solution.py:385
  28.8 1.1 %collective-permute-done.6.refs_5_ = bf16[8,16,320]{2,1,0:T(8,128)(2,1)S(1)} collective-permute-done((bf16[8,16,320]{2,1,0:T(8,128)(2,1)S(1)}, bf16[8,16,320]{2,1,0:T(8,128)(2,1)S(1)}, u32[]{:S(2)}, u32[]{:S(2)}) %collective-permute-start.6) | collective-permute-done | bytes 81952 | tf_op jit(solution)/shard_map/ppermute | solution.py:385
  29.9 1.1 %collective-permute-done.7.refs_6_ = bf16[8,16,320]{2,1,0:T(8,128)(2,1)S(1)} collective-permute-done((bf16[8,16,320]{2,1,0:T(8,128)(2,1)S(1)}, bf16[8,16,320]{2,1,0:T(8,128)(2,1)S(1)}, u32[]{:S(2)}, u32[]{:S(2)}) %collective-permute-start.7) | collective-permute-done | bytes 81952 | tf_op jit(solution)/shard_map/ppermute | solution.py:385
  31.1 1.7 %collective-permute-start.14 = (bf16[4,4,16,320]{3,2,1,0:T(8,128)(2,1)S(1)}, bf16[4,4,16,320]{3,2,1,0:T(8,128)(2,1)S(1)}, u32[]{:S(2)}, u32[]{:S(2)}) collective-permute-start(bf16[4,4,16,320]{3,2,1,0:T(8,128)(2,1)S(1)} %get-tuple-element.55), channel_id=1, source_target_pairs={{0,8},{2,10},{4,12},{6,14},{8,0},{10,2},{12,4},{14,6},{16,24},{18,... | collective-permute-start | bytes 491528 | tf_op jit(solution)/shard_map/ppermute | solution.py:400
  32.8 4.4 %collective-permute-start.15 = (bf16[4,4,16,320]{3,2,1,0:T(8,128)(2,1)S(1)}, bf16[4,4,16,320]{3,2,1,0:T(8,128)(2,1)S(1)}, u32[]{:S(2)}, u32[]{:S(2)}) collective-permute-start(bf16[4,4,16,320]{3,2,1,0:T(8,128)(2,1)S(1)} %get-tuple-element.56), channel_id=1, source_target_pairs={{8,16},{10,18},{12,20},{14,22},{24,32},{26,34},{28,36},{30,38},{40... | collective-permute-start | bytes 491528 | tf_op jit(solution)/shard_map/ppermute | solution.py:399
  37.2 3.0 %collective-permute-start.10 = (bf16[4,4,16,320]{3,2,1,0:T(8,128)(2,1)S(1)}, bf16[4,4,16,320]{3,2,1,0:T(8,128)(2,1)S(1)}, u32[]{:S(2)}, u32[]{:S(2)}) collective-permute-start(bf16[4,4,16,320]{3,2,1,0:T(8,128)(2,1)S(1)} %get-tuple-element.48), channel_id=1, source_target_pairs={{8,16},{10,18},{12,20},{14,22},{24,32},{26,34},{28,36},{30,38},{40... | collective-permute-start | bytes 491528 | tf_op jit(solution)/shard_map/ppermute | solution.py:399
  40.2 0.3 collective-permute-start.9
  40.5 1.9 %own_frames.1 = (bf16[8,128,384]{2,1,0:T(8,128)(2,1)S(1)}, bf16[8,128,768]{2,1,0:T(8,128)(2,1)S(1)}, bf16[320,768]{1,0:T(8,128)(2,1)S(1)}, f32[128,256]{1,0:T(8,128)S(1)}) custom-call(bf16[8,8,16,320]{3,2,1,0:T(8,128)(2,1)S(1)} %get-tuple-element.44.own_ref, f32[1,320]{1,0:T(1,128)S(1)} %reshape.36.gain_ref, bf16[320,320]{1,0:T(8,128)(2,1)S(1)} %copy-done.2, ...), custom_call_target="tpu_custom_call" | custom-call | flops 2000000000 | tf_op jit(solution)/shard_map/own_frames/pallas_call | solution.py:402
  42.6 1.9 %window_attention.3 = (bf16[4,32,320]{2,1,0:T(8,128)(2,1)S(1)}, bf16[4,32,320]{2,1,0:T(8,128)(2,1)S(1)}, bf16[4,32,320]{2,1,0:T(8,128)(2,1)S(1)}, bf16[4,32,320]{2,1,0:T(8,128)(2,1)S(1)}) custom-call(bf16[8,8,16,320]{3,2,1,0:T(8,128)(2,1)S(1)} %get-tuple-element.44.own_ref, bf16[8,128,384]{2,1,0:T(8,128)(2,1)S(1)} %get-tuple-element.45.q_ref, ...), custom_call_target="tpu_custom_call" | custom-call | flops 2000000000 | tf_op jit(solution)/shard_map/window_attention/pallas_call | solution.py:421
  44.5 0.6 collective-permute-start.16
  45.1 2.7 %collective-permute-start.17 = (bf16[4,32,320]{2,1,0:T(8,128)(2,1)S(1)}, bf16[4,32,320]{2,1,0:T(8,128)(2,1)S(1)}, u32[]{:S(2)}, u32[]{:S(2)}) collective-permute-start(bf16[4,32,320]{2,1,0:T(8,128)(2,1)S(1)} %get-tuple-element.59), channel_id=1, source_target_pairs={{0,6},{2,4},{4,2},{6,0},{8,14},{10,12},{12,10},{14,8},{16,22},{18,... | collective-permute-start | bytes 245768 | tf_op jit(solution)/shard_map/ppermute | solution.py:436
  47.8 1.9 %window_attention.2 = (bf16[4,32,320]{2,1,0:T(8,128)(2,1)S(1)}, bf16[4,32,320]{2,1,0:T(8,128)(2,1)S(1)}, bf16[4,32,320]{2,1,0:T(8,128)(2,1)S(1)}, bf16[4,32,320]{2,1,0:T(8,128)(2,1)S(1)}) custom-call(bf16[8,8,16,320]{3,2,1,0:T(8,128)(2,1)S(1)} %get-tuple-element.44.own_ref, bf16[8,128,384]{2,1,0:T(8,128)(2,1)S(1)} %get-tuple-element.45.q_ref, ...), custom_call_target="tpu_custom_call" | custom-call | flops 2000000000 | tf_op jit(solution)/shard_map/window_attention/pallas_call | solution.py:421
  49.7 0.6 collective-permute-start.11
  50.2 1.9 %collective-permute-start.12 = (bf16[4,32,320]{2,1,0:T(8,128)(2,1)S(1)}, bf16[4,32,320]{2,1,0:T(8,128)(2,1)S(1)}, u32[]{:S(2)}, u32[]{:S(2)}) collective-permute-start(bf16[4,32,320]{2,1,0:T(8,128)(2,1)S(1)} %get-tuple-element.53), channel_id=1, source_target_pairs={{0,6},{2,4},{4,2},{6,0},{8,14},{10,12},{12,10},{14,8},{16,22},{18,... | collective-permute-start | bytes 245768 | tf_op jit(solution)/shard_map/ppermute | solution.py:436
  52.2 0.9 %home.2.refs_4_ = bf16[4,2,320,128]{3,2,1,0:T(8,128)(2,1)} custom-call(bf16[4,32,320]{2,1,0:T(8,128)(2,1)S(1)} %get-tuple-element.57.refs_0_, bf16[4,32,320]{2,1,0:T(8,128)(2,1)S(1)} %collective-permute-done.16.refs_1_, bf16[4,32,320]{2,1,0:T(8,128)(2,1)S(1)} %collective-permute-done.17.refs_2_, bf16[4,32,320]{2,1,0:T(8,128)(2,1)S(1)} %collective-permute-done.18.refs_3_), custom_call_target="tpu_custom_call" | custom-call | flops 1000000 | tf_op jit(solution)/shard_map/home/pallas_call | solution.py:437
  53.2 3.4 %collective-permute-done.12.refs_2_ = bf16[4,32,320]{2,1,0:T(8,128)(2,1)S(1)} collective-permute-done((bf16[4,32,320]{2,1,0:T(8,128)(2,1)S(1)}, bf16[4,32,320]{2,1,0:T(8,128)(2,1)S(1)}, u32[]{:S(2)}, u32[]{:S(2)}) %collective-permute-start.12) | collective-permute-done | bytes 81952 | tf_op jit(solution)/shard_map/ppermute | solution.py:436
  56.6 0.9 %home.3 = bf16[4,2,320,128]{3,2,1,0:T(8,128)(2,1)} custom-call(bf16[4,32,320]{2,1,0:T(8,128)(2,1)S(1)} %get-tuple-element.51.refs_0_, bf16[4,32,320]{2,1,0:T(8,128)(2,1)S(1)} %collective-permute-done.11.refs_1_, bf16[4,32,320]{2,1,0:T(8,128)(2,1)S(1)} %collective-permute-done.12.refs_2_, ...), custom_call_target="tpu_custom_call", output_to_operand_aliasing={{}: (4, {})} | custom-call | flops 1000000 | tf_op jit(solution)/shard_map/home/pallas_call | solution.py:437
  (39 shorter events, 0.8 us)
Async XLA Ops:
  0.0 7.0 %copy-start = (bf16[320,320]{1,0:T(8,128)(2,1)S(1)}, bf16[320,320]{1,0:T(8,128)(2,1)}, u32[]{:S(2)}) copy-start(bf16[320,320]{1,0:T(8,128)(2,1)} %param.13) | copy-start | bytes 614404
  1.0 5.8 %copy-start.7 = (s32[4]{0:T(128)S(1)}, s32[4]{0:T(128)}, u32[]{:S(2)}) copy-start(s32[4]{0:T(128)} %param.11) | copy-start | bytes 52
  1.0 6.7 %copy-start.1 = (bf16[4,2,128,320]{2,3,1,0:T(8,128)(2,1)S(1)}, bf16[4,2,128,320]{2,3,1,0:T(8,128)(2,1)}, u32[]{:S(2)}) copy-start(bf16[4,2,128,320]{2,3,1,0:T(8,128)(2,1)} %param.10) | copy-start | bytes 1966084
  1.0 6.7 %collective-permute-start.1 = (bf16[1,2,320,128]{3,2,1,0:T(8,128)(2,1)S(1)}, bf16[1,2,320,128]{3,2,1,0:T(8,128)(2,1)S(1)}, u32[]{:S(2)}, u32[]{:S(2)}) collective-permute-start(bf16[1,2,320,128]{3,2,1,0:T(8,128)(2,1)S(1)} %pick.1), channel_id=1, source_target_pairs={{0,1},{1,0},{2,3},{3,2},{4,5},{5,4},{6,7},{7,6},{8,9},{9,8},{10,11... | collective-permute-start | bytes 491528 | tf_op jit(solution)/shard_map/ppermute | solution.py:343
  6.6 6.3 %collective-permute-start = (bf16[1,2,320,128]{3,2,1,0:T(8,128)(2,1)S(1)}, bf16[1,2,320,128]{3,2,1,0:T(8,128)(2,1)S(1)}, u32[]{:S(2)}, u32[]{:S(2)}) collective-permute-start(bf16[1,2,320,128]{3,2,1,0:T(8,128)(2,1)S(1)} %get-tuple-element.33), channel_id=1, source_target_pairs={{0,1},{1,0},{2,3},{3,2},{4,5},{5,4},{6,7},{7,6},{8,9},{9,8},{10,11... | collective-permute-start | bytes 491528 | tf_op jit(solution)/shard_map/ppermute | solution.py:358
  11.7 16.3 %copy-start.6 = (f32[320]{0:T(512)S(1)}, f32[320]{0:T(512)}, u32[]{:S(2)}) copy-start(f32[320]{0:T(512)} %param.15) | copy-start | bytes 3844
  11.7 28.8 %copy-start.2 = (bf16[320,320]{1,0:T(8,128)(2,1)S(1)}, bf16[320,320]{1,0:T(8,128)(2,1)}, u32[]{:S(2)}) copy-start(bf16[320,320]{1,0:T(8,128)(2,1)} %wq_ref.1) | copy-start | bytes 614404
  11.7 28.8 %copy-start.3 = (bf16[320,320]{1,0:T(8,128)(2,1)S(1)}, bf16[320,320]{1,0:T(8,128)(2,1)}, u32[]{:S(2)}) copy-start(bf16[320,320]{1,0:T(8,128)(2,1)} %wk_ref.1) | copy-start | bytes 614404
  11.7 28.8 %copy-start.4 = (bf16[320,320]{1,0:T(8,128)(2,1)S(1)}, bf16[320,320]{1,0:T(8,128)(2,1)}, u32[]{:S(2)}) copy-start(bf16[320,320]{1,0:T(8,128)(2,1)} %wv_ref.1) | copy-start | bytes 614404
  17.1 7.4 %collective-permute-start.2 = (bf16[8,16,320]{2,1,0:T(8,128)(2,1)S(1)}, bf16[8,16,320]{2,1,0:T(8,128)(2,1)S(1)}, u32[]{:S(2)}, u32[]{:S(2)}) collective-permute-start(bf16[8,16,320]{2,1,0:T(8,128)(2,1)S(1)} %get-tuple-element.37), channel_id=1, source_target_pairs={{0,1},{1,0},{2,3},{3,2},{4,5},{5,4},{6,7},{7,6},{8,9},{9,8},{10,11... | collective-permute-start | bytes 245768 | tf_op jit(solution)/shard_map/ppermute | solution.py:385
  18.8 7.4 %collective-permute-start.3 = (bf16[8,16,320]{2,1,0:T(8,128)(2,1)S(1)}, bf16[8,16,320]{2,1,0:T(8,128)(2,1)S(1)}, u32[]{:S(2)}, u32[]{:S(2)}) collective-permute-start(bf16[8,16,320]{2,1,0:T(8,128)(2,1)S(1)} %get-tuple-element.38), channel_id=1, source_target_pairs={{0,3},{1,2},{2,1},{3,0},{4,7},{5,6},{6,5},{7,4},{8,11},{9,10},{10,... | collective-permute-start | bytes 245768 | tf_op jit(solution)/shard_map/ppermute | solution.py:385
  22.1 5.8 %collective-permute-start.4 = (bf16[8,16,320]{2,1,0:T(8,128)(2,1)S(1)}, bf16[8,16,320]{2,1,0:T(8,128)(2,1)S(1)}, u32[]{:S(2)}, u32[]{:S(2)}) collective-permute-start(bf16[8,16,320]{2,1,0:T(8,128)(2,1)S(1)} %get-tuple-element.39), channel_id=1, source_target_pairs={{0,4},{1,5},{2,6},{3,7},{4,0},{5,1},{6,2},{7,3},{8,12},{9,13},{10,... | collective-permute-start | bytes 245768 | tf_op jit(solution)/shard_map/ppermute | solution.py:385
  22.5 6.2 %collective-permute-start.5 = (bf16[8,16,320]{2,1,0:T(8,128)(2,1)S(1)}, bf16[8,16,320]{2,1,0:T(8,128)(2,1)S(1)}, u32[]{:S(2)}, u32[]{:S(2)}) collective-permute-start(bf16[8,16,320]{2,1,0:T(8,128)(2,1)S(1)} %get-tuple-element.40), channel_id=1, source_target_pairs={{0,5},{1,4},{2,7},{3,6},{4,1},{5,0},{6,3},{7,2},{8,13},{9,12},{10,... | collective-permute-start | bytes 245768 | tf_op jit(solution)/shard_map/ppermute | solution.py:385
  24.4 5.4 %collective-permute-start.6 = (bf16[8,16,320]{2,1,0:T(8,128)(2,1)S(1)}, bf16[8,16,320]{2,1,0:T(8,128)(2,1)S(1)}, u32[]{:S(2)}, u32[]{:S(2)}) collective-permute-start(bf16[8,16,320]{2,1,0:T(8,128)(2,1)S(1)} %get-tuple-element.41), channel_id=1, source_target_pairs={{0,6},{1,7},{2,4},{3,5},{4,2},{5,3},{6,0},{7,1},{8,14},{9,15},{10,... | collective-permute-start | bytes 245768 | tf_op jit(solution)/shard_map/ppermute | solution.py:385
  24.4 6.5 %collective-permute-start.7 = (bf16[8,16,320]{2,1,0:T(8,128)(2,1)S(1)}, bf16[8,16,320]{2,1,0:T(8,128)(2,1)S(1)}, u32[]{:S(2)}, u32[]{:S(2)}) collective-permute-start(bf16[8,16,320]{2,1,0:T(8,128)(2,1)S(1)} %get-tuple-element.42), channel_id=1, source_target_pairs={{0,7},{1,6},{2,5},{3,4},{4,3},{5,2},{6,1},{7,0},{8,15},{9,14},{10,... | collective-permute-start | bytes 245768 | tf_op jit(solution)/shard_map/ppermute | solution.py:385
  26.2 4.8 %collective-permute-start.8 = (bf16[8,16,320]{2,1,0:T(8,128)(2,1)S(1)}, bf16[8,16,320]{2,1,0:T(8,128)(2,1)S(1)}, u32[]{:S(2)}, u32[]{:S(2)}) collective-permute-start(bf16[8,16,320]{2,1,0:T(8,128)(2,1)S(1)} %get-tuple-element.43), channel_id=1, source_target_pairs={{0,2},{1,3},{2,0},{3,1},{4,6},{5,7},{6,4},{7,5},{8,10},{9,11},{10,... | collective-permute-start | bytes 245768 | tf_op jit(solution)/shard_map/ppermute | solution.py:385
  31.1 11.3 %collective-permute-start.14 = (bf16[4,4,16,320]{3,2,1,0:T(8,128)(2,1)S(1)}, bf16[4,4,16,320]{3,2,1,0:T(8,128)(2,1)S(1)}, u32[]{:S(2)}, u32[]{:S(2)}) collective-permute-start(bf16[4,4,16,320]{3,2,1,0:T(8,128)(2,1)S(1)} %get-tuple-element.55), channel_id=1, source_target_pairs={{0,8},{2,10},{4,12},{6,14},{8,0},{10,2},{12,4},{14,6},{16,24},{18,... | collective-permute-start | bytes 491528 | tf_op jit(solution)/shard_map/ppermute | solution.py:400
  32.8 9.8 %collective-permute-start.15 = (bf16[4,4,16,320]{3,2,1,0:T(8,128)(2,1)S(1)}, bf16[4,4,16,320]{3,2,1,0:T(8,128)(2,1)S(1)}, u32[]{:S(2)}, u32[]{:S(2)}) collective-permute-start(bf16[4,4,16,320]{3,2,1,0:T(8,128)(2,1)S(1)} %get-tuple-element.56), channel_id=1, source_target_pairs={{8,16},{10,18},{12,20},{14,22},{24,32},{26,34},{28,36},{30,38},{40... | collective-permute-start | bytes 491528 | tf_op jit(solution)/shard_map/ppermute | solution.py:399
  37.2 10.5 %collective-permute-start.10 = (bf16[4,4,16,320]{3,2,1,0:T(8,128)(2,1)S(1)}, bf16[4,4,16,320]{3,2,1,0:T(8,128)(2,1)S(1)}, u32[]{:S(2)}, u32[]{:S(2)}) collective-permute-start(bf16[4,4,16,320]{3,2,1,0:T(8,128)(2,1)S(1)} %get-tuple-element.48), channel_id=1, source_target_pairs={{8,16},{10,18},{12,20},{14,22},{24,32},{26,34},{28,36},{30,38},{40... | collective-permute-start | bytes 491528 | tf_op jit(solution)/shard_map/ppermute | solution.py:399
  40.2 7.5 %collective-permute-start.9 = (bf16[4,4,16,320]{3,2,1,0:T(8,128)(2,1)S(1)}, bf16[4,4,16,320]{3,2,1,0:T(8,128)(2,1)S(1)}, u32[]{:S(2)}, u32[]{:S(2)}) collective-permute-start(bf16[4,4,16,320]{3,2,1,0:T(8,128)(2,1)S(1)} %get-tuple-element.47), channel_id=1, source_target_pairs={{0,8},{2,10},{4,12},{6,14},{8,0},{10,2},{12,4},{14,6},{16,24},{18,... | collective-permute-start | bytes 491528 | tf_op jit(solution)/shard_map/ppermute | solution.py:400
  40.5 2.1 %copy-start.5 = (bf16[320,320]{1,0:T(8,128)(2,1)S(1)}, bf16[320,320]{1,0:T(8,128)(2,1)}, u32[]{:S(2)}) copy-start(bf16[320,320]{1,0:T(8,128)(2,1)} %wo_ref.3) | copy-start | bytes 614404
  44.5 7.7 %collective-permute-start.16 = (bf16[4,32,320]{2,1,0:T(8,128)(2,1)S(1)}, bf16[4,32,320]{2,1,0:T(8,128)(2,1)S(1)}, u32[]{:S(2)}, u32[]{:S(2)}) collective-permute-start(bf16[4,32,320]{2,1,0:T(8,128)(2,1)S(1)} %get-tuple-element.58), channel_id=1, source_target_pairs={{0,4},{2,6},{4,0},{6,2},{8,12},{10,14},{12,8},{14,10},{16,20},{18,... | collective-permute-start | bytes 245768 | tf_op jit(solution)/shard_map/ppermute | solution.py:436
  45.1 7.1 %collective-permute-start.17 = (bf16[4,32,320]{2,1,0:T(8,128)(2,1)S(1)}, bf16[4,32,320]{2,1,0:T(8,128)(2,1)S(1)}, u32[]{:S(2)}, u32[]{:S(2)}) collective-permute-start(bf16[4,32,320]{2,1,0:T(8,128)(2,1)S(1)} %get-tuple-element.59), channel_id=1, source_target_pairs={{0,6},{2,4},{4,2},{6,0},{8,14},{10,12},{12,10},{14,8},{16,22},{18,... | collective-permute-start | bytes 245768 | tf_op jit(solution)/shard_map/ppermute | solution.py:436
  47.8 4.4 %collective-permute-start.18 = (bf16[4,32,320]{2,1,0:T(8,128)(2,1)S(1)}, bf16[4,32,320]{2,1,0:T(8,128)(2,1)S(1)}, u32[]{:S(2)}, u32[]{:S(2)}) collective-permute-start(bf16[4,32,320]{2,1,0:T(8,128)(2,1)S(1)} %get-tuple-element.60), channel_id=1, source_target_pairs={{0,2},{2,0},{4,6},{6,4},{8,10},{10,8},{12,14},{14,12},{16,18},{18,... | collective-permute-start | bytes 245768 | tf_op jit(solution)/shard_map/ppermute | solution.py:436
  49.7 3.5 %collective-permute-start.11 = (bf16[4,32,320]{2,1,0:T(8,128)(2,1)S(1)}, bf16[4,32,320]{2,1,0:T(8,128)(2,1)S(1)}, u32[]{:S(2)}, u32[]{:S(2)}) collective-permute-start(bf16[4,32,320]{2,1,0:T(8,128)(2,1)S(1)} %get-tuple-element.52), channel_id=1, source_target_pairs={{0,4},{2,6},{4,0},{6,2},{8,12},{10,14},{12,8},{14,10},{16,20},{18,... | collective-permute-start | bytes 245768 | tf_op jit(solution)/shard_map/ppermute | solution.py:436
  50.2 6.3 %collective-permute-start.12 = (bf16[4,32,320]{2,1,0:T(8,128)(2,1)S(1)}, bf16[4,32,320]{2,1,0:T(8,128)(2,1)S(1)}, u32[]{:S(2)}, u32[]{:S(2)}) collective-permute-start(bf16[4,32,320]{2,1,0:T(8,128)(2,1)S(1)} %get-tuple-element.53), channel_id=1, source_target_pairs={{0,6},{2,4},{4,2},{6,0},{8,14},{10,12},{12,10},{14,8},{16,22},{18,... | collective-permute-start | bytes 245768 | tf_op jit(solution)/shard_map/ppermute | solution.py:436
  52.2 4.4 %collective-permute-start.13 = (bf16[4,32,320]{2,1,0:T(8,128)(2,1)S(1)}, bf16[4,32,320]{2,1,0:T(8,128)(2,1)S(1)}, u32[]{:S(2)}, u32[]{:S(2)}) collective-permute-start(bf16[4,32,320]{2,1,0:T(8,128)(2,1)S(1)} %get-tuple-element.54), channel_id=1, source_target_pairs={{0,2},{2,0},{4,6},{6,4},{8,10},{10,8},{12,14},{14,12},{16,18},{18,... | collective-permute-start | bytes 245768 | tf_op jit(solution)/shard_map/ppermute | solution.py:436

commit v7 on v6

--- a/solution.py
+++ b/solution.py
@@ -19,7 +19,7 @@
 AXES = ("tm", "height")
 F32 = jnp.float32
 HOME = [0, 2, 3, 1]
-ORDER = [0, 1, 3, 4, 5, 6, 7, 2]
+ORDER = [0, 3, 1, 4, 5, 6, 7, 2]
 BF16 = jnp.bfloat16
 
 

time: 57.8 us -> 57.2 us (0.990)
  starting transfers between devices: 29.2 us -> 27.9 us
  waiting for transfers between devices: 8.24 us -> 8.89 us
    ppermute x7, starting transfers between devices: 10.9 us -> 9.36 us  [body(): lax.ppermute(pieces[k], AXES, swaps[ORDER[k]])]
    ppermute x7, waiting for transfers between devices: 3 us -> 3.81 us  [body(): lax.ppermute(pieces[k], AXES, swaps[ORDER[k]])]
  transfers between devices with their start and end apart: 19 -> 19, of which waited for: 8 -> 10; matrix products, arithmetic and copies ran while one was open for 1% -> 1% of each run, Pallas kernels for 23% -> 23%
where the time goes in v7:
time: 57.2 us; the launch traced here: 56.9 us
  starting transfers between devices  27.9 us (49%)
  Pallas kernels  19.3 us (34%)
  waiting for transfers between devices  8.89 us (16%)
    ppermute x7, starting transfers between devices, body(): lax.ppermute(pieces[k], AXES, swaps[ORDER[k]])  9.36 us
    pallas_call x2, Pallas kernels, body(): pl.pallas_call(functools.partial(block_kernel, frame), out_shape=piece if...  8.12 us
    ppermute x2, starting transfers between devices, body(): far = [lax.ppermute(x, 'tm', both) for x in halves[2:]]  7.38 us
    ppermute x6, starting transfers between devices, body(): lax.ppermute(pieces[k], 'tm', swaps[HOME[k]])  5.92 us
    ppermute x7, waiting for transfers between devices, body(): lax.ppermute(pieces[k], AXES, swaps[ORDER[k]])  3.81 us
    pallas_call x2, Pallas kernels, body(): pl.pallas_call(functools.partial(attention_kernel, part), out_shape=[arra...  3.78 us
    ppermute x6, waiting for transfers between devices, body(): lax.ppermute(pieces[k], 'tm', swaps[HOME[k]])  3.5 us
    ppermute x1, starting transfers between devices, body(): got = [lax.ppermute(send, 'height', [(0, 1), (1, 0)])]  2.99 us
  transfers between devices with their start and end apart: 19, of which 10 were waited for; matrix products, arithmetic and copies ran while one was open for 1% of the time, Pallas kernels for 23%

profile of v7, /device:TPU:7, one launch (start us, length us, event | category | flops | bytes accessed | tf_op | source)
XLA Modules:
  0.0 56.9 jit_solution(5417253245193107136)
XLA Ops:
  0.0 1.0 %pick.1 = bf16[1,2,320,128]{3,2,1,0:T(8,128)(2,1)S(1)} custom-call(bf16[4,2,320,128]{3,2,1,0:T(8,128)(2,1)} %bitcast.3), custom_call_target="tpu_custom_call" | custom-call | tf_op jit(solution)/shard_map/pick/pallas_call | solution.py:334
  1.0 3.0 %collective-permute-start.1 = (bf16[1,2,320,128]{3,2,1,0:T(8,128)(2,1)S(1)}, bf16[1,2,320,128]{3,2,1,0:T(8,128)(2,1)S(1)}, u32[]{:S(2)}, u32[]{:S(2)}) collective-permute-start(bf16[1,2,320,128]{3,2,1,0:T(8,128)(2,1)S(1)} %pick.1), channel_id=1, source_target_pairs={{0,1},{1,0},{2,3},{3,2},{4,5},{5,4},{6,7},{7,6},{8,9},{9,8},{10,11... | collective-permute-start | bytes 491528 | tf_op jit(solution)/shard_map/ppermute | solution.py:343
  4.0 2.6 %pack_weights.1 = (bf16[1024,960]{1,0:T(8,128)(2,1)S(1)}, bf16[1024,960]{1,0:T(8,128)(2,1)S(1)}, bf16[1,2,320,128]{3,2,1,0:T(8,128)(2,1)S(1)}) custom-call(bf16[3,3,320,320]{3,2,1,0:T(8,128)(2,1)} %first_ref.1, bf16[3,3,320,320]{3,2,1,0:T(8,128)(2,1)} %second_ref.1, bf16[4,2,320,128]{3,2,1,0:T(8,128)(2,1)} %bitcast.4), custom_call_target="tpu_custom_call" | custom-call | flops 1000000000 | tf_op jit(solution)/shard_map/pack_weights/pallas_call | solution.py:344
  7.0 0.2 fusion.1.emb_ref
  7.3 0.3 collective-permute-done.1.got_ref
  7.7 4.0 %resblock.2.rest_0_ = f32[512,320]{1,0:T(8,128)S(1)} custom-call(bf16[4,2,320,128]{3,2,1,0:T(8,128)(2,1)S(1)} %bitcast.5, bf16[1,2,320,128]{3,2,1,0:T(8,128)(2,1)S(1)} %collective-permute-done.1.got_ref, bf16[1024,960]{1,0:T(8,128)(2,1)S(1)} %get-tuple-element.34.first_ref, bf16[1024,960]{1,0:T(8,128)(2,1)S(1)} %get-tuple-element.35.second_ref, ...), custom_call_target="tpu_custom_call" | custom-call | flops 4000000000 | tf_op jit(solution)/shard_map/resblock/pallas_call | solution.py:367
  11.7 1.2 %collective-permute-done.got_ref = bf16[1,2,320,128]{3,2,1,0:T(8,128)(2,1)S(1)} collective-permute-done((bf16[1,2,320,128]{3,2,1,0:T(8,128)(2,1)S(1)}, bf16[1,2,320,128]{3,2,1,0:T(8,128)(2,1)S(1)}, u32[]{:S(2)}, u32[]{:S(2)}) %collective-permute-start) | collective-permute-done | bytes 163872 | tf_op jit(solution)/shard_map/ppermute | solution.py:358
  12.9 4.1 %resblock.3 = (bf16[8,16,320]{2,1,0:T(8,128)(2,1)S(1)}, bf16[8,16,320]{2,1,0:T(8,128)(2,1)S(1)}, bf16[8,16,320]{2,1,0:T(8,128)(2,1)S(1)}, bf16[8,16,320]{2,1,0:T...) custom-call(bf16[4,2,320,128]{3,2,1,0:T(8,128)(2,1)S(1)} %bitcast.6,, ...), custom_call_target="tpu_custom_call" | custom-call | flops 4000000000 | tf_op jit(solution)/shard_map/resblock/pallas_call | solution.py:367
  17.1 3.9 %collective-permute-start.2 = (bf16[8,16,320]{2,1,0:T(8,128)(2,1)S(1)}, bf16[8,16,320]{2,1,0:T(8,128)(2,1)S(1)}, u32[]{:S(2)}, u32[]{:S(2)}) collective-permute-start(bf16[8,16,320]{2,1,0:T(8,128)(2,1)S(1)} %get-tuple-element.37), channel_id=1, source_target_pairs={{0,3},{1,2},{2,1},{3,0},{4,7},{5,6},{6,5},{7,4},{8,11},{9,10},{10,... | collective-permute-start | bytes 245768 | tf_op jit(solution)/shard_map/ppermute | solution.py:385
  20.9 0.9 %collective-permute-start.3 = (bf16[8,16,320]{2,1,0:T(8,128)(2,1)S(1)}, bf16[8,16,320]{2,1,0:T(8,128)(2,1)S(1)}, u32[]{:S(2)}, u32[]{:S(2)}) collective-permute-start(bf16[8,16,320]{2,1,0:T(8,128)(2,1)S(1)} %get-tuple-element.38), channel_id=1, source_target_pairs={{0,1},{1,0},{2,3},{3,2},{4,5},{5,4},{6,7},{7,6},{8,9},{9,8},{10,11... | collective-permute-start | bytes 245768 | tf_op jit(solution)/shard_map/ppermute | solution.py:385
  21.9 0.4 collective-permute-start.4
  22.2 1.9 %collective-permute-start.5 = (bf16[8,16,320]{2,1,0:T(8,128)(2,1)S(1)}, bf16[8,16,320]{2,1,0:T(8,128)(2,1)S(1)}, u32[]{:S(2)}, u32[]{:S(2)}) collective-permute-start(bf16[8,16,320]{2,1,0:T(8,128)(2,1)S(1)} %get-tuple-element.40), channel_id=1, source_target_pairs={{0,5},{1,4},{2,7},{3,6},{4,1},{5,0},{6,3},{7,2},{8,13},{9,12},{10,... | collective-permute-start | bytes 245768 | tf_op jit(solution)/shard_map/ppermute | solution.py:385
  24.2 2.2 %collective-permute-start.7 = (bf16[8,16,320]{2,1,0:T(8,128)(2,1)S(1)}, bf16[8,16,320]{2,1,0:T(8,128)(2,1)S(1)}, u32[]{:S(2)}, u32[]{:S(2)}) collective-permute-start(bf16[8,16,320]{2,1,0:T(8,128)(2,1)S(1)} %get-tuple-element.42), channel_id=1, source_target_pairs={{0,7},{1,6},{2,5},{3,4},{4,3},{5,2},{6,1},{7,0},{8,15},{9,14},{10,... | collective-permute-start | bytes 245768 | tf_op jit(solution)/shard_map/ppermute | solution.py:385
  26.4 0.5 collective-permute-done.3.refs_2_
  27.0 0.4 collective-permute-done.4.refs_3_
  27.4 1.4 %collective-permute-done.5.refs_4_ = bf16[8,16,320]{2,1,0:T(8,128)(2,1)S(1)} collective-permute-done((bf16[8,16,320]{2,1,0:T(8,128)(2,1)S(1)}, bf16[8,16,320]{2,1,0:T(8,128)(2,1)S(1)}, u32[]{:S(2)}, u32[]{:S(2)}) %collective-permute-start.5) | collective-permute-done | bytes 81952 | tf_op jit(solution)/shard_map/ppermute | solution.py:385
  28.7 0.7 %collective-permute-done.6.refs_5_ = bf16[8,16,320]{2,1,0:T(8,128)(2,1)S(1)} collective-permute-done((bf16[8,16,320]{2,1,0:T(8,128)(2,1)S(1)}, bf16[8,16,320]{2,1,0:T(8,128)(2,1)S(1)}, u32[]{:S(2)}, u32[]{:S(2)}) %collective-permute-start.6) | collective-permute-done | bytes 81952 | tf_op jit(solution)/shard_map/ppermute | solution.py:385
  29.5 0.8 %collective-permute-done.7.refs_6_ = bf16[8,16,320]{2,1,0:T(8,128)(2,1)S(1)} collective-permute-done((bf16[8,16,320]{2,1,0:T(8,128)(2,1)S(1)}, bf16[8,16,320]{2,1,0:T(8,128)(2,1)S(1)}, u32[]{:S(2)}, u32[]{:S(2)}) %collective-permute-start.7) | collective-permute-done | bytes 81952 | tf_op jit(solution)/shard_map/ppermute | solution.py:385
  30.4 1.8 %collective-permute-start.14 = (bf16[4,4,16,320]{3,2,1,0:T(8,128)(2,1)S(1)}, bf16[4,4,16,320]{3,2,1,0:T(8,128)(2,1)S(1)}, u32[]{:S(2)}, u32[]{:S(2)}) collective-permute-start(bf16[4,4,16,320]{3,2,1,0:T(8,128)(2,1)S(1)} %get-tuple-element.55), channel_id=1, source_target_pairs={{0,8},{2,10},{4,12},{6,14},{8,0},{10,2},{12,4},{14,6},{16,24},{18,... | collective-permute-start | bytes 491528 | tf_op jit(solution)/shard_map/ppermute | solution.py:400
  32.1 4.4 %collective-permute-start.15 = (bf16[4,4,16,320]{3,2,1,0:T(8,128)(2,1)S(1)}, bf16[4,4,16,320]{3,2,1,0:T(8,128)(2,1)S(1)}, u32[]{:S(2)}, u32[]{:S(2)}) collective-permute-start(bf16[4,4,16,320]{3,2,1,0:T(8,128)(2,1)S(1)} %get-tuple-element.56), channel_id=1, source_target_pairs={{8,16},{10,18},{12,20},{14,22},{24,32},{26,34},{28,36},{30,38},{40... | collective-permute-start | bytes 491528 | tf_op jit(solution)/shard_map/ppermute | solution.py:399
  36.6 3.0 %collective-permute-start.10 = (bf16[4,4,16,320]{3,2,1,0:T(8,128)(2,1)S(1)}, bf16[4,4,16,320]{3,2,1,0:T(8,128)(2,1)S(1)}, u32[]{:S(2)}, u32[]{:S(2)}) collective-permute-start(bf16[4,4,16,320]{3,2,1,0:T(8,128)(2,1)S(1)} %get-tuple-element.48), channel_id=1, source_target_pairs={{8,16},{10,18},{12,20},{14,22},{24,32},{26,34},{28,36},{30,38},{40... | collective-permute-start | bytes 491528 | tf_op jit(solution)/shard_map/ppermute | solution.py:399
  39.5 0.3 collective-permute-start.9
  39.9 1.9 %own_frames.1 = (bf16[8,128,384]{2,1,0:T(8,128)(2,1)S(1)}, bf16[8,128,768]{2,1,0:T(8,128)(2,1)S(1)}, bf16[320,768]{1,0:T(8,128)(2,1)S(1)}, f32[128,256]{1,0:T(8,128)S(1)}) custom-call(bf16[8,8,16,320]{3,2,1,0:T(8,128)(2,1)S(1)} %get-tuple-element.44.own_ref, f32[1,320]{1,0:T(1,128)S(1)} %reshape.36.gain_ref, bf16[320,320]{1,0:T(8,128)(2,1)S(1)} %copy-done.2, ...), custom_call_target="tpu_custom_call" | custom-call | flops 2000000000 | tf_op jit(solution)/shard_map/own_frames/pallas_call | solution.py:402
  41.8 1.9 %window_attention.3 = (bf16[4,32,320]{2,1,0:T(8,128)(2,1)S(1)}, bf16[4,32,320]{2,1,0:T(8,128)(2,1)S(1)}, bf16[4,32,320]{2,1,0:T(8,128)(2,1)S(1)}, bf16[4,32,320]{2,1,0:T(8,128)(2,1)S(1)}) custom-call(bf16[8,8,16,320]{3,2,1,0:T(8,128)(2,1)S(1)} %get-tuple-element.44.own_ref, bf16[8,128,384]{2,1,0:T(8,128)(2,1)S(1)} %get-tuple-element.45.q_ref, ...), custom_call_target="tpu_custom_call" | custom-call | flops 2000000000 | tf_op jit(solution)/shard_map/window_attention/pallas_call | solution.py:421
  43.7 0.7 %collective-permute-start.16 = (bf16[4,32,320]{2,1,0:T(8,128)(2,1)S(1)}, bf16[4,32,320]{2,1,0:T(8,128)(2,1)S(1)}, u32[]{:S(2)}, u32[]{:S(2)}) collective-permute-start(bf16[4,32,320]{2,1,0:T(8,128)(2,1)S(1)} %get-tuple-element.58), channel_id=1, source_target_pairs={{0,4},{2,6},{4,0},{6,2},{8,12},{10,14},{12,8},{14,10},{16,20},{18,... | collective-permute-start | bytes 245768 | tf_op jit(solution)/shard_map/ppermute | solution.py:436
  44.3 2.9 %collective-permute-start.17 = (bf16[4,32,320]{2,1,0:T(8,128)(2,1)S(1)}, bf16[4,32,320]{2,1,0:T(8,128)(2,1)S(1)}, u32[]{:S(2)}, u32[]{:S(2)}) collective-permute-start(bf16[4,32,320]{2,1,0:T(8,128)(2,1)S(1)} %get-tuple-element.59), channel_id=1, source_target_pairs={{0,6},{2,4},{4,2},{6,0},{8,14},{10,12},{12,10},{14,8},{16,22},{18,... | collective-permute-start | bytes 245768 | tf_op jit(solution)/shard_map/ppermute | solution.py:436
  47.2 1.9 %window_attention.2 = (bf16[4,32,320]{2,1,0:T(8,128)(2,1)S(1)}, bf16[4,32,320]{2,1,0:T(8,128)(2,1)S(1)}, bf16[4,32,320]{2,1,0:T(8,128)(2,1)S(1)}, bf16[4,32,320]{2,1,0:T(8,128)(2,1)S(1)}) custom-call(bf16[8,8,16,320]{3,2,1,0:T(8,128)(2,1)S(1)} %get-tuple-element.44.own_ref, bf16[8,128,384]{2,1,0:T(8,128)(2,1)S(1)} %get-tuple-element.45.q_ref, ...), custom_call_target="tpu_custom_call" | custom-call | flops 2000000000 | tf_op jit(solution)/shard_map/window_attention/pallas_call | solution.py:421
  49.1 0.5 collective-permute-start.11
  49.7 1.8 %collective-permute-start.12 = (bf16[4,32,320]{2,1,0:T(8,128)(2,1)S(1)}, bf16[4,32,320]{2,1,0:T(8,128)(2,1)S(1)}, u32[]{:S(2)}, u32[]{:S(2)}) collective-permute-start(bf16[4,32,320]{2,1,0:T(8,128)(2,1)S(1)} %get-tuple-element.53), channel_id=1, source_target_pairs={{0,6},{2,4},{4,2},{6,0},{8,14},{10,12},{12,10},{14,8},{16,22},{18,... | collective-permute-start | bytes 245768 | tf_op jit(solution)/shard_map/ppermute | solution.py:436
  51.6 0.9 %home.2.refs_4_ = bf16[4,2,320,128]{3,2,1,0:T(8,128)(2,1)} custom-call(bf16[4,32,320]{2,1,0:T(8,128)(2,1)S(1)} %get-tuple-element.57.refs_0_, bf16[4,32,320]{2,1,0:T(8,128)(2,1)S(1)} %collective-permute-done.16.refs_1_, bf16[4,32,320]{2,1,0:T(8,128)(2,1)S(1)} %collective-permute-done.17.refs_2_, bf16[4,32,320]{2,1,0:T(8,128)(2,1)S(1)} %collective-permute-done.18.refs_3_), custom_call_target="tpu_custom_call" | custom-call | flops 1000000 | tf_op jit(solution)/shard_map/home/pallas_call | solution.py:437
  52.7 3.2 %collective-permute-done.12.refs_2_ = bf16[4,32,320]{2,1,0:T(8,128)(2,1)S(1)} collective-permute-done((bf16[4,32,320]{2,1,0:T(8,128)(2,1)S(1)}, bf16[4,32,320]{2,1,0:T(8,128)(2,1)S(1)}, u32[]{:S(2)}, u32[]{:S(2)}) %collective-permute-start.12) | collective-permute-done | bytes 81952 | tf_op jit(solution)/shard_map/ppermute | solution.py:436
  55.9 0.9 %home.3 = bf16[4,2,320,128]{3,2,1,0:T(8,128)(2,1)} custom-call(bf16[4,32,320]{2,1,0:T(8,128)(2,1)S(1)} %get-tuple-element.51.refs_0_, bf16[4,32,320]{2,1,0:T(8,128)(2,1)S(1)} %collective-permute-done.11.refs_1_, bf16[4,32,320]{2,1,0:T(8,128)(2,1)S(1)} %collective-permute-done.12.refs_2_, ...), custom_call_target="tpu_custom_call", output_to_operand_aliasing={{}: (4, {})} | custom-call | flops 1000000 | tf_op jit(solution)/shard_map/home/pallas_call | solution.py:437
  (39 shorter events, 1.0 us)
Async XLA Ops:
  0.0 7.0 %copy-start = (bf16[320,320]{1,0:T(8,128)(2,1)S(1)}, bf16[320,320]{1,0:T(8,128)(2,1)}, u32[]{:S(2)}) copy-start(bf16[320,320]{1,0:T(8,128)(2,1)} %param.13) | copy-start | bytes 614404
  1.0 5.8 %copy-start.7 = (s32[4]{0:T(128)S(1)}, s32[4]{0:T(128)}, u32[]{:S(2)}) copy-start(s32[4]{0:T(128)} %param.11) | copy-start | bytes 52
  1.0 6.7 %copy-start.1 = (bf16[4,2,128,320]{2,3,1,0:T(8,128)(2,1)S(1)}, bf16[4,2,128,320]{2,3,1,0:T(8,128)(2,1)}, u32[]{:S(2)}) copy-start(bf16[4,2,128,320]{2,3,1,0:T(8,128)(2,1)} %param.10) | copy-start | bytes 1966084
  1.0 6.7 %collective-permute-start.1 = (bf16[1,2,320,128]{3,2,1,0:T(8,128)(2,1)S(1)}, bf16[1,2,320,128]{3,2,1,0:T(8,128)(2,1)S(1)}, u32[]{:S(2)}, u32[]{:S(2)}) collective-permute-start(bf16[1,2,320,128]{3,2,1,0:T(8,128)(2,1)S(1)} %pick.1), channel_id=1, source_target_pairs={{0,1},{1,0},{2,3},{3,2},{4,5},{5,4},{6,7},{7,6},{8,9},{9,8},{10,11... | collective-permute-start | bytes 491528 | tf_op jit(solution)/shard_map/ppermute | solution.py:343
  6.6 6.3 %collective-permute-start = (bf16[1,2,320,128]{3,2,1,0:T(8,128)(2,1)S(1)}, bf16[1,2,320,128]{3,2,1,0:T(8,128)(2,1)S(1)}, u32[]{:S(2)}, u32[]{:S(2)}) collective-permute-start(bf16[1,2,320,128]{3,2,1,0:T(8,128)(2,1)S(1)} %get-tuple-element.33), channel_id=1, source_target_pairs={{0,1},{1,0},{2,3},{3,2},{4,5},{5,4},{6,7},{7,6},{8,9},{9,8},{10,11... | collective-permute-start | bytes 491528 | tf_op jit(solution)/shard_map/ppermute | solution.py:358
  11.7 15.3 %copy-start.6 = (f32[320]{0:T(512)S(1)}, f32[320]{0:T(512)}, u32[]{:S(2)}) copy-start(f32[320]{0:T(512)} %param.15) | copy-start | bytes 3844
  11.7 28.2 %copy-start.2 = (bf16[320,320]{1,0:T(8,128)(2,1)S(1)}, bf16[320,320]{1,0:T(8,128)(2,1)}, u32[]{:S(2)}) copy-start(bf16[320,320]{1,0:T(8,128)(2,1)} %wq_ref.1) | copy-start | bytes 614404
  11.7 28.1 %copy-start.3 = (bf16[320,320]{1,0:T(8,128)(2,1)S(1)}, bf16[320,320]{1,0:T(8,128)(2,1)}, u32[]{:S(2)}) copy-start(bf16[320,320]{1,0:T(8,128)(2,1)} %wk_ref.1) | copy-start | bytes 614404
  11.7 28.1 %copy-start.4 = (bf16[320,320]{1,0:T(8,128)(2,1)S(1)}, bf16[320,320]{1,0:T(8,128)(2,1)}, u32[]{:S(2)}) copy-start(bf16[320,320]{1,0:T(8,128)(2,1)} %wv_ref.1) | copy-start | bytes 614404
  17.1 7.1 %collective-permute-start.2 = (bf16[8,16,320]{2,1,0:T(8,128)(2,1)S(1)}, bf16[8,16,320]{2,1,0:T(8,128)(2,1)S(1)}, u32[]{:S(2)}, u32[]{:S(2)}) collective-permute-start(bf16[8,16,320]{2,1,0:T(8,128)(2,1)S(1)} %get-tuple-element.37), channel_id=1, source_target_pairs={{0,3},{1,2},{2,1},{3,0},{4,7},{5,6},{6,5},{7,4},{8,11},{9,10},{10,... | collective-permute-start | bytes 245768 | tf_op jit(solution)/shard_map/ppermute | solution.py:385
  20.9 6.1 %collective-permute-start.3 = (bf16[8,16,320]{2,1,0:T(8,128)(2,1)S(1)}, bf16[8,16,320]{2,1,0:T(8,128)(2,1)S(1)}, u32[]{:S(2)}, u32[]{:S(2)}) collective-permute-start(bf16[8,16,320]{2,1,0:T(8,128)(2,1)S(1)} %get-tuple-element.38), channel_id=1, source_target_pairs={{0,1},{1,0},{2,3},{3,2},{4,5},{5,4},{6,7},{7,6},{8,9},{9,8},{10,11... | collective-permute-start | bytes 245768 | tf_op jit(solution)/shard_map/ppermute | solution.py:385
  21.9 5.5 %collective-permute-start.4 = (bf16[8,16,320]{2,1,0:T(8,128)(2,1)S(1)}, bf16[8,16,320]{2,1,0:T(8,128)(2,1)S(1)}, u32[]{:S(2)}, u32[]{:S(2)}) collective-permute-start(bf16[8,16,320]{2,1,0:T(8,128)(2,1)S(1)} %get-tuple-element.39), channel_id=1, source_target_pairs={{0,4},{1,5},{2,6},{3,7},{4,0},{5,1},{6,2},{7,3},{8,12},{9,13},{10,... | collective-permute-start | bytes 245768 | tf_op jit(solution)/shard_map/ppermute | solution.py:385
  22.2 6.5 %collective-permute-start.5 = (bf16[8,16,320]{2,1,0:T(8,128)(2,1)S(1)}, bf16[8,16,320]{2,1,0:T(8,128)(2,1)S(1)}, u32[]{:S(2)}, u32[]{:S(2)}) collective-permute-start(bf16[8,16,320]{2,1,0:T(8,128)(2,1)S(1)} %get-tuple-element.40), channel_id=1, source_target_pairs={{0,5},{1,4},{2,7},{3,6},{4,1},{5,0},{6,3},{7,2},{8,13},{9,12},{10,... | collective-permute-start | bytes 245768 | tf_op jit(solution)/shard_map/ppermute | solution.py:385
  24.2 5.3 %collective-permute-start.6 = (bf16[8,16,320]{2,1,0:T(8,128)(2,1)S(1)}, bf16[8,16,320]{2,1,0:T(8,128)(2,1)S(1)}, u32[]{:S(2)}, u32[]{:S(2)}) collective-permute-start(bf16[8,16,320]{2,1,0:T(8,128)(2,1)S(1)} %get-tuple-element.41), channel_id=1, source_target_pairs={{0,6},{1,7},{2,4},{3,5},{4,2},{5,3},{6,0},{7,1},{8,14},{9,15},{10,... | collective-permute-start | bytes 245768 | tf_op jit(solution)/shard_map/ppermute | solution.py:385
  24.2 6.1 %collective-permute-start.7 = (bf16[8,16,320]{2,1,0:T(8,128)(2,1)S(1)}, bf16[8,16,320]{2,1,0:T(8,128)(2,1)S(1)}, u32[]{:S(2)}, u32[]{:S(2)}) collective-permute-start(bf16[8,16,320]{2,1,0:T(8,128)(2,1)S(1)} %get-tuple-element.42), channel_id=1, source_target_pairs={{0,7},{1,6},{2,5},{3,4},{4,3},{5,2},{6,1},{7,0},{8,15},{9,14},{10,... | collective-permute-start | bytes 245768 | tf_op jit(solution)/shard_map/ppermute | solution.py:385
  27.0 3.3 %collective-permute-start.8 = (bf16[8,16,320]{2,1,0:T(8,128)(2,1)S(1)}, bf16[8,16,320]{2,1,0:T(8,128)(2,1)S(1)}, u32[]{:S(2)}, u32[]{:S(2)}) collective-permute-start(bf16[8,16,320]{2,1,0:T(8,128)(2,1)S(1)} %get-tuple-element.43), channel_id=1, source_target_pairs={{0,2},{1,3},{2,0},{3,1},{4,6},{5,7},{6,4},{7,5},{8,10},{9,11},{10,... | collective-permute-start | bytes 245768 | tf_op jit(solution)/shard_map/ppermute | solution.py:385
  30.4 11.3 %collective-permute-start.14 = (bf16[4,4,16,320]{3,2,1,0:T(8,128)(2,1)S(1)}, bf16[4,4,16,320]{3,2,1,0:T(8,128)(2,1)S(1)}, u32[]{:S(2)}, u32[]{:S(2)}) collective-permute-start(bf16[4,4,16,320]{3,2,1,0:T(8,128)(2,1)S(1)} %get-tuple-element.55), channel_id=1, source_target_pairs={{0,8},{2,10},{4,12},{6,14},{8,0},{10,2},{12,4},{14,6},{16,24},{18,... | collective-permute-start | bytes 491528 | tf_op jit(solution)/shard_map/ppermute | solution.py:400
  32.1 9.6 %collective-permute-start.15 = (bf16[4,4,16,320]{3,2,1,0:T(8,128)(2,1)S(1)}, bf16[4,4,16,320]{3,2,1,0:T(8,128)(2,1)S(1)}, u32[]{:S(2)}, u32[]{:S(2)}) collective-permute-start(bf16[4,4,16,320]{3,2,1,0:T(8,128)(2,1)S(1)} %get-tuple-element.56), channel_id=1, source_target_pairs={{8,16},{10,18},{12,20},{14,22},{24,32},{26,34},{28,36},{30,38},{40... | collective-permute-start | bytes 491528 | tf_op jit(solution)/shard_map/ppermute | solution.py:399
  36.6 10.7 %collective-permute-start.10 = (bf16[4,4,16,320]{3,2,1,0:T(8,128)(2,1)S(1)}, bf16[4,4,16,320]{3,2,1,0:T(8,128)(2,1)S(1)}, u32[]{:S(2)}, u32[]{:S(2)}) collective-permute-start(bf16[4,4,16,320]{3,2,1,0:T(8,128)(2,1)S(1)} %get-tuple-element.48), channel_id=1, source_target_pairs={{8,16},{10,18},{12,20},{14,22},{24,32},{26,34},{28,36},{30,38},{40... | collective-permute-start | bytes 491528 | tf_op jit(solution)/shard_map/ppermute | solution.py:399
  39.5 7.7 %collective-permute-start.9 = (bf16[4,4,16,320]{3,2,1,0:T(8,128)(2,1)S(1)}, bf16[4,4,16,320]{3,2,1,0:T(8,128)(2,1)S(1)}, u32[]{:S(2)}, u32[]{:S(2)}) collective-permute-start(bf16[4,4,16,320]{3,2,1,0:T(8,128)(2,1)S(1)} %get-tuple-element.47), channel_id=1, source_target_pairs={{0,8},{2,10},{4,12},{6,14},{8,0},{10,2},{12,4},{14,6},{16,24},{18,... | collective-permute-start | bytes 491528 | tf_op jit(solution)/shard_map/ppermute | solution.py:400
  39.8 1.9 %copy-start.5 = (bf16[320,320]{1,0:T(8,128)(2,1)S(1)}, bf16[320,320]{1,0:T(8,128)(2,1)}, u32[]{:S(2)}) copy-start(bf16[320,320]{1,0:T(8,128)(2,1)} %wo_ref.3) | copy-start | bytes 614404
  43.7 7.8 %collective-permute-start.16 = (bf16[4,32,320]{2,1,0:T(8,128)(2,1)S(1)}, bf16[4,32,320]{2,1,0:T(8,128)(2,1)S(1)}, u32[]{:S(2)}, u32[]{:S(2)}) collective-permute-start(bf16[4,32,320]{2,1,0:T(8,128)(2,1)S(1)} %get-tuple-element.58), channel_id=1, source_target_pairs={{0,4},{2,6},{4,0},{6,2},{8,12},{10,14},{12,8},{14,10},{16,20},{18,... | collective-permute-start | bytes 245768 | tf_op jit(solution)/shard_map/ppermute | solution.py:436
  44.3 7.3 %collective-permute-start.17 = (bf16[4,32,320]{2,1,0:T(8,128)(2,1)S(1)}, bf16[4,32,320]{2,1,0:T(8,128)(2,1)S(1)}, u32[]{:S(2)}, u32[]{:S(2)}) collective-permute-start(bf16[4,32,320]{2,1,0:T(8,128)(2,1)S(1)} %get-tuple-element.59), channel_id=1, source_target_pairs={{0,6},{2,4},{4,2},{6,0},{8,14},{10,12},{12,10},{14,8},{16,22},{18,... | collective-permute-start | bytes 245768 | tf_op jit(solution)/shard_map/ppermute | solution.py:436
  47.2 4.4 %collective-permute-start.18 = (bf16[4,32,320]{2,1,0:T(8,128)(2,1)S(1)}, bf16[4,32,320]{2,1,0:T(8,128)(2,1)S(1)}, u32[]{:S(2)}, u32[]{:S(2)}) collective-permute-start(bf16[4,32,320]{2,1,0:T(8,128)(2,1)S(1)} %get-tuple-element.60), channel_id=1, source_target_pairs={{0,2},{2,0},{4,6},{6,4},{8,10},{10,8},{12,14},{14,12},{16,18},{18,... | collective-permute-start | bytes 245768 | tf_op jit(solution)/shard_map/ppermute | solution.py:436
  49.1 3.5 %collective-permute-start.11 = (bf16[4,32,320]{2,1,0:T(8,128)(2,1)S(1)}, bf16[4,32,320]{2,1,0:T(8,128)(2,1)S(1)}, u32[]{:S(2)}, u32[]{:S(2)}) collective-permute-start(bf16[4,32,320]{2,1,0:T(8,128)(2,1)S(1)} %get-tuple-element.52), channel_id=1, source_target_pairs={{0,4},{2,6},{4,0},{6,2},{8,12},{10,14},{12,8},{14,10},{16,20},{18,... | collective-permute-start | bytes 245768 | tf_op jit(solution)/shard_map/ppermute | solution.py:436
  49.7 6.2 %collective-permute-start.12 = (bf16[4,32,320]{2,1,0:T(8,128)(2,1)S(1)}, bf16[4,32,320]{2,1,0:T(8,128)(2,1)S(1)}, u32[]{:S(2)}, u32[]{:S(2)}) collective-permute-start(bf16[4,32,320]{2,1,0:T(8,128)(2,1)S(1)} %get-tuple-element.53), channel_id=1, source_target_pairs={{0,6},{2,4},{4,2},{6,0},{8,14},{10,12},{12,10},{14,8},{16,22},{18,... | collective-permute-start | bytes 245768 | tf_op jit(solution)/shard_map/ppermute | solution.py:436
  51.5 4.4 %collective-permute-start.13 = (bf16[4,32,320]{2,1,0:T(8,128)(2,1)S(1)}, bf16[4,32,320]{2,1,0:T(8,128)(2,1)S(1)}, u32[]{:S(2)}, u32[]{:S(2)}) collective-permute-start(bf16[4,32,320]{2,1,0:T(8,128)(2,1)S(1)} %get-tuple-element.54), channel_id=1, source_target_pairs={{0,2},{2,0},{4,6},{6,4},{8,10},{10,8},{12,14},{14,12},{16,18},{18,... | collective-permute-start | bytes 245768 | tf_op jit(solution)/shard_map/ppermute | solution.py:436
